TPU v7x, 256 devices: a whole 4x4x8 slice. The times are simulated.
256 devices in a mesh: tm: 8 (over x, core), rows: 32 (over z, y).
Axes of the slice: x: 4, y: 4, z: 8, core: 2. Of those that a mesh axis runs over, the one named last changes fastest.
Arguments:
- features: bfloat16 [16, 192, 32, 384], P('tm', 'rows'), may hold values from -6 to 6
- norm_gain: float32 [384], replicated, may hold values from 0.1 to 1.9
- res_weight: bfloat16 [3, 3, 3, 384, 384], replicated, may hold values from -0.0625 to 0.0625
- time_weight: bfloat16 [3, 384, 768], replicated, may hold values from -0.1875 to 0.1875
- up_weight: bfloat16 [3, 3, 384, 192], replicated, may hold values from -0.109375 to 0.109375
Outputs:
- decoded: bfloat16 [32, 384, 64, 192], P('tm', 'rows')
All inputs are finite; a program needn't handle non-finite values.
Results may differ from a plain program's by a relative error of at most 0.0059.
Values may be sent and summed in bfloat16 or wider, within the bound.
No kernel may reach another device: no remote copies, remote signals or barrier semaphores. Data moves between devices by JAX's collectives and lax.ppermute only.
A program may use at most 128 MiB of HBM per device.

v0:
```python
import jax
import jax.numpy as jnp
from jax import lax
from jax.sharding import PartitionSpec as P


def passed_along(block, axis, distance):
    devices = range(lax.axis_size(axis))
    route = [(i - distance, i) for i in devices if i - distance in devices]
    return lax.ppermute(block, axis, route)


def with_halo(block, sides, width):
    for axis, dim in sides:
        count = lax.axis_size(axis)
        forward = [(i, i + 1) for i in range(count - 1)]
        backward = [(target, source) for source, target in forward]
        low = lax.ppermute(
            lax.slice_in_dim(block, block.shape[dim] - width, None, axis=dim), axis, forward
        )
        high = lax.ppermute(lax.slice_in_dim(block, 0, width, axis=dim), axis, backward)
        block = jnp.concatenate([low, block, high], axis=dim)
    return block


def activate(block, norm_gain):
    values = block.astype(jnp.float32)
    inv_rms = lax.rsqrt(jnp.mean(values * values, axis=-1, keepdims=True) + 1e-06)
    return jax.nn.silu(values * inv_rms * norm_gain).astype(jnp.bfloat16)


def column_taps(block):
    columns = block.shape[2]
    padded = jnp.pad(block, ((0, 0), (0, 0), (1, 1), (0, 0)))
    return jnp.concatenate(
        [padded[:, :, 0:columns], padded[:, :, 1 : columns + 1], padded[:, :, 2 : columns + 2]],
        axis=-1,
    )


def residual_conv(stacked, res_weight):
    frames = stacked.shape[0] - 2
    rows_out = stacked.shape[1] - 2
    columns = stacked.shape[2]
    channels = res_weight.shape[-1]
    col_taps = column_taps(stacked)
    kernel = res_weight.reshape(3, 3, 3 * channels, channels)
    running = jnp.zeros((frames * rows_out * columns, channels), jnp.float32)
    for step_t in range(3):
        for step_h in range(3):
            window = col_taps[step_t : step_t + frames, step_h : step_h + rows_out].reshape(
                -1, 3 * channels
            )
            running = running + jnp.dot(
                window, kernel[step_t, step_h], preferred_element_type=jnp.float32
            )
    return running.reshape(frames, rows_out, columns, channels)


def time_upsample(extended, time_weight):
    frames = extended.shape[0] - 2
    rows_in = extended.shape[1]
    columns = extended.shape[2]
    channels = extended.shape[3]
    running = jnp.zeros((frames * rows_in * columns, 2 * channels), jnp.float32)
    for offset in range(3):
        window = extended[offset : offset + frames].reshape(-1, channels)
        running = running + jnp.dot(window, time_weight[offset], preferred_element_type=jnp.float32)
    doubled = running.astype(jnp.bfloat16).reshape(frames, rows_in, columns, 2, channels)
    return jnp.moveaxis(doubled, 3, 1).reshape(2 * frames, rows_in, columns, channels)


def upsample_conv_dense(rimmed_up, up_weight):
    frames, rows_pad, columns, channels = rimmed_up.shape
    rows_low = rows_pad - 2
    enlarged = jnp.repeat(jnp.repeat(rimmed_up, 2, axis=1), 2, axis=2)
    enlarged = enlarged[:, 1 : 2 * rows_low + 3]
    col_taps = column_taps(enlarged)
    kernel = up_weight.reshape(3, 3 * channels, -1)
    running = jnp.zeros((frames * 2 * rows_low * 2 * columns, kernel.shape[-1]), jnp.float32)
    for step_h in range(3):
        window = col_taps[:, step_h : step_h + 2 * rows_low].reshape(-1, 3 * channels)
        running = running + jnp.dot(window, kernel[step_h], preferred_element_type=jnp.float32)
    return running.reshape(frames, 2 * rows_low, 2 * columns, -1).astype(jnp.bfloat16)


def shards(features, norm_gain, res_weight, time_weight, up_weight):
    earlier = passed_along(features, "tm", 1)
    stacked = jnp.concatenate([earlier, features], axis=0)
    rim_depth = 1
    rimmed = with_halo(stacked, (("rows", 1),), rim_depth)
    carried = rimmed[2:, 1:-1].astype(jnp.float32)
    branch = residual_conv(activate(rimmed, norm_gain), res_weight)
    mixed = carried + branch
    blended = mixed.astype(jnp.bfloat16)
    time_stack = jnp.concatenate([passed_along(blended, "tm", 1), blended], axis=0)
    frames_up = time_upsample(time_stack, time_weight)
    rimmed_up = with_halo(frames_up, (("rows", 1),), 1)
    return upsample_conv_dense(rimmed_up, up_weight)


def solution(mesh):
    placed = (P("tm", "rows", None, None), P(), P(), P(), P())
    return jax.shard_map(
        shards, mesh=mesh, in_specs=placed, out_specs=P("tm", "rows", None, None), check_vma=False
    )
```

profile of v0, /device:TPU:122, one launch (start us, length us, event | category | flops | bytes accessed | tf_op | source)
XLA Modules:
  0.0 82.6 jit_solution(12006135484800391666)
XLA Ops:
  0.0 1.9 %collective-permute-start = (bf16[2,6,32,384]{3,2,1,0:T(8,128)(2,1)}, bf16[2,6,32,384]{3,2,1,0:T(8,128)(2,1)S(1)}, u32[]{:S(2)}, u32[]{:S(2)}) collective-permute-start(bf16[2,6,32,384]{3,2,1,0:T(8,128)(2,1)} %param.5), channel_id=1, source_target_pairs={{0,32},{32,64},{64,96},{96,128},{128,160},{160,192},{192,224},{1,3... | collective-permute-start | bytes 884744 | tf_op jit(solution)/shard_map/ppermute | solution.py:10
  1.9 6.3 %collective-permute-done = bf16[2,6,32,384]{3,2,1,0:T(8,128)(2,1)S(1)} collective-permute-done((bf16[2,6,32,384]{3,2,1,0:T(8,128)(2,1)}, bf16[2,6,32,384]{3,2,1,0:T(8,128)(2,1)S(1)}, u32[]{:S(2)}, u32[]{:S(2)}) %collective-permute-start) | collective-permute-done | bytes 294944 | tf_op jit(solution)/shard_map/ppermute | solution.py:10
  8.3 1.0 %constant_dynamic-update-slice_fusion = bf16[4,6,32,384]{3,2,1,0:T(8,128)(2,1)S(1)} fusion(bf16[4,6,32,384]{3,2,1,0:T(8,128)(2,1)S(1)} %constant_dynamic-update-slice_fusion.1, bf16[2,6,32,384]{3,2,1,0:T(8,128)(2,1)} %param.5), kind=kLoop, calls=%fused_computation.53 | loop fusion | bytes 589824 | tf_op jit(solution)/shard_map/concatenate | solution.py:89
  9.3 4.7 %collective-permute-start.1 = (bf16[4,1,32,384]{3,2,1,0:T(8,128)(2,1)S(1)}, bf16[4,1,32,384]{3,2,1,0:T(8,128)(2,1)S(1)}, u32[]{:S(2)}, u32[]{:S(2)}) collective-permute-start(bf16[4,1,32,384]{3,2,1,0:T(8,128)(2,1)S(1)} %get-tuple-element.26), channel_id=1, source_target_pairs={{0,1},{1,2},{2,3},{3,4},{4,5},{5,6},{6,7},{7,8},{8,9},{9,10},{10,1... | collective-permute-start | bytes 294920 | tf_op jit(solution)/shard_map/ppermute | solution.py:18
  14.0 1.9 %collective-permute-start.2 = (bf16[4,1,32,384]{3,2,1,0:T(8,128)(2,1)S(1)}, bf16[4,1,32,384]{3,2,1,0:T(8,128)(2,1)S(1)}, u32[]{:S(2)}, u32[]{:S(2)}) collective-permute-start(bf16[4,1,32,384]{3,2,1,0:T(8,128)(2,1)S(1)} %get-tuple-element.27), channel_id=1, source_target_pairs={{1,0},{2,1},{3,2},{4,3},{5,4},{6,5},{7,6},{8,7},{9,8},{10,9},{11,1... | collective-permute-start | bytes 294920 | tf_op jit(solution)/shard_map/ppermute | solution.py:21
  16.0 0.3 collective-permute-done.1
  16.2 7.6 %collective-permute-done.2 = bf16[4,1,32,384]{3,2,1,0:T(8,128)(2,1)S(1)} collective-permute-done((bf16[4,1,32,384]{3,2,1,0:T(8,128)(2,1)S(1)}, bf16[4,1,32,384]{3,2,1,0:T(8,128)(2,1)S(1)}, u32[]{:S(2)}, u32[]{:S(2)}) %collective-permute-start.2) | collective-permute-done | bytes 98336 | tf_op jit(solution)/shard_map/ppermute | solution.py:21
  23.9 0.2 fusion.1
  24.1 1.2 %fusion.8 = bf16[4,8,32,384]{3,2,1,0:T(8,128)(2,1)S(1)} fusion(f32[384]{0:T(512)} %param.6, f32[4,8,32]{2,1,0:T(8,128)S(1)} %add_rsqrt_fusion, bf16[4,1,32,384]{3,2,1,0:T(8,128)(2,1)S(1)} %collective-permute-done.2, bf16[4,6,32,384]{3,2,1,0:T(8,128)(2,1)S(1)} %constant_dynamic-update-slice_fusion, bf16[4,1,32,384]{3,2,1,0:T(8,128)(2,1)S(1)} %collective-permute-done.1), kind=kLoop, calls=%fused_computation.16 | loop fusion | flops 3932160 | bytes 1578496 | tf_op jit(solution)/shard_map/convert_element_type | solution.py:29
  25.3 0.5 pad_slice_fusion.3
  25.8 0.0 slice-start
  25.8 0.2 pad_maximum_fusion.1
  26.0 0.0 slice-start.1
  26.0 1.0 %fusion.21 = (bf16[2,6,32,1152]{3,2,1,0:T(8,128)(2,1)S(1)}, bf16[2,6,32,1152]{3,2,1,0:T(8,128)(2,1)S(1)}, bf16[2,6,32,1152]{3,2,1,0:T(8,128)(2,1)S(1)}, bf16[2,6...) fusion(bf16[4,8,32,1152]{3,2,1,0:T(8,128)(2,1)S(1)} %pad_maximu, ...), kind=kLoop, calls=%fused_computation.56 | loop fusion | bytes 15925248 | tf_op jit(solution)/shard_map/slice | solution.py:51
  27.0 0.8 %slice-done = s8[3768320]{0:T(1024)(128)(4,1)S(1)} async-done(((s8[7962624]{0:T(1024)(128)(4,1)}), s8[3768320]{0:T(1024)(128)(4,1)S(1)}, s32[]{:S(2)}) %slice-start) | async-done | bytes 3768344
  27.8 1.3 %slice-done.1 = s8[4194304]{0:T(1024)(128)(4,1)S(1)} async-done(((s8[7962624]{0:T(1024)(128)(4,1)}), s8[4194304]{0:T(1024)(128)(4,1)S(1)}, s32[]{:S(2)}) %slice-start.1) | async-done | bytes 4194328
  29.2 0.6 fusion.11
  29.8 0.6 convolution_add_fusion.10
  30.5 0.6 convolution_add_fusion.9
  31.1 0.6 convolution_add_fusion.8
  31.8 0.6 convolution_add_fusion.7
  32.4 0.6 convolution_add_fusion.6
  33.0 0.6 convolution_add_fusion.5
  33.7 0.0 copy-start.5
  33.7 0.6 convolution_add_fusion.4
  34.3 0.0 copy-start.3
  34.4 0.6 convolution_add_fusion.3
  35.0 0.0 copy-done.5
  35.0 0.1 add_convert_fusion
  35.1 1.9 %collective-permute-start.3 = (bf16[2,6,32,384]{3,2,1,0:T(8,128)(2,1)S(1)}, bf16[2,6,32,384]{3,2,1,0:T(8,128)(2,1)S(1)}, u32[]{:S(2)}, u32[]{:S(2)}) collective-permute-start(bf16[2,6,32,384]{3,2,1,0:T(8,128)(2,1)S(1)} %add_convert_fusion), channel_id=1, source_target_pairs={{0,32},{32,64},{64,96},{96,128},{128,160},{160,192},{192,224},{1,3... | collective-permute-start | bytes 884744 | tf_op jit(solution)/shard_map/ppermute | solution.py:10
  37.0 0.0 copy-done.3
  37.0 0.5 fusion.12
  37.5 5.6 %collective-permute-done.3 = bf16[2,6,32,384]{3,2,1,0:T(8,128)(2,1)S(1)} collective-permute-done((bf16[2,6,32,384]{3,2,1,0:T(8,128)(2,1)S(1)}, bf16[2,6,32,384]{3,2,1,0:T(8,128)(2,1)S(1)}, u32[]{:S(2)}, u32[]{:S(2)}) %collective-permute-start.3) | collective-permute-done | bytes 294944 | tf_op jit(solution)/shard_map/ppermute | solution.py:10
  43.2 0.5 fusion.14
  43.6 0.0 copy-start.4
  43.7 0.5 fusion.10
  44.1 0.1 reshape.95
  44.3 0.1 copy.7
  44.4 1.9 %collective-permute-start.4 = (bf16[4,1,32,384]{3,2,1,0:T(8,128)(2,1)S(1)}, bf16[4,1,32,384]{3,2,1,0:T(8,128)(2,1)S(1)}, u32[]{:S(2)}, u32[]{:S(2)}) collective-permute-start(bf16[4,1,32,384]{3,2,1,0:T(8,128)(2,1)S(1)} %get-tuple-element.24), channel_id=1, source_target_pairs={{0,1},{1,2},{2,3},{3,4},{4,5},{5,6},{6,7},{7,8},{8,9},{9,10},{10,1... | collective-permute-start | bytes 294920 | tf_op jit(solution)/shard_map/ppermute | solution.py:18
  46.3 4.1 %collective-permute-start.5 = (bf16[4,1,32,384]{3,2,1,0:T(8,128)(2,1)S(1)}, bf16[4,1,32,384]{3,2,1,0:T(8,128)(2,1)S(1)}, u32[]{:S(2)}, u32[]{:S(2)}) collective-permute-start(bf16[4,1,32,384]{3,2,1,0:T(8,128)(2,1)S(1)} %get-tuple-element.25), channel_id=1, source_target_pairs={{1,0},{2,1},{3,2},{4,3},{5,4},{6,5},{7,6},{8,7},{9,8},{10,9},{11,1... | collective-permute-start | bytes 294920 | tf_op jit(solution)/shard_map/ppermute | solution.py:21
  50.4 0.0 copy-done.4
  50.4 0.1 fusion.22
  50.6 0.4 copy.8
  51.0 0.8 %copy.12 = bf16[24,8,3,384]{3,1,2,0:T(8,128)(2,1)} copy(bf16[24,8,3,384]{3,2,1,0:T(4,128)(2,1)S(1)} %bitcast.118) | data formatting | bytes 884736
  51.8 0.4 copy.9
  52.2 0.8 copy.13
  53.0 0.4 copy.10
  53.4 0.8 %copy.14 = bf16[24,8,3,384]{3,1,2,0:T(8,128)(2,1)} copy(bf16[24,8,3,384]{3,2,1,0:T(4,128)(2,1)S(1)} %bitcast.120) | data formatting | bytes 884736
  54.2 0.0 collective-permute-done.4
  54.2 1.9 %collective-permute-done.5 = bf16[4,1,32,384]{3,2,1,0:T(8,128)(2,1)S(1)} collective-permute-done((bf16[4,1,32,384]{3,2,1,0:T(8,128)(2,1)S(1)}, bf16[4,1,32,384]{3,2,1,0:T(8,128)(2,1)S(1)}, u32[]{:S(2)}, u32[]{:S(2)}) %collective-permute-start.5) | collective-permute-done | bytes 98336 | tf_op jit(solution)/shard_map/ppermute | solution.py:21
  56.1 0.1 pad_maximum_fusion.3
  56.3 1.3 %broadcast_in_dim.8 = bf16[4,8,2,32,384]{4,3,2,1,0:T(8,128)(2,1)} broadcast(bf16[4,8,32,384]{3,2,1,0:T(8,128)(2,1)S(1)} %pad_maximum_fusion.3), dimensions={0,1,3,4} | broadcast | bytes 2359296 | tf_op jit(solution)/shard_map/broadcast_in_dim | solution.py:76
  57.6 4.7 %broadcast_in_dim.9 = bf16[4,16,32,2,384]{4,3,2,1,0:T(2,128)(2,1)S(1)} broadcast(bf16[4,16,32,384]{3,2,1,0:T(8,128)(2,1)} %bitcast.105), dimensions={0,1,2,4} | broadcast | bytes 4718592 | tf_op jit(solution)/shard_map/broadcast_in_dim | solution.py:76
  62.3 2.7 %reshape.98 = bf16[4,16,64,384]{3,2,1,0:T(8,128)(2,1)} reshape(bf16[4,16,32,2,384]{4,3,2,1,0:T(2,128)(2,1)S(1)} %broadcast_in_dim.9) | data formatting | bytes 6291456 | tf_op jit(solution)/shard_map/reshape | solution.py:76
  65.0 2.1 %slice.175 = bf16[4,14,64,384]{3,2,1,0:T(8,128)(2,1)S(1)} slice(bf16[4,16,64,384]{3,2,1,0:T(8,128)(2,1)} %reshape.98), slice={[0:4], [1:15], [0:64], [0:384]} | slice | bytes 5505024 | tf_op jit(solution)/shard_map/slice | solution.py:77
  67.1 3.1 %pad_slice_fusion.1 = (bf16[4,14,64,384]{3,2,1,0:T(8,128)(2,1)S(1)}, bf16[4,14,64,384]{3,2,1,0:T(8,128)(2,1)S(1)}) fusion(bf16[4,14,64,384]{3,2,1,0:T(8,128)(2,1)S(1)} %slice.175), kind=kLoop, calls=%fused_computation.5 | loop fusion | bytes 8257536 | tf_op jit(solution)/shard_map/slice | solution.py:36
  70.2 1.2 %pad_maximum_fusion = bf16[4,14,64,1152]{3,2,1,0:T(8,128)(2,1)S(1)} fusion(bf16[4,14,64,384]{3,2,1,0:T(8,128)(2,1)S(1)} %get-tuple-element.9, bf16[4,14,64,384]{3,2,1,0:T(8,128)(2,1)S(1)} %slice.175, bf16[4,14,64,384]{3,2,1,0:T(8,128)(2,1)S(1)} %get-tuple-element.8), kind=kLoop, calls=%fused_computation | loop fusion | flops 24772608 | bytes 16515072 | tf_op jit(solution)/shard_map/concatenate | solution.py:35
  71.4 0.0 copy-start
  71.4 2.1 %fusion.20 = (bf16[4,12,64,1152]{3,2,1,0:T(8,128)(2,1)S(1)}, bf16[4,12,64,1152]{3,2,1,0:T(8,128)(2,1)S(1)}, bf16[4,12,64,1152]{3,2,1,0:T(8,128)(2,1)S(1)}) fusion(bf16[4,14,64,1152]{3,2,1,0:T(8,128)(2,1)S(1)} %pad_maximum_fusion), kind=kLoop, calls=%fused_computation.55 | loop fusion | bytes 42467328 | tf_op jit(solution)/shard_map/slice | solution.py:82
  73.5 0.0 copy-done
  73.5 2.5 %fusion.25 = f32[3072,192]{0,1:T(8,128)S(1)} fusion(bf16[3072,1152]{1,0:T(8,128)(2,1)S(1)} %bitcast.91, bf16[1152,192]{0,1:T(8,128)(2,1)S(1)} %bitcast.121), kind=kOutput, calls=%fused_computation.60 | convolution fusion | flops 1358954496 | bytes 9879552 | tf_op jit(solution)/shard_map/dot_general | solution.py:83
  76.0 2.5 %convolution_add_fusion.1 = f32[3072,192]{0,1:T(8,128)S(1)} fusion(f32[3072,192]{0,1:T(8,128)S(1)} %fusion.25, bf16[3072,1152]{1,0:T(8,128)(2,1)S(1)} %bitcast.93, bf16[1152,192]{0,1:T(8,128)(2,1)S(1)} %bitcast.122), kind=kOutput, calls=%fused_computation.2 | convolution fusion | flops 1359544320 | bytes 12238848 | tf_op jit(solution)/shard_map/dot_general | solution.py:83
  78.6 2.5 %fusion = bf16[3072,192]{0,1:T(8,128)(2,1)S(1)} fusion(f32[3072,192]{0,1:T(8,128)S(1)} %convolution_add_fusion.1, bf16[3072,1152]{1,0:T(8,128)(2,1)S(1)} %bitcast.92, bf16[1152,192]{0,1:T(8,128)(2,1)S(1)} %bitcast.123), kind=kOutput, calls=%fused_computation.3 | convolution fusion | flops 1360134144 | bytes 11059200 | tf_op jit(solution)/shard_map/dot_general | solution.py:83
  81.1 1.5 %copy.11 = bf16[3072,192]{1,0:T(8,128)(2,1)} copy(bf16[3072,192]{0,1:T(8,128)(2,1)S(1)} %fusion) | data formatting | bytes 2359296 | tf_op jit(solution)/shard_map/convert_element_type | solution.py:84
  (10 shorter events, 0.1 us)
Async XLA Ops:
  0.0 8.2 %collective-permute-start = (bf16[2,6,32,384]{3,2,1,0:T(8,128)(2,1)}, bf16[2,6,32,384]{3,2,1,0:T(8,128)(2,1)S(1)}, u32[]{:S(2)}, u32[]{:S(2)}) collective-permute-start(bf16[2,6,32,384]{3,2,1,0:T(8,128)(2,1)} %param.5), channel_id=1, source_target_pairs={{0,32},{32,64},{64,96},{96,128},{128,160},{160,192},{192,224},{1,3... | collective-permute-start | bytes 884744 | tf_op jit(solution)/shard_map/ppermute | solution.py:10
  9.3 6.9 %collective-permute-start.1 = (bf16[4,1,32,384]{3,2,1,0:T(8,128)(2,1)S(1)}, bf16[4,1,32,384]{3,2,1,0:T(8,128)(2,1)S(1)}, u32[]{:S(2)}, u32[]{:S(2)}) collective-permute-start(bf16[4,1,32,384]{3,2,1,0:T(8,128)(2,1)S(1)} %get-tuple-element.26), channel_id=1, source_target_pairs={{0,1},{1,2},{2,3},{3,4},{4,5},{5,6},{6,7},{7,8},{8,9},{9,10},{10,1... | collective-permute-start | bytes 294920 | tf_op jit(solution)/shard_map/ppermute | solution.py:18
  14.0 9.8 %collective-permute-start.2 = (bf16[4,1,32,384]{3,2,1,0:T(8,128)(2,1)S(1)}, bf16[4,1,32,384]{3,2,1,0:T(8,128)(2,1)S(1)}, u32[]{:S(2)}, u32[]{:S(2)}) collective-permute-start(bf16[4,1,32,384]{3,2,1,0:T(8,128)(2,1)S(1)} %get-tuple-element.27), channel_id=1, source_target_pairs={{1,0},{2,1},{3,2},{4,3},{5,4},{6,5},{7,6},{8,7},{9,8},{10,9},{11,1... | collective-permute-start | bytes 294920 | tf_op jit(solution)/shard_map/ppermute | solution.py:21
  25.8 2.1 %slice-start = ((s8[7962624]{0:T(1024)(128)(4,1)}), s8[3768320]{0:T(1024)(128)(4,1)S(1)}, s32[]{:S(2)}) async-start(s8[7962624]{0:T(1024)(128)(4,1)} %bitcast.94), calls=%async_computation | async-start | bytes 7536640
  26.0 3.1 %slice-start.1 = ((s8[7962624]{0:T(1024)(128)(4,1)}), s8[4194304]{0:T(1024)(128)(4,1)S(1)}, s32[]{:S(2)}) async-start(s8[7962624]{0:T(1024)(128)(4,1)} %bitcast.94), calls=%async_computation.1 | async-start | bytes 8388608
  33.7 1.3 %copy-start.5 = (bf16[2,6,32,384]{3,2,1,0:T(8,128)(2,1)S(1)}, bf16[2,6,32,384]{3,2,1,0:T(8,128)(2,1)}, u32[]{:S(2)}) copy-start(bf16[2,6,32,384]{3,2,1,0:T(8,128)(2,1)} %param.5) | copy-start | bytes 884740
  34.3 2.7 %copy-start.3 = (bf16[3,384,768]{2,1,0:T(8,128)(2,1)S(1)}, bf16[3,384,768]{2,1,0:T(8,128)(2,1)}, u32[]{:S(2)}) copy-start(bf16[3,384,768]{2,1,0:T(8,128)(2,1)} %param.8) | copy-start | bytes 5308420
  35.1 8.0 %collective-permute-start.3 = (bf16[2,6,32,384]{3,2,1,0:T(8,128)(2,1)S(1)}, bf16[2,6,32,384]{3,2,1,0:T(8,128)(2,1)S(1)}, u32[]{:S(2)}, u32[]{:S(2)}) collective-permute-start(bf16[2,6,32,384]{3,2,1,0:T(8,128)(2,1)S(1)} %add_convert_fusion), channel_id=1, source_target_pairs={{0,32},{32,64},{64,96},{96,128},{128,160},{160,192},{192,224},{1,3... | collective-permute-start | bytes 884744 | tf_op jit(solution)/shard_map/ppermute | solution.py:10
  43.6 6.8 %copy-start.4 = (bf16[3,3,384,192]{2,3,1,0:T(8,128)(2,1)S(1)}, bf16[3,3,384,192]{2,3,1,0:T(8,128)(2,1)}, u32[]{:S(2)}) copy-start(bf16[3,3,384,192]{2,3,1,0:T(8,128)(2,1)} %param.9) | copy-start | bytes 3981316
  44.4 9.8 %collective-permute-start.4 = (bf16[4,1,32,384]{3,2,1,0:T(8,128)(2,1)S(1)}, bf16[4,1,32,384]{3,2,1,0:T(8,128)(2,1)S(1)}, u32[]{:S(2)}, u32[]{:S(2)}) collective-permute-start(bf16[4,1,32,384]{3,2,1,0:T(8,128)(2,1)S(1)} %get-tuple-element.24), channel_id=1, source_target_pairs={{0,1},{1,2},{2,3},{3,4},{4,5},{5,6},{6,7},{7,8},{8,9},{9,10},{10,1... | collective-permute-start | bytes 294920 | tf_op jit(solution)/shard_map/ppermute | solution.py:18
  46.3 9.8 %collective-permute-start.5 = (bf16[4,1,32,384]{3,2,1,0:T(8,128)(2,1)S(1)}, bf16[4,1,32,384]{3,2,1,0:T(8,128)(2,1)S(1)}, u32[]{:S(2)}, u32[]{:S(2)}) collective-permute-start(bf16[4,1,32,384]{3,2,1,0:T(8,128)(2,1)S(1)} %get-tuple-element.25), channel_id=1, source_target_pairs={{1,0},{2,1},{3,2},{4,3},{5,4},{6,5},{7,6},{8,7},{9,8},{10,9},{11,1... | collective-permute-start | bytes 294920 | tf_op jit(solution)/shard_map/ppermute | solution.py:21
  71.4 2.1 %copy-start = (bf16[24,8,3,384]{3,1,2,0:T(8,128)(2,1)S(1)}, bf16[24,8,3,384]{3,1,2,0:T(8,128)(2,1)}, u32[]{:S(2)}) copy-start(bf16[24,8,3,384]{3,1,2,0:T(8,128)(2,1)} %copy.12) | copy-start | bytes 1327108
  73.5 2.5 %copy-start.1 = (bf16[24,8,3,384]{3,1,2,0:T(8,128)(2,1)S(1)}, bf16[24,8,3,384]{3,1,2,0:T(8,128)(2,1)}, u32[]{:S(2)}) copy-start(bf16[24,8,3,384]{3,1,2,0:T(8,128)(2,1)} %copy.13) | copy-start | bytes 1327108
  76.0 2.5 %copy-start.2 = (bf16[24,8,3,384]{3,1,2,0:T(8,128)(2,1)S(1)}, bf16[24,8,3,384]{3,1,2,0:T(8,128)(2,1)}, u32[]{:S(2)}) copy-start(bf16[24,8,3,384]{3,1,2,0:T(8,128)(2,1)} %copy.14) | copy-start | bytes 1327108
where the time goes:
time: 83 us; the launch traced here: 82.6 us
  local copies, waits for them, and re-layouts  26.2 us (32%)
  waiting for transfers between devices  21.8 us (26%)
  starting transfers between devices  16.5 us (20%)
  matrix products  14.6 us (18%)
  other arithmetic  3.08 us (4%)
    ppermute x2, waiting for transfers between devices, passed_along(): return lax.ppermute(block, axis, route)  12 us
    ppermute x2, waiting for transfers between devices, with_halo(): lax.ppermute(lax.slice_in_dim(block, 0, width, axis=dim), axis, backward)  9.55 us
    dot_general x3, matrix products, upsample_conv_dense(): jnp.dot(window, kernel[step_h], preferred_element_type=jnp.float32)  7.49 us
    ppermute x2, starting transfers between devices, with_halo(): lax.ppermute(lax.slice_in_dim(block, block.shape[dim] - width, None, axis...  6.62 us
    ppermute x2, starting transfers between devices, with_halo(): lax.ppermute(lax.slice_in_dim(block, 0, width, axis=dim), axis, backward)  6.02 us
    broadcast_in_dim x2, local copies, waits for them, and re-layouts, upsample_conv_dense(): enlarged = jnp.repeat(jnp.repeat(rimmed_up, 2, axis=1), 2, axis=2)  6.01 us
    dot_general x9, matrix products, residual_conv(): jnp.dot(window, kernel[step_t, step_h], preferred_element_type=jnp.float32)  5.73 us
    unnamed x20, local copies, waits for them, and re-layouts  4.74 us
  transfers between devices with their start and end apart: 6, of which 5 were waited for; matrix products, arithmetic and copies ran while one was open for 5% of the time, Pallas kernels for 0%

commit v1 on v0

v1 whole, which is shorter than its diff:
```python
import jax
import jax.numpy as jnp
from jax import lax
from jax.experimental import pallas as pl
from jax.experimental.pallas import tpu as pltpu
from jax.sharding import PartitionSpec as P

F32 = jnp.float32
BF16 = jnp.bfloat16
VMEM = pl.BlockSpec(memory_space=pltpu.VMEM)
SMEM = pl.BlockSpec(memory_space=pltpu.SMEM)


def ring(block, axes, shift, sizes):
    total = 1
    for size in sizes:
        total *= size
    pairs = []
    for source in range(total):
        coords, rest = [], source
        for size in reversed(sizes):
            coords.insert(0, rest % size)
            rest //= size
        target = 0
        for coord, step, size in zip(coords, shift, sizes):
            target = target * size + (coord + step) % size
        pairs.append((source, target))
    return lax.ppermute(block, axes, pairs)


def activated(values, gain):
    inv = lax.rsqrt(jnp.mean(values * values, axis=-1, keepdims=True) + 1e-06)
    normed = values * inv * gain
    half = 0.5 * normed
    return half + half * jnp.tanh(half)


def residual_kernel(flags, own, prev, up, dn, pup, pdn, gain, weight, out, act):
    rows, cols, ch = own.shape[1:]
    not_first_t = flags[0].astype(F32)
    not_first_r = flags[1].astype(F32)
    not_last_r = flags[2].astype(F32)
    g = gain[...].reshape(1, 1, 1, ch)

    def put(src, frame, row, keep):
        values = src[...].astype(F32)
        a = activated(values, g)
        if keep is not None:
            a = a * keep
        act[frame : frame + 2, row : row + src.shape[1]] = a.astype(BF16)

    put(own, 2, 2, None)
    put(prev, 0, 2, not_first_t)
    put(up, 2, 0, not_first_r)
    put(dn, 2, rows + 2, not_last_r)
    put(pup, 0, 0, not_first_r * not_first_t)
    put(pdn, 0, rows + 2, not_last_r * not_first_t)

    size = 2 * (rows + 2) * cols
    acc = None
    for kt in range(3):
        lhs = jnp.concatenate(
            [act[kt : kt + 2, kh : kh + rows + 2].reshape(size, ch) for kh in range(3)], axis=1
        )
        rhs = jnp.concatenate(
            [weight[kt, :, kw].reshape(3 * ch, ch) for kw in range(3)], axis=1
        )
        part = jnp.dot(lhs, rhs, preferred_element_type=F32)
        acc = part if acc is None else acc + part
    col = lax.broadcasted_iota(jnp.int32, (size, ch), 0) % cols
    left = jnp.where(col == 0, 0.0, pltpu.roll(acc[:, :ch], 1, 0))
    right = jnp.where(col == cols - 1, 0.0, pltpu.roll(acc[:, 2 * ch :], size - 1, 0))
    branch = (left + acc[:, ch : 2 * ch] + right).reshape(2, rows + 2, cols, ch)
    out[:, 0:1] = ((up[:, 1:2].astype(F32) + branch[:, 0:1]) * not_first_r).astype(BF16)
    out[:, 1 : rows + 1] = (own[...].astype(F32) + branch[:, 1 : rows + 1]).astype(BF16)
    out[:, rows + 1 :] = ((dn[:, 0:1].astype(F32) + branch[:, rows + 1 :]) * not_last_r).astype(BF16)


def combine_kernel(weight, out):
    ch = weight.shape[2]
    w = [[weight[kh, kw].astype(F32) for kw in range(3)] for kh in range(3)]
    for phase in range(2):
        for tap in range(2):
            if phase == 0:
                r = w[0] if tap == 0 else [w[1][k] + w[2][k] for k in range(3)]
            else:
                r = [w[0][k] + w[1][k] for k in range(3)] if tap == 0 else w[2]
            row = jnp.concatenate([r[0], r[0] + r[1], r[1] + r[2], r[2]], axis=1)
            out[phase, tap * ch : (tap + 1) * ch] = row.astype(BF16)


def upsample_kernel(flags, own, prev, time_weight, up_weight, out, stack, up, woven):
    frames, rows2, cols, ch = own.shape
    rows = rows2 - 2
    stack[2:4] = own[...]
    stack[0:2] = prev[...] * flags[0].astype(BF16)
    size = frames * rows2 * cols
    lhs = jnp.concatenate([stack[k : k + 2].reshape(size, ch) for k in range(3)], axis=1)
    doubled = jnp.dot(lhs, time_weight[...].reshape(3 * ch, 2 * ch), preferred_element_type=F32)
    doubled = doubled.astype(BF16).reshape(frames, rows2, cols, 2 * ch)
    for p in range(2):
        up[:, p] = doubled[..., p * ch : (p + 1) * ch]
    co = out.shape[-1]
    ups = 2 * frames
    size = ups * rows * cols
    for phase in range(2):
        lhs = jnp.concatenate(
            [
                up[:, :, phase + tap : phase + tap + rows].reshape(size, ch)
                for tap in range(2)
            ],
            axis=1,
        )
        y = jnp.dot(lhs, up_weight[phase], preferred_element_type=F32)
        a, b = y[:, : 2 * co], y[:, 2 * co :]
        col = lax.broadcasted_iota(jnp.int32, (size, 2 * co), 0) % cols
        lane = lax.broadcasted_iota(jnp.int32, (size, 2 * co), 1)
        shift_a = jnp.where(col == 0, 0.0, pltpu.roll(a, 1, 0))
        shift_b = jnp.where(col == cols - 1, 0.0, pltpu.roll(b, size - 1, 0))
        z = jnp.where(lane < co, shift_a + b, a + shift_b)
        for parity, value in ((0, z), (1, pltpu.roll(z, co, 1))):
            for half in range(2):
                woven[half, pl.ds(parity, size, 2), :] = value[:, half * 128 : half * 128 + 128]
        for f in range(ups):
            for r in range(rows):
                at = (f * rows + r) * 2 * cols
                line = jnp.concatenate([woven[half, at : at + 2 * cols] for half in range(2)], axis=1)
                out[f, 2 * r + phase] = line[:, :co].astype(BF16)


def shards(features, norm_gain, res_weight, time_weight, up_weight):
    frames, rows, cols, ch = features.shape
    nt, nr = lax.axis_size("tm"), lax.axis_size("rows")
    co = up_weight.shape[-1]
    t, r = lax.axis_index("tm"), lax.axis_index("rows")
    flags = jnp.stack([t > 0, r > 0, r < nr - 1]).astype(jnp.int32)

    top, bottom = features[:, :2], features[:, -2:]
    axes, sizes = ("tm", "rows"), (nt, nr)
    prev = ring(features, axes, (1, 0), sizes)
    up = ring(bottom, axes, (0, 1), sizes)
    dn = ring(top, axes, (0, -1), sizes)
    pup = ring(bottom, axes, (1, 1), sizes)
    pdn = ring(top, axes, (1, -1), sizes)

    blended = pl.pallas_call(
        residual_kernel,
        out_shape=jax.ShapeDtypeStruct((2, rows + 2, cols, ch), BF16),
        in_specs=[SMEM] + [VMEM] * 8,
        out_specs=VMEM,
        scratch_shapes=[pltpu.VMEM((4, rows + 4, cols, ch), BF16)],
        compiler_params=pltpu.CompilerParams(vmem_limit_bytes=48 * 2**20),
        name="residual",
    )(flags, features, prev, up, dn, pup, pdn, norm_gain.reshape(1, ch), res_weight)

    combined = pl.pallas_call(
        combine_kernel,
        out_shape=jax.ShapeDtypeStruct((2, 2 * ch, 4 * co), BF16),
        in_specs=[VMEM],
        out_specs=VMEM,
        compiler_params=pltpu.CompilerParams(vmem_limit_bytes=32 * 2**20),
        name="combine",
    )(up_weight)

    earlier = ring(blended, axes, (1, 0), sizes)
    return pl.pallas_call(
        upsample_kernel,
        out_shape=jax.ShapeDtypeStruct((2 * frames, 2 * rows, 2 * cols, co), BF16),
        in_specs=[SMEM] + [VMEM] * 4,
        out_specs=VMEM,
        scratch_shapes=[
            pltpu.VMEM((4, rows + 2, cols, ch), BF16),
            pltpu.VMEM((2, 2, rows + 2, cols, ch), BF16),
            pltpu.VMEM((2, 2 * frames * rows * 2 * cols, 128), F32),
        ],
        compiler_params=pltpu.CompilerParams(vmem_limit_bytes=48 * 2**20),
        name="upsample",
    )(flags, blended, earlier, time_weight, combined)


def solution(mesh):
    placed = (P("tm", "rows", None, None), P(), P(), P(), P())
    return jax.shard_map(
        shards, mesh=mesh, in_specs=placed, out_specs=P("tm", "rows", None, None), check_vma=False
    )
```

time: 83 us -> 44.8 us (0.54)
  the two profiles are of different devices: /device:TPU:122 before, /device:TPU:0 now
where the time goes in v1:
time: 44.8 us; the launch traced here: 44.5 us
  Pallas kernels  15.3 us (34%)
  waiting for transfers between devices  14.1 us (31%)
  starting transfers between devices  9.93 us (22%)
  local copies, waits for them, and re-layouts  5.14 us (11%)
    ppermute x6, waiting for transfers between devices, ring(): return lax.ppermute(block, axes, pairs)  14.1 us
    ppermute x6, starting transfers between devices, ring(): return lax.ppermute(block, axes, pairs)  9.93 us
    pallas_call x1, Pallas kernels, shards(): pl.pallas_call(residual_kernel, out_shape=jax.ShapeDtypeStruct((2, rows +...  8.72 us
    pallas_call x1, Pallas kernels, shards(): pl.pallas_call(upsample_kernel, out_shape=jax.ShapeDtypeStruct((2 * frame...  5.78 us
    unnamed x5, local copies, waits for them, and re-layouts  3.49 us
    slice x1, local copies, waits for them, and re-layouts, shards(): top, bottom = (features[:, :2], features[:, -2:])  0.96 us
  transfers between devices with their start and end apart: 6, of which 4 were waited for; matrix products, arithmetic and copies ran while one was open for 10% of the time, Pallas kernels for 2%

profile of v1, /device:TPU:0, one launch (start us, length us, event | category | flops | bytes accessed | tf_op | source)
XLA Modules:
  0.0 44.5 jit_solution(6520092887195538804)
XLA Ops:
  0.0 0.0 collective-permute-start
  0.0 1.0 %fusion = (bf16[2,2,32,384]{3,2,1,0:T(8,128)(2,1)S(1)}, bf16[2,2,32,384]{3,2,1,0:T(8,128)(2,1)S(1)}) fusion(bf16[2,6,32,384]{3,2,1,0:T(8,128)(2,1)} %own.1), kind=kLoop, calls=%fused_computation.1 | loop fusion | bytes 393216 | tf_op jit(solution)/shard_map/slice | solution.py:138
  1.0 7.9 %collective-permute-start.4 = (bf16[2,2,32,384]{3,2,1,0:T(8,128)(2,1)S(1)}, bf16[2,2,32,384]{3,2,1,0:T(8,128)(2,1)S(1)}, u32[]{:S(2)}, u32[]{:S(2)}) collective-permute-start(bf16[2,2,32,384]{3,2,1,0:T(8,128)(2,1)S(1)} %get-tuple-element.5), channel_id=1, source_target_pairs={{0,63},{1,32},{2,33},{3,34},{4,35},{5,36},{6,37},{7,38},{8,39},{9,... | collective-permute-start | bytes 294920 | tf_op jit(solution)/shard_map/ppermute | solution.py:28
  8.8 0.7 %collective-permute-start.2 = (bf16[2,2,32,384]{3,2,1,0:T(8,128)(2,1)S(1)}, bf16[2,2,32,384]{3,2,1,0:T(8,128)(2,1)S(1)}, u32[]{:S(2)}, u32[]{:S(2)}) collective-permute-start(bf16[2,2,32,384]{3,2,1,0:T(8,128)(2,1)S(1)} %get-tuple-element.5), channel_id=1, source_target_pairs={{0,31},{1,0},{2,1},{3,2},{4,3},{5,4},{6,5},{7,6},{8,7},{9,8},{10,9... | collective-permute-start | bytes 294920 | tf_op jit(solution)/shard_map/ppermute | solution.py:28
  9.6 0.4 collective-permute-start.3
  10.0 0.9 %collective-permute-start.1 = (bf16[2,2,32,384]{3,2,1,0:T(8,128)(2,1)S(1)}, bf16[2,2,32,384]{3,2,1,0:T(8,128)(2,1)S(1)}, u32[]{:S(2)}, u32[]{:S(2)}) collective-permute-start(bf16[2,2,32,384]{3,2,1,0:T(8,128)(2,1)S(1)} %get-tuple-element.6), channel_id=1, source_target_pairs={{0,1},{1,2},{2,3},{3,4},{4,5},{5,6},{6,7},{7,8},{8,9},{9,10},{10,1... | collective-permute-start | bytes 294920 | tf_op jit(solution)/shard_map/ppermute | solution.py:28
  10.9 0.7 %reshape.3.gain = f32[1,384]{1,0:T(1,128)S(1)} reshape(f32[384]{0:T(512)} %param.6) | data formatting | bytes 3072 | tf_op jit(solution)/shard_map/reshape | solution.py:154
  11.6 0.1 add_convert_fusion.flags
  11.6 0.4 collective-permute-done.4.pdn
  12.0 2.0 %collective-permute-done.2.dn = bf16[2,2,32,384]{3,2,1,0:T(8,128)(2,1)S(1)} collective-permute-done((bf16[2,2,32,384]{3,2,1,0:T(8,128)(2,1)S(1)}, bf16[2,2,32,384]{3,2,1,0:T(8,128)(2,1)S(1)}, u32[]{:S(2)}, u32[]{:S(2)}) %collective-permute-start.2) | collective-permute-done | bytes 98336 | tf_op jit(solution)/shard_map/ppermute | solution.py:28
  14.0 6.6 %collective-permute-done.3.pup = bf16[2,2,32,384]{3,2,1,0:T(8,128)(2,1)S(1)} collective-permute-done((bf16[2,2,32,384]{3,2,1,0:T(8,128)(2,1)S(1)}, bf16[2,2,32,384]{3,2,1,0:T(8,128)(2,1)S(1)}, u32[]{:S(2)}, u32[]{:S(2)}) %collective-permute-start.3) | collective-permute-done | bytes 98336 | tf_op jit(solution)/shard_map/ppermute | solution.py:28
  20.6 0.0 collective-permute-done.1.up
  20.6 0.0 collective-permute-done.prev
  20.6 0.0 copy-start.1
  20.6 1.0 %copy-done.1 = bf16[2,6,32,384]{3,2,1,0:T(8,128)(2,1)S(1)} copy-done((bf16[2,6,32,384]{3,2,1,0:T(8,128)(2,1)S(1)}, bf16[2,6,32,384]{3,2,1,0:T(8,128)(2,1)}, u32[]{:S(2)}) %copy-start.1) | copy-done | bytes 294936
  21.6 8.7 %residual.1.own = bf16[2,8,32,384]{3,2,1,0:T(8,128)(2,1)S(1)} custom-call(s32[3]{0:T(128)S(1)} %add_convert_fusion.flags, bf16[2,6,32,384]{3,2,1,0:T(8,128)(2,1)S(1)} %copy-done.1, bf16[2,6,32,384]{3,2,1,0:T(8,128)(2,1)S(1)} %collective-permute-done.prev, bf16[2,2,32,384]{3,2,1,0:T(8,128)(2,1)S(1)} %collective-permute-done.1.up, ...), custom_call_target="tpu_custom_call" | custom-call | tf_op jit(solution)/shard_map/residual/pallas_call | solution.py:146
  30.3 0.0 collective-permute-start.5
  30.3 2.5 %copy.6.weight = bf16[3,3,384,192]{3,2,1,0:T(8,128)(2,1)S(1)} copy(bf16[3,3,384,192]{2,3,1,0:T(8,128)(2,1)} %param.9) | data formatting | bytes 2654208 | tf_op args[4]
  32.9 0.0 copy-start
  32.9 0.8 %combine.1.up_weight = bf16[2,768,768]{2,1,0:T(8,128)(2,1)S(1)} custom-call(bf16[3,3,384,192]{3,2,1,0:T(8,128)(2,1)S(1)} %copy.6.weight), custom_call_target="tpu_custom_call" | custom-call | tf_op jit(solution)/shard_map/combine/pallas_call | solution.py:156
  33.7 5.1 %collective-permute-done.5.prev = bf16[2,8,32,384]{3,2,1,0:T(8,128)(2,1)S(1)} collective-permute-done((bf16[2,8,32,384]{3,2,1,0:T(8,128)(2,1)S(1)}, bf16[2,8,32,384]{3,2,1,0:T(8,128)(2,1)S(1)}, u32[]{:S(2)}, u32[]{:S(2)}) %collective-permute-start.5) | collective-permute-done | bytes 393248 | tf_op jit(solution)/shard_map/ppermute | solution.py:28
  38.7 0.0 copy-done
  38.7 5.8 %upsample.1 = bf16[4,12,64,192]{3,2,1,0:T(8,128)(2,1)} custom-call(s32[3]{0:T(128)S(1)} %add_convert_fusion.flags, bf16[2,8,32,384]{3,2,1,0:T(8,128)(2,1)S(1)} %residual.1.own, bf16[2,8,32,384]{3,2,1,0:T(8,128)(2,1)S(1)} %collective-permute-done.5.prev, bf16[3,384,768]{2,1,0:T(8,128)(2,1)S(1)} %copy-done, bf16[2,768,768]{2,1,0:T(8,128)(2,1)S(1)} %combine.1.up_weight), custom_call_target="tpu_custom_call" | custom-call | tf_op jit(solution)/shard_map/upsample/pallas_call | solution.py:166
Async XLA Ops:
  0.0 20.6 %collective-permute-start = (bf16[2,6,32,384]{3,2,1,0:T(8,128)(2,1)}, bf16[2,6,32,384]{3,2,1,0:T(8,128)(2,1)S(1)}, u32[]{:S(2)}, u32[]{:S(2)}) collective-permute-start(bf16[2,6,32,384]{3,2,1,0:T(8,128)(2,1)} %own.1), channel_id=1, source_target_pairs={{0,32},{1,33},{2,34},{3,35},{4,36},{5,37},{6,38},{7,39},{8,40},{9,... | collective-permute-start | bytes 884744 | tf_op jit(solution)/shard_map/ppermute | solution.py:28
  1.0 11.1 %collective-permute-start.4 = (bf16[2,2,32,384]{3,2,1,0:T(8,128)(2,1)S(1)}, bf16[2,2,32,384]{3,2,1,0:T(8,128)(2,1)S(1)}, u32[]{:S(2)}, u32[]{:S(2)}) collective-permute-start(bf16[2,2,32,384]{3,2,1,0:T(8,128)(2,1)S(1)} %get-tuple-element.5), channel_id=1, source_target_pairs={{0,63},{1,32},{2,33},{3,34},{4,35},{5,36},{6,37},{7,38},{8,39},{9,... | collective-permute-start | bytes 294920 | tf_op jit(solution)/shard_map/ppermute | solution.py:28
  8.8 5.2 %collective-permute-start.2 = (bf16[2,2,32,384]{3,2,1,0:T(8,128)(2,1)S(1)}, bf16[2,2,32,384]{3,2,1,0:T(8,128)(2,1)S(1)}, u32[]{:S(2)}, u32[]{:S(2)}) collective-permute-start(bf16[2,2,32,384]{3,2,1,0:T(8,128)(2,1)S(1)} %get-tuple-element.5), channel_id=1, source_target_pairs={{0,31},{1,0},{2,1},{3,2},{4,3},{5,4},{6,5},{7,6},{8,7},{9,8},{10,9... | collective-permute-start | bytes 294920 | tf_op jit(solution)/shard_map/ppermute | solution.py:28
  9.6 11.0 %collective-permute-start.3 = (bf16[2,2,32,384]{3,2,1,0:T(8,128)(2,1)S(1)}, bf16[2,2,32,384]{3,2,1,0:T(8,128)(2,1)S(1)}, u32[]{:S(2)}, u32[]{:S(2)}) collective-permute-start(bf16[2,2,32,384]{3,2,1,0:T(8,128)(2,1)S(1)} %get-tuple-element.6), channel_id=1, source_target_pairs={{0,33},{1,34},{2,35},{3,36},{4,37},{5,38},{6,39},{7,40},{8,41},{9,... | collective-permute-start | bytes 294920 | tf_op jit(solution)/shard_map/ppermute | solution.py:28
  10.0 10.6 %collective-permute-start.1 = (bf16[2,2,32,384]{3,2,1,0:T(8,128)(2,1)S(1)}, bf16[2,2,32,384]{3,2,1,0:T(8,128)(2,1)S(1)}, u32[]{:S(2)}, u32[]{:S(2)}) collective-permute-start(bf16[2,2,32,384]{3,2,1,0:T(8,128)(2,1)S(1)} %get-tuple-element.6), channel_id=1, source_target_pairs={{0,1},{1,2},{2,3},{3,4},{4,5},{5,6},{6,7},{7,8},{8,9},{9,10},{10,1... | collective-permute-start | bytes 294920 | tf_op jit(solution)/shard_map/ppermute | solution.py:28
  20.6 1.0 %copy-start.1 = (bf16[2,6,32,384]{3,2,1,0:T(8,128)(2,1)S(1)}, bf16[2,6,32,384]{3,2,1,0:T(8,128)(2,1)}, u32[]{:S(2)}) copy-start(bf16[2,6,32,384]{3,2,1,0:T(8,128)(2,1)} %own.1) | copy-start | bytes 884740
  30.3 8.4 %collective-permute-start.5 = (bf16[2,8,32,384]{3,2,1,0:T(8,128)(2,1)S(1)}, bf16[2,8,32,384]{3,2,1,0:T(8,128)(2,1)S(1)}, u32[]{:S(2)}, u32[]{:S(2)}) collective-permute-start(bf16[2,8,32,384]{3,2,1,0:T(8,128)(2,1)S(1)} %residual.1.own), channel_id=1, source_target_pairs={{0,32},{1,33},{2,34},{3,35},{4,36},{5,37},{6,38},{7,39},{8,40},{9,... | collective-permute-start | bytes 1179656 | tf_op jit(solution)/shard_map/ppermute | solution.py:28
  32.9 5.9 %copy-start = (bf16[3,384,768]{2,1,0:T(8,128)(2,1)S(1)}, bf16[3,384,768]{2,1,0:T(8,128)(2,1)}, u32[]{:S(2)}) copy-start(bf16[3,384,768]{2,1,0:T(8,128)(2,1)} %time_weight.1) | copy-start | bytes 5308420

commit v2 on v0

v2 whole, which is shorter than its diff:
```python
import jax
import jax.numpy as jnp
from jax import lax
from jax.experimental import pallas as pl
from jax.experimental.pallas import tpu as pltpu
from jax.sharding import PartitionSpec as P

F32 = jnp.float32
BF16 = jnp.bfloat16
VMEM = pl.BlockSpec(memory_space=pltpu.VMEM)
SMEM = pl.BlockSpec(memory_space=pltpu.SMEM)
HBM = pl.BlockSpec(memory_space=pltpu.HBM)


def moved(block, sizes, target):
    nt, nr = sizes
    pairs = []
    for t in range(nt):
        for r in range(nr):
            to_t, to_r = target(t, r)
            pairs.append((t * nr + r, to_t * nr + to_r))
    return lax.ppermute(block, ("tm", "rows"), pairs)


def activated(values, gain):
    inv = lax.rsqrt(jnp.mean(values * values, axis=-1, keepdims=True) + 1e-06)
    half = values * inv * gain * 0.5
    return half + half * jnp.tanh(half)


def prepare_kernel(
    features, gain, up_weight, time_weight, res_weight,
    own, act, gain_out, combined, time_out, res_out,
    gain_in, up_in, small, large,
):
    ch = own.shape[-1]
    first = [
        pltpu.make_async_copy(features, own, small.at[0]),
        pltpu.make_async_copy(gain, gain_in, small.at[1]),
        pltpu.make_async_copy(up_weight, up_in, small.at[2]),
    ]
    second = [
        pltpu.make_async_copy(res_weight.at[kt], res_out.at[kt], large.at[kt]) for kt in range(3)
    ] + [pltpu.make_async_copy(time_weight, time_out, large.at[3])]
    for copy in first + second:
        copy.start()
    for copy in first:
        copy.wait()
    g = gain_in[...].reshape(1, ch)
    gain_out[...] = g
    act[...] = activated(own[...].astype(F32), g.reshape(1, 1, 1, ch)).astype(BF16)
    w = [[up_in[kh, kw].astype(F32) for kw in range(3)] for kh in range(3)]
    for phase in range(2):
        for tap in range(2):
            if phase == 0:
                r = w[0] if tap == 0 else [w[1][k] + w[2][k] for k in range(3)]
            else:
                r = [w[0][k] + w[1][k] for k in range(3)] if tap == 0 else w[2]
            block = jnp.concatenate([r[0], r[0] + r[1], r[1] + r[2], r[2]], axis=0)
            combined[phase, tap * ch : (tap + 1) * ch] = block.T.astype(BF16)
    for copy in second:
        copy.wait()


def columns_summed(acc, cols, ch):
    size = acc.shape[0]
    col = lax.broadcasted_iota(jnp.int32, (size, ch), 0) % cols
    left = jnp.where(col == 0, 0.0, pltpu.roll(acc[:, :ch], 1, 0))
    right = jnp.where(col == cols - 1, 0.0, pltpu.roll(acc[:, 2 * ch :], size - 1, 0))
    return left + acc[:, ch : 2 * ch] + right


def taps(windows, weight, first, count):
    ch = weight.shape[-1]
    lhs = jnp.concatenate(windows, axis=1)
    rhs = jnp.concatenate(
        [weight[first : first + count, :, kw].reshape(count * 3 * ch, ch) for kw in range(3)], axis=1
    )
    return jnp.dot(lhs, rhs, preferred_element_type=F32)


def inner_kernel(flags, act_own, own, prev, gain, weight, out, act_rim, act):
    rows, cols, ch = own.shape[1:]
    act[2:4] = act_own[...]
    keep = flags[0].astype(F32)
    act[0:2] = (activated(prev[...].astype(F32), gain[...].reshape(1, 1, 1, ch)) * keep).astype(BF16)
    act_rim[:, 0] = act[:, 0:2]
    act_rim[:, 1] = act[:, rows - 2 : rows]
    lines = rows - 2

    windows = [
        act[kt : kt + 2, kh : kh + lines].reshape(2 * lines * cols, ch)
        for kt in range(3)
        for kh in range(3)
    ]
    branch = columns_summed(taps(windows, weight, 0, 3), cols, ch).reshape(2, lines, cols, ch)
    out[...] = (own[:, 1 : rows - 1].astype(F32) + branch).astype(BF16)


def halo_kernel(flags, pair, cross, gain, out):
    ch = pair.shape[-1]
    odd = flags[3]
    inside = jnp.where(odd == 1, flags[2], flags[1]).astype(F32)
    g = gain[...].reshape(1, 1, 1, ch)
    out[:, 1 - odd] = activated(pair[...].astype(F32), g).astype(BF16)
    out[:, odd] = (activated(cross[...].astype(F32), g) * inside).astype(BF16)


def rim_windows(act, start, count, cols, ch):
    return [
        act[start : start + count, :, kh : kh + 2].reshape(count * 4 * cols, ch) for kh in range(3)
    ]


def rim_own_kernel(flags, act_rim, halo, own, pair, cross, weight, out, act):
    rows, cols, ch = own.shape[1:]
    odd = flags[3]
    act[:, 0, 0:2] = halo[:, 0]
    act[:, 0, 2:4] = act_rim[2:4, 0]
    act[:, 1, 0:2] = act_rim[2:4, 1]
    act[:, 1, 2:4] = halo[:, 1]
    both = taps(rim_windows(act, 0, 2, cols, ch), weight, 2, 1)
    late = taps(rim_windows(act, 0, 1, cols, ch), weight, 1, 1)
    half = late.shape[0]
    acc = jnp.concatenate([both[:half], both[half:] + late], axis=0)
    branch = columns_summed(acc, cols, ch).reshape(2, 2, 2, cols, ch)
    out[:, 0, 1] = own[:, 0].astype(F32) + branch[:, 0, 1]
    out[:, 1, 0] = own[:, rows - 1].astype(F32) + branch[:, 1, 0]
    above = jnp.where(odd == 1, pair[:, 1].astype(F32), cross[:, 1].astype(F32))
    below = jnp.where(odd == 1, cross[:, 0].astype(F32), pair[:, 0].astype(F32))
    out[:, 0, 0] = above + branch[:, 0, 0]
    out[:, 1, 1] = below + branch[:, 1, 1]


def rim_kernel(flags, act_rim, halo, partial, weight, out, act):
    cols, ch = partial.shape[3:]
    keep = flags[0].astype(BF16)
    act[:, 0, 0:2] = halo[:, 0] * keep
    act[:, 0, 2:4] = act_rim[0:2, 0]
    act[:, 1, 0:2] = act_rim[0:2, 1]
    act[:, 1, 2:4] = halo[:, 1] * keep
    both = taps(rim_windows(act, 0, 2, cols, ch), weight, 0, 1)
    early = taps(rim_windows(act, 1, 1, cols, ch), weight, 1, 1)
    half = early.shape[0]
    acc = jnp.concatenate([both[:half] + early, both[half:]], axis=0)
    blended = partial[...] + columns_summed(acc, cols, ch).reshape(2, 2, 2, cols, ch)
    out[:, 0, 0] = (blended[:, 0, 0] * flags[1].astype(F32)).astype(BF16)
    out[:, 0, 1] = blended[:, 0, 1].astype(BF16)
    out[:, 1, 0] = blended[:, 1, 0].astype(BF16)
    out[:, 1, 1] = (blended[:, 1, 1] * flags[2].astype(F32)).astype(BF16)


def time_upsampled(own, prev, keep, time_weight, stack):
    frames, lines, cols, ch = own.shape
    stack[2:4] = own
    stack[0:2] = prev * keep
    size = frames * lines * cols
    lhs = jnp.concatenate([stack[k : k + 2].reshape(size, ch) for k in range(3)], axis=1)
    doubled = jnp.dot(lhs, time_weight[...].reshape(3 * ch, 2 * ch), preferred_element_type=F32)
    return doubled.astype(BF16).reshape(frames, lines, cols, 2 * ch)


def woven_columns(upper, lower, weight, woven, cols, co):
    y = jnp.dot(jnp.concatenate([upper, lower], axis=1), weight, preferred_element_type=F32)
    size = y.shape[0]
    a, b = y[:, : 2 * co], y[:, 2 * co :]
    col = lax.broadcasted_iota(jnp.int32, (size, 2 * co), 0) % cols
    lane = lax.broadcasted_iota(jnp.int32, (size, 2 * co), 1)
    shift_a = jnp.where(col == 0, 0.0, pltpu.roll(a, 1, 0))
    shift_b = jnp.where(col == cols - 1, 0.0, pltpu.roll(b, size - 1, 0))
    z = jnp.where(lane < co, shift_a + b, a + shift_b)
    for parity, value in ((0, z), (1, pltpu.roll(z, co, 1))):
        for half in range(2):
            woven[half, pl.ds(parity, size, 2), :] = value[:, half * 128 : half * 128 + 128]

    def line(index):
        at = index * 2 * cols
        both = jnp.concatenate([woven[half, at : at + 2 * cols] for half in range(2)], axis=1)
        return both[:, :co].astype(BF16)

    return line


def up_inner_kernel(flags, own, prev, time_weight, weight, out, rim, stack, up, woven, stage, sem):
    frames, lines, cols, ch = own.shape
    co = out.shape[-1]
    keep = flags[0].astype(BF16)
    doubled = time_upsampled(own[...], prev[...], keep, time_weight, stack)
    for p in range(2):
        up[:, p] = doubled[..., p * ch : (p + 1) * ch]
    for p in range(2):
        rim[:, p, 0] = up[:, p, 0]
        rim[:, p, 1] = up[:, p, lines - 1]
    pairs = lines - 1
    size = 2 * frames * pairs * cols
    upper = up[:, :, 0:pairs].reshape(size, ch)
    lower = up[:, :, 1 : pairs + 1].reshape(size, ch)
    for phase in range(2):
        line = woven_columns(upper, lower, weight[phase], woven, cols, co)
        for f in range(2 * frames):
            for j in range(pairs):
                stage[f, 2 * j + 1 - phase] = line(f * pairs + j)
    copy = pltpu.make_async_copy(stage, out.at[:, 3 : 3 + 2 * pairs], sem)
    copy.start()
    copy.wait()


def up_rim_kernel(
    flags, own, prev, inner, time_weight, weight, partial, out, stack, up, woven, stage, sems
):
    del partial
    frames, sides, lines, cols, ch = own.shape
    co = out.shape[-1]
    keep = flags[0].astype(BF16)
    flat = (frames, sides * lines, cols, ch)
    doubled = time_upsampled(own[...].reshape(flat), prev[...].reshape(flat), keep, time_weight, stack)
    for p in range(2):
        part = doubled[..., p * ch : (p + 1) * ch]
        up[:, p, 0, 0:2] = part[:, 0:2]
        up[:, p, 1, 1:3] = part[:, 2:4]
        up[:, p, 0, 2] = inner[:, p, 0]
        up[:, p, 1, 0] = inner[:, p, 1]
    size = 2 * frames * 3 * cols
    last = out.shape[1] - 3
    for phase in range(2):
        picks = ((0, 0, 0), (0, 1, 2), (1, 0, 1)) if phase == 0 else ((0, 1, 1), (1, 0, 0), (1, 1, 2))

        def taken(step):
            lines_taken = [up[:, :, s, i + step : i + step + 1] for s, i, _ in picks]
            return jnp.concatenate(lines_taken, axis=2).reshape(size, ch)

        line = woven_columns(taken(0), taken(1), weight[phase], woven, cols, co)
        for f in range(2 * frames):
            for j, (s, _, at) in enumerate(picks):
                stage[s, f, at] = line(f * 3 + j)
    copies = [
        pltpu.make_async_copy(stage.at[s], out.at[:, start : start + 3], sems.at[s])
        for s, start in ((0, 0), (1, last))
    ]
    for copy in copies:
        copy.start()
    for copy in copies:
        copy.wait()


def call(kernel, name, shapes, specs, scratch, mib, args, in_out=None, out_specs=None, us=1):
    several = isinstance(shapes, list)
    return pl.pallas_call(
        kernel,
        out_shape=shapes,
        in_specs=specs,
        out_specs=out_specs if out_specs is not None else ([VMEM] * len(shapes) if several else VMEM),
        scratch_shapes=scratch,
        compiler_params=pltpu.CompilerParams(vmem_limit_bytes=mib * 2**20),
        cost_estimate=pl.CostEstimate(flops=us * 10**9, bytes_accessed=us * 3 * 10**9 // 1000, transcendentals=0),
        input_output_aliases=in_out or {},
        name=name,
    )(*args)


def vmem_out(shape, dtype):
    return pltpu.VMEM(shape, dtype)


def in_hbm(array):
    return pltpu.with_memory_space_constraint(array, pltpu.HBM)


def in_vmem(array):
    return pltpu.with_memory_space_constraint(array, pltpu.VMEM)


def shards(features, norm_gain, res_weight, time_weight, up_weight):
    frames, rows, cols, ch = features.shape
    nt, nr = lax.axis_size("tm"), lax.axis_size("rows")
    co = up_weight.shape[-1]
    t, r = lax.axis_index("tm"), lax.axis_index("rows")
    flags = jnp.stack([t > 0, r > 0, r < nr - 1, (r & 1) == 1]).astype(jnp.int32)
    sizes = (nt, nr)
    shape = jax.ShapeDtypeStruct

    def paired(r):
        return r ^ 1

    def crossed(r):
        return min(max((r + 1 ^ 1) - 1, 0), nr - 1)

    def later(block):
        return moved(block, sizes, lambda t, r: ((t + 1) % nt, r))

    prev = later(features)
    odd = (r & 1) == 1
    top, bottom = features[:, :2], features[:, -2:]
    to_pair = jnp.where(odd, top, bottom)
    to_cross = jnp.where(odd, bottom, top)
    cross = moved(to_cross, sizes, lambda t, r: (t, crossed(r)))
    pair = moved(to_pair, sizes, lambda t, r: (t, paired(r)))
    up_turned = jnp.swapaxes(up_weight, 2, 3)
    own, act_own, gain, combined, time_held, res_held = call(
        prepare_kernel,
        "prepare",
        [
            vmem_out(features.shape, BF16),
            vmem_out(features.shape, BF16),
            vmem_out((1, ch), F32),
            vmem_out((2, 2 * ch, 4 * co), BF16),
            vmem_out(time_weight.shape, BF16),
            vmem_out(res_weight.shape, BF16),
        ],
        [HBM] * 5,
        [
            pltpu.VMEM((ch,), F32),
            pltpu.VMEM(up_turned.shape, BF16),
            pltpu.SemaphoreType.DMA((3,)),
            pltpu.SemaphoreType.DMA((4,)),
        ],
        24,
        tuple(in_hbm(a) for a in (features, norm_gain, up_turned, time_weight, res_weight)),
    )
    halo = call(
        halo_kernel,
        "halo",
        vmem_out((2, 2, 2, cols, ch), BF16),
        [SMEM] + [VMEM] * 3,
        [],
        8,
        (flags, pair, cross, gain),
    )
    prev_halo = later(halo)
    lines = rows - 2
    inner, act_rim = call(
        inner_kernel,
        "inner",
        [shape((2, lines, cols, ch), BF16), shape((4, 2, 2, cols, ch), BF16)],
        [SMEM] + [VMEM] * 5,
        [pltpu.VMEM((4, rows, cols, ch), BF16)],
        16,
        (flags, act_own, own, prev, gain, in_vmem(res_held)),
    )
    inner_prev = later(inner)
    side_rows = [pltpu.VMEM((2, 2, 4, cols, ch), BF16)]
    rim_own = call(
        rim_own_kernel,
        "rim_own",
        vmem_out((2, 2, 2, cols, ch), F32),
        [SMEM] + [VMEM] * 6,
        side_rows,
        16,
        (flags, act_rim, halo, own, pair, cross, in_vmem(res_held)),
    )
    rim = call(
        rim_kernel,
        "rim",
        shape((2, 2, 2, cols, ch), BF16),
        [SMEM] + [VMEM] * 4,
        side_rows,
        16,
        (flags, act_rim, prev_halo, rim_own, in_vmem(res_held)),
    )
    rim_prev = later(rim)
    out_shape = shape((2 * frames, 2 * rows, 2 * cols, co), BF16)
    partial, up_rim = call(
        up_inner_kernel,
        "up_inner",
        [out_shape, shape((2, 2, 2, cols, ch), BF16)],
        [SMEM] + [VMEM] * 4,
        [
            pltpu.VMEM((4, lines, cols, ch), BF16),
            pltpu.VMEM((2, 2, lines, cols, ch), BF16),
            pltpu.VMEM((2, 2 * frames * (lines - 1) * 2 * cols, 128), F32),
            pltpu.VMEM((2 * frames, 2 * (lines - 1), 2 * cols, co), BF16),
            pltpu.SemaphoreType.DMA,
        ],
        24,
        (flags, inner, inner_prev, in_vmem(time_held), in_vmem(combined)),
        out_specs=[HBM, VMEM],
    )
    return call(
        up_rim_kernel,
        "up_rim",
        out_shape,
        [SMEM] + [VMEM] * 5 + [HBM],
        [
            pltpu.VMEM((4, 4, cols, ch), BF16),
            pltpu.VMEM((2, 2, 2, 3, cols, ch), BF16),
            pltpu.VMEM((2, 2 * frames * 3 * 2 * cols, 128), F32),
            pltpu.VMEM((2, 2 * frames, 3, 2 * cols, co), BF16),
            pltpu.SemaphoreType.DMA((2,)),
        ],
        24,
        (flags, rim, rim_prev, up_rim, in_vmem(time_held), in_vmem(combined), partial),
        in_out={6: 0},
        out_specs=HBM,
    )


def solution(mesh):
    placed = (P("tm", "rows", None, None), P(), P(), P(), P())
    return jax.shard_map(
        shards, mesh=mesh, in_specs=placed, out_specs=P("tm", "rows", None, None), check_vma=False
    )
```

time: 83 us -> 31.8 us (0.38)
  the two profiles are of different devices: /device:TPU:122 before, /device:TPU:192 now
where the time goes in v2:
time: 31.8 us; the launch traced here: 31.5 us
  Pallas kernels  20.2 us (64%)
  starting transfers between devices  8.01 us (25%)
  waiting for transfers between devices  2.15 us (7%)
  other arithmetic  1.04 us (3%)
    pallas_call x7, Pallas kernels, call(): pl.pallas_call(kernel, out_shape=shapes, in_specs=specs, out_specs=out_sp...  20.2 us
    ppermute x6, starting transfers between devices, moved(): return lax.ppermute(block, ('tm', 'rows'), pairs)  8.01 us
    ppermute x6, waiting for transfers between devices, moved(): return lax.ppermute(block, ('tm', 'rows'), pairs)  2.15 us
    select_n x1, other arithmetic, shards(): to_cross = jnp.where(odd, bottom, top)  0.97 us
  transfers between devices with their start and end apart: 6, of which 3 were waited for; matrix products, arithmetic and copies ran while one was open for 3% of the time, Pallas kernels for 53%

profile of v2, /device:TPU:192, one launch (start us, length us, event | category | flops | bytes accessed | tf_op | source)
XLA Modules:
  0.0 31.5 jit_solution(381333939044548392)
XLA Ops:
  0.0 0.0 collective-permute-start
  0.0 1.0 %broadcast_select_fusion = (bf16[2,2,32,384]{3,2,1,0:T(8,128)(2,1)S(1)}, bf16[2,2,32,384]{3,2,1,0:T(8,128)(2,1)S(1)}) fusion(pred[]{:T(512)} %eq.4, bf16[2,6,32,384]{3,2,1,0:T(8,128)(2,1)} %features.1), kind=kLoop, calls=%fused_computation | loop fusion | flops 98304 | bytes 393217 | tf_op jit(solution)/shard_map/jit(_where)/select_n | solution.py:295
  1.0 5.4 %collective-permute-start.2 = (bf16[2,2,32,384]{3,2,1,0:T(8,128)(2,1)S(1)}, bf16[2,2,32,384]{3,2,1,0:T(8,128)(2,1)S(1)}, u32[]{:S(2)}, u32[]{:S(2)}) collective-permute-start(bf16[2,2,32,384]{3,2,1,0:T(8,128)(2,1)S(1)} %get-tuple-element.25), channel_id=1, source_target_pairs={{0,0},{1,2},{2,1},{3,4},{4,3},{5,6},{6,5},{7,8},{8,7},{9,10},{10,9... | collective-permute-start | bytes 294920 | tf_op jit(solution)/shard_map/ppermute | solution.py:22
  6.3 0.1 collective-permute-start.1
  6.5 0.1 add_convert_fusion.flags
  6.5 4.8 %prepare.1 = (bf16[2,6,32,384]{3,2,1,0:T(8,128)(2,1)S(1)}, bf16[2,6,32,384]{3,2,1,0:T(8,128)(2,1)S(1)}, f32[1,384]{1,0:T(1,128)S(1)}, bf16[2,768,768]{2,1,0:T(8,...) custom-call(bf16[2,6,32,384]{3,2,1,0:T(8,128)(2,1)} %features.1, f32[384]{0:T(512)} %gain.1, ...), custom_call_target="tpu_custom_call" | custom-call | flops 1000000000 | bytes 3000000 | tf_op jit(solution)/shard_map/prepare/pallas_call | solution.py:248
  11.4 0.0 collective-permute-done.2.cross
  11.4 0.4 %collective-permute-done.1.pair = bf16[2,2,32,384]{3,2,1,0:T(8,128)(2,1)S(1)} collective-permute-done((bf16[2,2,32,384]{3,2,1,0:T(8,128)(2,1)S(1)}, bf16[2,2,32,384]{3,2,1,0:T(8,128)(2,1)S(1)}, u32[]{:S(2)}, u32[]{:S(2)}) %collective-permute-start.1) | collective-permute-done | bytes 98336 | tf_op jit(solution)/shard_map/ppermute | solution.py:22
  11.8 0.8 %halo.1 = bf16[2,2,2,32,384]{4,3,2,1,0:T(8,128)(2,1)S(1)} custom-call(s32[4]{0:T(128)S(1)} %add_convert_fusion.flags, bf16[2,2,32,384]{3,2,1,0:T(8,128)(2,1)S(1)} %collective-permute-done.1.pair, bf16[2,2,32,384]{3,2,1,0:T(8,128)(2,1)S(1)} %collective-permute-done.2.cross, f32[1,384]{1,0:T(1,128)S(1)} %get-tuple-element.17.gain), custom_call_target="tpu_custom_call" | custom-call | flops 1000000000 | bytes 3000000 | tf_op jit(solution)/shard_map/halo/pallas_call | solution.py:248
  12.6 0.9 %collective-permute-start.3 = (bf16[2,2,2,32,384]{4,3,2,1,0:T(8,128)(2,1)S(1)}, bf16[2,2,2,32,384]{4,3,2,1,0:T(8,128)(2,1)S(1)}, u32[]{:S(2)}, u32[]{:S(2)}) collective-permute-start(bf16[2,2,2,32,384]{4,3,2,1,0:T(8,128)(2,1)S(1)} %halo.1), channel_id=1, source_target_pairs={{0,32},{1,33},{2,34},{3,35},{4,36},{5,37},{6,38},{7,39},{8,40},{9,... | collective-permute-start | bytes 589832 | tf_op jit(solution)/shard_map/ppermute | solution.py:22
  13.5 0.0 collective-permute-done.prev
  13.5 3.3 %inner.1 = (bf16[2,4,32,384]{3,2,1,0:T(8,128)(2,1)S(1)}, bf16[4,2,2,32,384]{4,3,2,1,0:T(8,128)(2,1)S(1)}) custom-call(s32[4]{0:T(128)S(1)} %add_convert_fusion.flags, bf16[2,6,32,384]{3,2,1,0:T(8,128)(2,1)S(1)} %get-tuple-element.15.act_own, bf16[2,6,32,384]{3,2,1,0:T(8,128)(2,1)S(1)} %get-tuple-element.16.own, ...), custom_call_target="tpu_custom_call" | custom-call | flops 1000000000 | bytes 3000000 | tf_op jit(solution)/shard_map/inner/pallas_call | solution.py:248
  16.8 0.7 %collective-permute-start.5 = (bf16[2,4,32,384]{3,2,1,0:T(8,128)(2,1)S(1)}, bf16[2,4,32,384]{3,2,1,0:T(8,128)(2,1)S(1)}, u32[]{:S(2)}, u32[]{:S(2)}) collective-permute-start(bf16[2,4,32,384]{3,2,1,0:T(8,128)(2,1)S(1)} %get-tuple-element.20.own), channel_id=1, source_target_pairs={{0,32},{1,33},{2,34},{3,35},{4,36},{5,37},{6,38},{7,39},{8,40},{9,... | collective-permute-start | bytes 589832 | tf_op jit(solution)/shard_map/ppermute | solution.py:22
  17.5 2.0 %rim_own.1.partial = f32[2,2,2,32,384]{4,3,2,1,0:T(8,128)S(1)} custom-call(s32[4]{0:T(128)S(1)} %add_convert_fusion.flags, bf16[4,2,2,32,384]{4,3,2,1,0:T(8,128)(2,1)S(1)} %get-tuple-element.19.act_rim, bf16[2,2,2,32,384]{4,3,2,1,0:T(8,128)(2,1)S(1)} %halo.1, bf16[2,6,32,384]{3,2,1,0:T(8,128)(2,1)S(1)} %get-tuple-element.16.own, ...), custom_call_target="tpu_custom_call" | custom-call | flops 1000000000 | bytes 3000000 | tf_op jit(solution)/shard_map/rim_own/pallas_call | solution.py:248
  19.5 0.0 collective-permute-done.3.halo
  19.5 2.0 %rim.1.own = bf16[2,2,2,32,384]{4,3,2,1,0:T(8,128)(2,1)S(1)} custom-call(s32[4]{0:T(128)S(1)} %add_convert_fusion.flags, bf16[4,2,2,32,384]{4,3,2,1,0:T(8,128)(2,1)S(1)} %get-tuple-element.19.act_rim, bf16[2,2,2,32,384]{4,3,2,1,0:T(8,128)(2,1)S(1)} %collective-permute-done.3.halo, f32[2,2,2,32,384]{4,3,2,1,0:T(8,128)S(1)} %rim_own.1.partial, ...), custom_call_target="tpu_custom_call" | custom-call | flops 1000000000 | bytes 3000000 | tf_op jit(solution)/shard_map/rim/pallas_call | solution.py:248
  21.5 0.9 %collective-permute-start.4 = (bf16[2,2,2,32,384]{4,3,2,1,0:T(8,128)(2,1)S(1)}, bf16[2,2,2,32,384]{4,3,2,1,0:T(8,128)(2,1)S(1)}, u32[]{:S(2)}, u32[]{:S(2)}) collective-permute-start(bf16[2,2,2,32,384]{4,3,2,1,0:T(8,128)(2,1)S(1)} %rim.1.own), channel_id=1, source_target_pairs={{0,32},{1,33},{2,34},{3,35},{4,36},{5,37},{6,38},{7,39},{8,40},{9,... | collective-permute-start | bytes 589832 | tf_op jit(solution)/shard_map/ppermute | solution.py:22
  22.4 0.7 %collective-permute-done.5.prev = bf16[2,4,32,384]{3,2,1,0:T(8,128)(2,1)S(1)} collective-permute-done((bf16[2,4,32,384]{3,2,1,0:T(8,128)(2,1)S(1)}, bf16[2,4,32,384]{3,2,1,0:T(8,128)(2,1)S(1)}, u32[]{:S(2)}, u32[]{:S(2)}) %collective-permute-start.5) | collective-permute-done | bytes 196640 | tf_op jit(solution)/shard_map/ppermute | solution.py:22
  23.1 3.7 %up_inner.1 = (bf16[4,12,64,192]{3,2,1,0:T(8,128)(2,1)}, bf16[2,2,2,32,384]{4,3,2,1,0:T(8,128)(2,1)S(1)}) custom-call(s32[4]{0:T(128)S(1)} %add_convert_fusion.flags, bf16[2,4,32,384]{3,2,1,0:T(8,128)(2,1)S(1)} %get-tuple-element.20.own, bf16[2,4,32,384]{3,2,1,0:T(8,128)(2,1)S(1)} %collective-permute-done.5.prev, ...), custom_call_target="tpu_custom_call" | custom-call | flops 1000000000 | bytes 3000000 | tf_op jit(solution)/shard_map/up_inner/pallas_call | solution.py:248
  26.8 1.0 %collective-permute-done.4.prev = bf16[2,2,2,32,384]{4,3,2,1,0:T(8,128)(2,1)S(1)} collective-permute-done((bf16[2,2,2,32,384]{4,3,2,1,0:T(8,128)(2,1)S(1)}, bf16[2,2,2,32,384]{4,3,2,1,0:T(8,128)(2,1)S(1)}, u32[]{:S(2)}, u32[]{:S(2)}) %collective-permute-start.4) | collective-permute-done | bytes 196640 | tf_op jit(solution)/shard_map/ppermute | solution.py:22
  27.8 3.7 %up_rim.1 = bf16[4,12,64,192]{3,2,1,0:T(8,128)(2,1)} custom-call(s32[4]{0:T(128)S(1)} %add_convert_fusion.flags, bf16[2,2,2,32,384]{4,3,2,1,0:T(8,128)(2,1)S(1)} %rim.1.own, bf16[2,2,2,32,384]{4,3,2,1,0:T(8,128)(2,1)S(1)} %collective-permute-done.4.prev, bf16[2,2,2,32,384]{4,3,2,1,0:T(8,128)(2,1)S(1)} %get-tuple-element.23.inner, ...), custom_call_target="tpu_custom_call", output_to_operand_aliasing={{}: (6, {})} | custom-call | flops 1000000000 | bytes 3000000 | tf_op jit(solution)/shard_map/up_rim/pallas_call | solution.py:248
Async XLA Ops:
  0.0 13.5 %collective-permute-start = (bf16[2,6,32,384]{3,2,1,0:T(8,128)(2,1)}, bf16[2,6,32,384]{3,2,1,0:T(8,128)(2,1)S(1)}, u32[]{:S(2)}, u32[]{:S(2)}) collective-permute-start(bf16[2,6,32,384]{3,2,1,0:T(8,128)(2,1)} %features.1), channel_id=1, source_target_pairs={{0,32},{1,33},{2,34},{3,35},{4,36},{5,37},{6,38},{7,39},{8,40},{9,... | collective-permute-start | bytes 884744 | tf_op jit(solution)/shard_map/ppermute | solution.py:22
  1.0 10.4 %collective-permute-start.2 = (bf16[2,2,32,384]{3,2,1,0:T(8,128)(2,1)S(1)}, bf16[2,2,32,384]{3,2,1,0:T(8,128)(2,1)S(1)}, u32[]{:S(2)}, u32[]{:S(2)}) collective-permute-start(bf16[2,2,32,384]{3,2,1,0:T(8,128)(2,1)S(1)} %get-tuple-element.25), channel_id=1, source_target_pairs={{0,0},{1,2},{2,1},{3,4},{4,3},{5,6},{6,5},{7,8},{8,7},{9,10},{10,9... | collective-permute-start | bytes 294920 | tf_op jit(solution)/shard_map/ppermute | solution.py:22
  6.3 5.5 %collective-permute-start.1 = (bf16[2,2,32,384]{3,2,1,0:T(8,128)(2,1)S(1)}, bf16[2,2,32,384]{3,2,1,0:T(8,128)(2,1)S(1)}, u32[]{:S(2)}, u32[]{:S(2)}) collective-permute-start(bf16[2,2,32,384]{3,2,1,0:T(8,128)(2,1)S(1)} %get-tuple-element.26), channel_id=1, source_target_pairs={{0,1},{1,0},{2,3},{3,2},{4,5},{5,4},{6,7},{7,6},{8,9},{9,8},{10,11... | collective-permute-start | bytes 294920 | tf_op jit(solution)/shard_map/ppermute | solution.py:22
  12.6 7.0 %collective-permute-start.3 = (bf16[2,2,2,32,384]{4,3,2,1,0:T(8,128)(2,1)S(1)}, bf16[2,2,2,32,384]{4,3,2,1,0:T(8,128)(2,1)S(1)}, u32[]{:S(2)}, u32[]{:S(2)}) collective-permute-start(bf16[2,2,2,32,384]{4,3,2,1,0:T(8,128)(2,1)S(1)} %halo.1), channel_id=1, source_target_pairs={{0,32},{1,33},{2,34},{3,35},{4,36},{5,37},{6,38},{7,39},{8,40},{9,... | collective-permute-start | bytes 589832 | tf_op jit(solution)/shard_map/ppermute | solution.py:22
  16.8 6.3 %collective-permute-start.5 = (bf16[2,4,32,384]{3,2,1,0:T(8,128)(2,1)S(1)}, bf16[2,4,32,384]{3,2,1,0:T(8,128)(2,1)S(1)}, u32[]{:S(2)}, u32[]{:S(2)}) collective-permute-start(bf16[2,4,32,384]{3,2,1,0:T(8,128)(2,1)S(1)} %get-tuple-element.20.own), channel_id=1, source_target_pairs={{0,32},{1,33},{2,34},{3,35},{4,36},{5,37},{6,38},{7,39},{8,40},{9,... | collective-permute-start | bytes 589832 | tf_op jit(solution)/shard_map/ppermute | solution.py:22
  21.5 6.3 %collective-permute-start.4 = (bf16[2,2,2,32,384]{4,3,2,1,0:T(8,128)(2,1)S(1)}, bf16[2,2,2,32,384]{4,3,2,1,0:T(8,128)(2,1)S(1)}, u32[]{:S(2)}, u32[]{:S(2)}) collective-permute-start(bf16[2,2,2,32,384]{4,3,2,1,0:T(8,128)(2,1)S(1)} %rim.1.own), channel_id=1, source_target_pairs={{0,32},{1,33},{2,34},{3,35},{4,36},{5,37},{6,38},{7,39},{8,40},{9,... | collective-permute-start | bytes 589832 | tf_op jit(solution)/shard_map/ppermute | solution.py:22

commit v3 on v2

v3 whole, which is shorter than its diff:
```python
import jax
import jax.numpy as jnp
from jax import lax
from jax.experimental import pallas as pl
from jax.experimental.pallas import tpu as pltpu
from jax.sharding import PartitionSpec as P

F32 = jnp.float32
BF16 = jnp.bfloat16
VMEM = pl.BlockSpec(memory_space=pltpu.VMEM)
SMEM = pl.BlockSpec(memory_space=pltpu.SMEM)
HBM = pl.BlockSpec(memory_space=pltpu.HBM)


def moved(block, sizes, target):
    nt, nr = sizes
    pairs = []
    for t in range(nt):
        for r in range(nr):
            to_t, to_r = target(t, r)
            pairs.append((t * nr + r, to_t * nr + to_r))
    return lax.ppermute(block, ("tm", "rows"), pairs)


def activated(values, gain):
    inv = lax.rsqrt(jnp.mean(values * values, axis=-1, keepdims=True) + 1e-06)
    half = values * inv * gain * 0.5
    return half + half * jnp.tanh(half)


def inner_windows(act, start, count, cols, ch):
    lines = act.shape[1] - 2
    return [
        act[start : start + count, kh : kh + lines].reshape(count * lines * cols, ch)
        for kh in range(3)
    ]


def prepare_kernel(
    features, gain, res_weight, own, act, gain_out, res_held, partial, gain_in, sems
):
    rows, cols, ch = own.shape[1:]
    copies = [
        pltpu.make_async_copy(source, target, sems.at[i])
        for i, (source, target) in enumerate(
            ((gain, gain_in), (features, own))
            + tuple((res_weight.at[kt], res_held.at[kt]) for kt in (2, 1, 0))
        )
    ]
    for copy in copies:
        copy.start()
    copies[0].wait()
    copies[1].wait()
    g = gain_in[...].reshape(1, ch)
    gain_out[...] = g
    act[...] = activated(own[...].astype(F32), g.reshape(1, 1, 1, ch)).astype(BF16)
    copies[2].wait()
    both = taps(inner_windows(act, 0, 2, cols, ch), res_held.at[2])
    copies[3].wait()
    late = taps(inner_windows(act, 0, 1, cols, ch), res_held.at[1])
    half = late.shape[0]
    acc = jnp.concatenate([both[:half], both[half:] + late], axis=0)
    branch = columns_summed(acc, cols, ch).reshape(2, rows - 2, cols, ch)
    partial[...] = own[:, 1 : rows - 1].astype(F32) + branch
    copies[4].wait()


def combine_kernel(up_weight, time_weight, after, combined, time_out, up_in, sems):
    del after
    ch = time_out.shape[1]
    copies = [
        pltpu.make_async_copy(source, target, sems.at[i])
        for i, (source, target) in enumerate(((up_weight, up_in), (time_weight, time_out)))
    ]
    for copy in copies:
        copy.start()
    copies[0].wait()
    w = [[up_in[kh, kw].astype(F32) for kw in range(3)] for kh in range(3)]
    for phase in range(2):
        for tap in range(2):
            if phase == 0:
                r = w[0] if tap == 0 else [w[1][k] + w[2][k] for k in range(3)]
            else:
                r = [w[0][k] + w[1][k] for k in range(3)] if tap == 0 else w[2]
            block = jnp.concatenate([r[0], r[0] + r[1], r[1] + r[2], r[2]], axis=0)
            combined[phase, tap * ch : (tap + 1) * ch] = block.T.astype(BF16)
    copies[1].wait()


def columns_summed(acc, cols, ch):
    size = acc.shape[0]
    col = lax.broadcasted_iota(jnp.int32, (size, ch), 0) % cols
    left = jnp.where(col == 0, 0.0, pltpu.roll(acc[:, :ch], 1, 0))
    right = jnp.where(col == cols - 1, 0.0, pltpu.roll(acc[:, 2 * ch :], size - 1, 0))
    return left + acc[:, ch : 2 * ch] + right


def taps(windows, weight):
    ch = weight.shape[-1]
    lhs = jnp.concatenate(windows, axis=1)
    rhs = jnp.concatenate([weight[:, kw].reshape(3 * ch, ch) for kw in range(3)], axis=1)
    return jnp.dot(lhs, rhs, preferred_element_type=F32)


def inner_kernel(flags, prev, gain, res_held, partial, out, act):
    rows, cols, ch = act.shape[1:]
    keep = flags[0].astype(F32)
    act[...] = (activated(prev[...].astype(F32), gain[...].reshape(1, 1, 1, ch)) * keep).astype(BF16)
    both = taps(inner_windows(act, 0, 2, cols, ch), res_held.at[0])
    early = taps(inner_windows(act, 1, 1, cols, ch), res_held.at[1])
    half = early.shape[0]
    acc = jnp.concatenate([both[:half] + early, both[half:]], axis=0)
    branch = columns_summed(acc, cols, ch).reshape(2, rows - 2, cols, ch)
    out[...] = (partial[...] + branch).astype(BF16)


def halo_kernel(flags, cross, pair, gain, out):
    ch = pair.shape[-1]
    odd = flags[3]
    inside = jnp.where(odd == 1, flags[2], flags[1]).astype(F32)
    g = gain[...].reshape(1, 1, 1, ch)
    out[:, 1 - odd] = activated(pair[...].astype(F32), g).astype(BF16)
    out[:, odd] = (activated(cross[...].astype(F32), g) * inside).astype(BF16)


def rim_windows(act, start, count, cols, ch):
    return [
        act[start : start + count, :, kh : kh + 2].reshape(count * 4 * cols, ch) for kh in range(3)
    ]


def rim_own_kernel(flags, act_own, halo, own, cross, pair, res_held, out, act):
    rows, cols, ch = own.shape[1:]
    odd = flags[3]
    act[:, 0, 0:2] = halo[:, 0]
    act[:, 0, 2:4] = act_own[:, 0:2]
    act[:, 1, 0:2] = act_own[:, rows - 2 : rows]
    act[:, 1, 2:4] = halo[:, 1]
    both = taps(rim_windows(act, 0, 2, cols, ch), res_held.at[2])
    late = taps(rim_windows(act, 0, 1, cols, ch), res_held.at[1])
    half = late.shape[0]
    acc = jnp.concatenate([both[:half], both[half:] + late], axis=0)
    branch = columns_summed(acc, cols, ch).reshape(2, 2, 2, cols, ch)
    out[:, 0, 1] = own[:, 0].astype(F32) + branch[:, 0, 1]
    out[:, 1, 0] = own[:, rows - 1].astype(F32) + branch[:, 1, 0]
    above = jnp.where(odd == 1, pair[:, 1].astype(F32), cross[:, 1].astype(F32))
    below = jnp.where(odd == 1, cross[:, 0].astype(F32), pair[:, 0].astype(F32))
    out[:, 0, 0] = above + branch[:, 0, 0]
    out[:, 1, 1] = below + branch[:, 1, 1]


def rim_kernel(flags, act_prev, halo, partial, res_held, out, act):
    rows = act_prev.shape[1]
    cols, ch = partial.shape[3:]
    keep = flags[0].astype(BF16)
    act[:, 0, 0:2] = halo[:, 0] * keep
    act[:, 0, 2:4] = act_prev[:, 0:2]
    act[:, 1, 0:2] = act_prev[:, rows - 2 : rows]
    act[:, 1, 2:4] = halo[:, 1] * keep
    both = taps(rim_windows(act, 0, 2, cols, ch), res_held.at[0])
    early = taps(rim_windows(act, 1, 1, cols, ch), res_held.at[1])
    half = early.shape[0]
    acc = jnp.concatenate([both[:half] + early, both[half:]], axis=0)
    blended = partial[...] + columns_summed(acc, cols, ch).reshape(2, 2, 2, cols, ch)
    out[:, 0, 0] = (blended[:, 0, 0] * flags[1].astype(F32)).astype(BF16)
    out[:, 0, 1] = blended[:, 0, 1].astype(BF16)
    out[:, 1, 0] = blended[:, 1, 0].astype(BF16)
    out[:, 1, 1] = (blended[:, 1, 1] * flags[2].astype(F32)).astype(BF16)


def time_products(windows, weight, first):
    ch = weight.shape[1]
    count = len(windows)
    lhs = jnp.concatenate(windows, axis=1) if count > 1 else windows[0]
    rhs = weight[first : first + count].reshape(count * ch, 2 * ch)
    return jnp.dot(lhs, rhs, preferred_element_type=F32)


def woven_columns(upper, lower, weight, woven, cols, co):
    y = jnp.dot(jnp.concatenate([upper, lower], axis=1), weight, preferred_element_type=F32)
    size = y.shape[0]
    a, b = y[:, : 2 * co], y[:, 2 * co :]
    col = lax.broadcasted_iota(jnp.int32, (size, 2 * co), 0) % cols
    lane = lax.broadcasted_iota(jnp.int32, (size, 2 * co), 1)
    shift_a = jnp.where(col == 0, 0.0, pltpu.roll(a, 1, 0))
    shift_b = jnp.where(col == cols - 1, 0.0, pltpu.roll(b, size - 1, 0))
    z = jnp.where(lane < co, shift_a + b, a + shift_b)
    for parity, value in ((0, z), (1, pltpu.roll(z, co, 1))):
        for half in range(2):
            woven[half, pl.ds(parity, size, 2), :] = value[:, half * 128 : half * 128 + 128]

    def line(index):
        at = index * 2 * cols
        both = jnp.concatenate([woven[half, at : at + 2 * cols] for half in range(2)], axis=1)
        return both[:, :co].astype(BF16)

    return line


def up_inner_kernel(flags, own, prev, rim_own, time_weight, weight, stage, inner_rim, rim_part, stack, up, woven):
    frames, lines, cols, ch = own.shape
    co = stage.shape[-1]
    stack[2:4] = own[...]
    stack[0:2] = prev[...] * flags[0].astype(BF16)
    size = frames * lines * cols
    windows = [stack[k : k + 2].reshape(size, ch) for k in range(3)]
    doubled = time_products(windows, time_weight, 0).astype(BF16).reshape(frames, lines, cols, 2 * ch)
    for p in range(2):
        up[:, p] = doubled[..., p * ch : (p + 1) * ch]
    for p in range(2):
        inner_rim[:, p, 0] = up[:, p, 0]
        inner_rim[:, p, 1] = up[:, p, lines - 1]
    pairs = lines - 1
    size = 2 * frames * pairs * cols
    upper = up[:, :, 0:pairs].reshape(size, ch)
    lower = up[:, :, 1 : pairs + 1].reshape(size, ch)
    for phase in range(2):
        line = woven_columns(upper, lower, weight[phase], woven, cols, co)
        for f in range(2 * frames):
            for j in range(pairs):
                stage[f, 2 * j + 1 - phase] = line(f * pairs + j)
    half = rim_own.shape[1] * rim_own.shape[2] * cols
    first = rim_own[0].reshape(half, ch)
    rim_part[0:half] = time_products([first], time_weight, 2)
    rim_part[half:] = time_products([first, rim_own[1].reshape(half, ch)], time_weight, 1)


def up_rim_kernel(
    flags, part, prev, inner_rim, inner_stage, time_weight, weight, out, up, woven, stage, sems
):
    frames, sides, lines, cols, ch = prev.shape
    co = out.shape[-1]
    middle = pltpu.make_async_copy(inner_stage, out.at[:, 3 : 3 + inner_stage.shape[1]], sems.at[6])
    middle.start()
    keep = flags[0].astype(BF16)
    half = sides * lines * cols
    before = prev[0].reshape(half, ch) * keep
    last = prev[1].reshape(half, ch) * keep
    products = (
        part[0:half] + time_products([before, last], time_weight, 0),
        part[half:] + time_products([last], time_weight, 0),
    )
    for frame in range(frames):
        doubled = products[frame].astype(BF16).reshape(sides * lines, cols, 2 * ch)
        for p in range(2):
            lot = doubled[..., p * ch : (p + 1) * ch]
            up[frame, p, 0, 0:2] = lot[0:2]
            up[frame, p, 1, 1:3] = lot[2:4]
            up[frame, p, 0, 2] = inner_rim[frame, p, 0]
            up[frame, p, 1, 0] = inner_rim[frame, p, 1]
    size = 2 * frames * 3 * cols
    start = out.shape[1] - 3
    copies = [middle]
    for phase in range(2):
        if phase == 0:
            picks = ((0, 0, 0), (0, 1, 2), (1, 0, start + 1))
        else:
            picks = ((0, 1, 1), (1, 0, start), (1, 1, start + 2))

        def taken(step):
            lines_taken = [up[:, :, s, i + step : i + step + 1] for s, i, _ in picks]
            return jnp.concatenate(lines_taken, axis=2).reshape(size, ch)

        line = woven_columns(taken(0), taken(1), weight[phase], woven, cols, co)
        for j, (_, _, row) in enumerate(picks):
            for f in range(2 * frames):
                stage[phase, j, f, 0] = line(f * 3 + j)
            copy = pltpu.make_async_copy(
                stage.at[phase, j], out.at[:, row : row + 1], sems.at[phase * 3 + j]
            )
            copy.start()
            copies.append(copy)
    for copy in copies:
        copy.wait()


def call(kernel, name, shapes, specs, scratch, mib, args, out_specs=None, us=1):
    several = isinstance(shapes, list)
    return pl.pallas_call(
        kernel,
        out_shape=shapes,
        in_specs=specs,
        out_specs=out_specs if out_specs is not None else ([VMEM] * len(shapes) if several else VMEM),
        scratch_shapes=scratch,
        compiler_params=pltpu.CompilerParams(vmem_limit_bytes=mib * 2**20),
        cost_estimate=pl.CostEstimate(flops=us * 10**9, bytes_accessed=us * 3 * 10**9 // 1000, transcendentals=0),
        name=name,
    )(*args)


def vmem_out(shape, dtype):
    return pltpu.VMEM(shape, dtype)


def in_hbm(array):
    return pltpu.with_memory_space_constraint(array, pltpu.HBM)


def in_vmem(array):
    return pltpu.with_memory_space_constraint(array, pltpu.VMEM)


def shards(features, norm_gain, res_weight, time_weight, up_weight):
    frames, rows, cols, ch = features.shape
    nt, nr = lax.axis_size("tm"), lax.axis_size("rows")
    co = up_weight.shape[-1]
    t, r = lax.axis_index("tm"), lax.axis_index("rows")
    flags = jnp.stack([t > 0, r > 0, r < nr - 1, (r & 1) == 1]).astype(jnp.int32)
    sizes = (nt, nr)
    shape = jax.ShapeDtypeStruct

    def paired(r):
        return r ^ 1

    def crossed(r):
        return min(max((r + 1 ^ 1) - 1, 0), nr - 1)

    def later(block):
        return moved(block, sizes, lambda t, r: ((t + 1) % nt, r))

    odd = (r & 1) == 1
    top, bottom = features[:, :2], features[:, -2:]
    to_pair = jnp.where(odd, top, bottom)
    to_cross = jnp.where(odd, bottom, top)
    to_cross, to_pair, sent = lax.optimization_barrier((to_cross, to_pair, features))
    prev = later(sent)
    cross = moved(to_cross, sizes, lambda t, r: (t, crossed(r)))
    pair = moved(to_pair, sizes, lambda t, r: (t, paired(r)))
    own, act_own, gain, res_held, inner_own = call(
        prepare_kernel,
        "prepare",
        [
            vmem_out(features.shape, BF16),
            vmem_out(features.shape, BF16),
            vmem_out((1, ch), F32),
            vmem_out(res_weight.shape, BF16),
            vmem_out((2, rows - 2, cols, ch), F32),
        ],
        [HBM] * 3,
        [pltpu.VMEM((ch,), F32), pltpu.SemaphoreType.DMA((5,))],
        16,
        tuple(in_hbm(a) for a in (features, norm_gain, res_weight)),
    )
    lines = rows - 2
    halo = call(
        halo_kernel,
        "halo",
        vmem_out((2, 2, 2, cols, ch), BF16),
        [SMEM] + [VMEM] * 3,
        [],
        8,
        (flags, cross, pair, gain),
    )
    prev_halo = later(halo)
    act_prev_shape = vmem_out((2, rows, cols, ch), BF16)
    inner, act_prev = call(
        inner_kernel,
        "inner",
        [shape((2, lines, cols, ch), BF16), act_prev_shape],
        [SMEM] + [VMEM] * 4,
        [],
        16,
        (flags, prev, gain, in_vmem(res_held), inner_own),
    )
    inner_prev = later(inner)
    side_rows = [pltpu.VMEM((2, 2, 4, cols, ch), BF16)]
    rim_own = call(
        rim_own_kernel,
        "rim_own",
        vmem_out((2, 2, 2, cols, ch), F32),
        [SMEM] + [VMEM] * 6,
        side_rows,
        16,
        (flags, act_own, halo, own, cross, pair, in_vmem(res_held)),
    )
    rim = call(
        rim_kernel,
        "rim",
        shape((2, 2, 2, cols, ch), BF16),
        [SMEM] + [VMEM] * 4,
        side_rows,
        16,
        (flags, act_prev, prev_halo, rim_own, in_vmem(res_held)),
    )
    rim_prev = later(rim)
    up_turned = jnp.swapaxes(up_weight, 2, 3)
    combined, time_held = call(
        combine_kernel,
        "combine",
        [vmem_out((2, 2 * ch, 4 * co), BF16), vmem_out(time_weight.shape, BF16)],
        [HBM] * 2 + [VMEM],
        [pltpu.VMEM(up_turned.shape, BF16), pltpu.SemaphoreType.DMA((2,))],
        16,
        (in_hbm(up_turned), in_hbm(time_weight), rim),
    )
    stage, inner_rim, rim_part = call(
        up_inner_kernel,
        "up_inner",
        [
            vmem_out((2 * frames, 2 * (lines - 1), 2 * cols, co), BF16),
            vmem_out((2, 2, 2, cols, ch), BF16),
            vmem_out((frames * 4 * cols, 2 * ch), F32),
        ],
        [SMEM] + [VMEM] * 5,
        [
            pltpu.VMEM((4, lines, cols, ch), BF16),
            pltpu.VMEM((2, 2, lines, cols, ch), BF16),
            pltpu.VMEM((2, 2 * frames * (lines - 1) * 2 * cols, 128), F32),
        ],
        24,
        (flags, inner, inner_prev, rim, in_vmem(time_held), in_vmem(combined)),
    )
    return call(
        up_rim_kernel,
        "up_rim",
        shape((2 * frames, 2 * rows, 2 * cols, co), BF16),
        [SMEM] + [VMEM] * 6,
        [
            pltpu.VMEM((2, 2, 2, 3, cols, ch), BF16),
            pltpu.VMEM((2, 2 * frames * 3 * 2 * cols, 128), F32),
            pltpu.VMEM((2, 3, 2 * frames, 1, 2 * cols, co), BF16),
            pltpu.SemaphoreType.DMA((7,)),
        ],
        24,
        (flags, rim_part, rim_prev, inner_rim, stage, in_vmem(time_held), in_vmem(combined)),
        out_specs=HBM,
    )


def solution(mesh):
    placed = (P("tm", "rows", None, None), P(), P(), P(), P())
    return jax.shard_map(
        shards, mesh=mesh, in_specs=placed, out_specs=P("tm", "rows", None, None), check_vma=False
    )
```

time: 31.8 us -> 29.5 us (0.928)
  Pallas kernels: 20.2 us -> 18.4 us
  starting transfers between devices: 8.01 us -> 7.3 us
  waiting for transfers between devices: 2.15 us -> 2.54 us
    pallas_call x7 -> x8, Pallas kernels: 20.2 us -> 18.4 us  [call(): pl.pallas_call(kernel, out_shape=shapes, in_specs=specs, out_specs=out_sp...]
    ppermute x6, starting transfers between devices: 8.01 us -> 7.3 us  [moved(): return lax.ppermute(block, ('tm', 'rows'), pairs)]
    ppermute x6, waiting for transfers between devices: 2.15 us -> 2.54 us  [moved(): return lax.ppermute(block, ('tm', 'rows'), pairs)]
  transfers between devices with their start and end apart: 6 -> 6, of which waited for: 3 -> 4; matrix products, arithmetic and copies ran while one was open for 3% -> 0% of each run, Pallas kernels for 53% -> 53%
where the time goes in v3:
time: 29.5 us; the launch traced here: 29.4 us
  Pallas kernels  18.4 us (62%)
  starting transfers between devices  7.3 us (25%)
  waiting for transfers between devices  2.54 us (9%)
  other arithmetic  1.04 us (4%)
    pallas_call x8, Pallas kernels, call(): pl.pallas_call(kernel, out_shape=shapes, in_specs=specs, out_specs=out_sp...  18.4 us
    ppermute x6, starting transfers between devices, moved(): return lax.ppermute(block, ('tm', 'rows'), pairs)  7.3 us
    ppermute x6, waiting for transfers between devices, moved(): return lax.ppermute(block, ('tm', 'rows'), pairs)  2.54 us
    select_n x1, other arithmetic, shards(): to_pair = jnp.where(odd, top, bottom)  0.96 us
  transfers between devices with their start and end apart: 6, of which 4 were waited for; matrix products, arithmetic and copies ran while one was open for 0% of the time, Pallas kernels for 53%

profile of v3, /device:TPU:192, one launch (start us, length us, event | category | flops | bytes accessed | tf_op | source)
XLA Modules:
  0.0 29.4 jit_solution(13376402527577472455)
XLA Ops:
  0.0 1.0 %broadcast_select_fusion = (bf16[2,2,32,384]{3,2,1,0:T(8,128)(2,1)S(1)}, bf16[2,2,32,384]{3,2,1,0:T(8,128)(2,1)S(1)}) fusion(pred[]{:T(512)} %eq.4, bf16[2,6,32,384]{3,2,1,0:T(8,128)(2,1)} %features.1), kind=kLoop, calls=%fused_computation | loop fusion | flops 98304 | bytes 393217 | tf_op jit(solution)/shard_map/jit(_where)/select_n | solution.py:323
  1.0 5.4 %collective-permute-start.2 = (bf16[2,2,32,384]{3,2,1,0:T(8,128)(2,1)S(1)}, bf16[2,2,32,384]{3,2,1,0:T(8,128)(2,1)S(1)}, u32[]{:S(2)}, u32[]{:S(2)}) collective-permute-start(bf16[2,2,32,384]{3,2,1,0:T(8,128)(2,1)S(1)} %get-tuple-element.26), channel_id=1, source_target_pairs={{0,0},{1,2},{2,1},{3,4},{4,3},{5,6},{6,5},{7,8},{8,7},{9,10},{10,9... | collective-permute-start | bytes 294920 | tf_op jit(solution)/shard_map/ppermute | solution.py:22
  6.3 0.1 collective-permute-start.3
  6.4 0.0 collective-permute-start
  6.5 0.1 add_convert_fusion.flags
  6.6 3.6 %prepare.1 = (bf16[2,6,32,384]{3,2,1,0:T(8,128)(2,1)S(1)}, bf16[2,6,32,384]{3,2,1,0:T(8,128)(2,1)S(1)}, f32[1,384]{1,0:T(1,128)S(1)}, bf16[3,3,3,384,384]{4,3,2,1,0:T(8,128)(2,1)S(1)}, f32[2,4,32,384]{3,2,1,0:T(8,128)S(1)}) custom-call(bf16[2,6,32,384]{3,2,1,0:T(8,128)(2,1)} %features.1, f32[384]{0:T(512)} %gain.1, bf16[3,3,3,384,384]{4,3,2,1,0:T(8,128)(2,1)} %res_weight.1), custom_call_target="tpu_custom_call" | custom-call | flops 1000000000 | bytes 3000000 | tf_op jit(solution)/shard_map/prepare/pallas_call | solution.py:279
  10.1 0.0 collective-permute-done.2.cross
  10.1 0.9 %collective-permute-done.3.pair = bf16[2,2,32,384]{3,2,1,0:T(8,128)(2,1)S(1)} collective-permute-done((bf16[2,2,32,384]{3,2,1,0:T(8,128)(2,1)S(1)}, bf16[2,2,32,384]{3,2,1,0:T(8,128)(2,1)S(1)}, u32[]{:S(2)}, u32[]{:S(2)}) %collective-permute-start.3) | collective-permute-done | bytes 98336 | tf_op jit(solution)/shard_map/ppermute | solution.py:22
  11.0 0.8 %halo.1 = bf16[2,2,2,32,384]{4,3,2,1,0:T(8,128)(2,1)S(1)} custom-call(s32[4]{0:T(128)S(1)} %add_convert_fusion.flags, bf16[2,2,32,384]{3,2,1,0:T(8,128)(2,1)S(1)} %collective-permute-done.2.cross, bf16[2,2,32,384]{3,2,1,0:T(8,128)(2,1)S(1)} %collective-permute-done.3.pair, f32[1,384]{1,0:T(1,128)S(1)} %get-tuple-element.21.gain), custom_call_target="tpu_custom_call" | custom-call | flops 1000000000 | bytes 3000000 | tf_op jit(solution)/shard_map/halo/pallas_call | solution.py:279
  11.8 0.7 %collective-permute-start.4 = (bf16[2,2,2,32,384]{4,3,2,1,0:T(8,128)(2,1)S(1)}, bf16[2,2,2,32,384]{4,3,2,1,0:T(8,128)(2,1)S(1)}, u32[]{:S(2)}, u32[]{:S(2)}) collective-permute-start(bf16[2,2,2,32,384]{4,3,2,1,0:T(8,128)(2,1)S(1)} %halo.1), channel_id=1, source_target_pairs={{0,32},{1,33},{2,34},{3,35},{4,36},{5,37},{6,38},{7,39},{8,40},{9,... | collective-permute-start | bytes 589832 | tf_op jit(solution)/shard_map/ppermute | solution.py:22
  12.5 2.0 %rim_own.1.partial = f32[2,2,2,32,384]{4,3,2,1,0:T(8,128)S(1)} custom-call(s32[4]{0:T(128)S(1)} %add_convert_fusion.flags, bf16[2,6,32,384]{3,2,1,0:T(8,128)(2,1)S(1)} %get-tuple-element.28.act_own, bf16[2,2,2,32,384]{4,3,2,1,0:T(8,128)(2,1)S(1)} %halo.1, bf16[2,6,32,384]{3,2,1,0:T(8,128)(2,1)S(1)} %get-tuple-element.29.own, ...), custom_call_target="tpu_custom_call" | custom-call | flops 1000000000 | bytes 3000000 | tf_op jit(solution)/shard_map/rim_own/pallas_call | solution.py:279
  14.5 0.0 collective-permute-done.prev
  14.5 2.2 %inner.1 = (bf16[2,4,32,384]{3,2,1,0:T(8,128)(2,1)S(1)}, bf16[2,6,32,384]{3,2,1,0:T(8,128)(2,1)S(1)}) custom-call(s32[4]{0:T(128)S(1)} %add_convert_fusion.flags, bf16[2,6,32,384]{3,2,1,0:T(8,128)(2,1)S(1)} %collective-permute-done.prev, f32[1,384]{1,0:T(1,128)S(1)} %get-tuple-element.21.gain, bf16[3,3,3,384,384]{4,3,2,1,0:T(8,128)(2,1)S(1)} %get-tuple-element.22.res_held, ...), custom_call_target="tpu_custom_call" | custom-call | flops 1000000000 | bytes 3000000 | tf_op jit(solution)/shard_map/inner/pallas_call | solution.py:279
  16.7 0.9 %collective-permute-start.1 = (bf16[2,4,32,384]{3,2,1,0:T(8,128)(2,1)S(1)}, bf16[2,4,32,384]{3,2,1,0:T(8,128)(2,1)S(1)}, u32[]{:S(2)}, u32[]{:S(2)}) collective-permute-start(bf16[2,4,32,384]{3,2,1,0:T(8,128)(2,1)S(1)} %get-tuple-element.24.own), channel_id=1, source_target_pairs={{0,32},{1,33},{2,34},{3,35},{4,36},{5,37},{6,38},{7,39},{8,40},{9,... | collective-permute-start | bytes 589832 | tf_op jit(solution)/shard_map/ppermute | solution.py:22
  17.6 0.5 %collective-permute-done.4.halo = bf16[2,2,2,32,384]{4,3,2,1,0:T(8,128)(2,1)S(1)} collective-permute-done((bf16[2,2,2,32,384]{4,3,2,1,0:T(8,128)(2,1)S(1)}, bf16[2,2,2,32,384]{4,3,2,1,0:T(8,128)(2,1)S(1)}, u32[]{:S(2)}, u32[]{:S(2)}) %collective-permute-start.4) | collective-permute-done | bytes 196640 | tf_op jit(solution)/shard_map/ppermute | solution.py:22
  18.1 2.0 %rim.1.after.rim_own = bf16[2,2,2,32,384]{4,3,2,1,0:T(8,128)(2,1)S(1)} custom-call(s32[4]{0:T(128)S(1)} %add_convert_fusion.flags, bf16[2,6,32,384]{3,2,1,0:T(8,128)(2,1)S(1)} %get-tuple-element.25.act_prev, bf16[2,2,2,32,384]{4,3,2,1,0:T(8,128)(2,1)S(1)} %collective-permute-done.4.halo, f32[2,2,2,32,384]{4,3,2,1,0:T(8,128)S(1)} %rim_own.1.partial, ...), custom_call_target="tpu_custom_call" | custom-call | flops 1000000000 | bytes 3000000 | tf_op jit(solution)/shard_map/rim/pallas_call | solution.py:279
  20.1 0.2 collective-permute-start.5
  20.3 2.1 %combine.1 = (bf16[2,768,768]{2,1,0:T(8,128)(2,1)S(1)}, bf16[3,384,768]{2,1,0:T(8,128)(2,1)S(1)}) custom-call(bf16[3,3,192,384]{3,2,1,0:T(8,128)(2,1)} %bitcast.5, bf16[3,384,768]{2,1,0:T(8,128)(2,1)} %time_weight.1, bf16[2,2,2,32,384]{4,3,2,1,0:T(8,128)(2,1)S(1)} %rim.1.after.rim_own), custom_call_target="tpu_custom_call" | custom-call | flops 1000000000 | bytes 3000000 | tf_op jit(solution)/shard_map/combine/pallas_call | solution.py:279
  22.4 0.6 %collective-permute-done.1.prev = bf16[2,4,32,384]{3,2,1,0:T(8,128)(2,1)S(1)} collective-permute-done((bf16[2,4,32,384]{3,2,1,0:T(8,128)(2,1)S(1)}, bf16[2,4,32,384]{3,2,1,0:T(8,128)(2,1)S(1)}, u32[]{:S(2)}, u32[]{:S(2)}) %collective-permute-start.1) | collective-permute-done | bytes 196640 | tf_op jit(solution)/shard_map/ppermute | solution.py:22
  23.0 2.9 %up_inner.1 = (bf16[4,6,64,192]{3,2,1,0:T(8,128)(2,1)S(1)}, bf16[2,2,2,32,384]{4,3,2,1,0:T(8,128)(2,1)S(1)}, f32[256,768]{1,0:T(8,128)S(1)}) custom-call(s32[4]{0:T(128)S(1)} %add_convert_fusion.flags, bf16[2,4,32,384]{3,2,1,0:T(8,128)(2,1)S(1)} %get-tuple-element.24.own, bf16[2,4,32,384]{3,2,1,0:T(8,128)(2,1)S(1)} %collective-permute-done.1.prev, ...), custom_call_target="tpu_custom_call" | custom-call | flops 1000000000 | bytes 3000000 | tf_op jit(solution)/shard_map/up_inner/pallas_call | solution.py:279
  25.9 0.5 %collective-permute-done.5.prev = bf16[2,2,2,32,384]{4,3,2,1,0:T(8,128)(2,1)S(1)} collective-permute-done((bf16[2,2,2,32,384]{4,3,2,1,0:T(8,128)(2,1)S(1)}, bf16[2,2,2,32,384]{4,3,2,1,0:T(8,128)(2,1)S(1)}, u32[]{:S(2)}, u32[]{:S(2)}) %collective-permute-start.5) | collective-permute-done | bytes 196640 | tf_op jit(solution)/shard_map/ppermute | solution.py:22
  26.4 2.9 %up_rim.1 = bf16[4,12,64,192]{3,2,1,0:T(8,128)(2,1)} custom-call(s32[4]{0:T(128)S(1)} %add_convert_fusion.flags, f32[256,768]{1,0:T(8,128)S(1)} %get-tuple-element.32.part, bf16[2,2,2,32,384]{4,3,2,1,0:T(8,128)(2,1)S(1)} %collective-permute-done.5.prev, bf16[2,2,2,32,384]{4,3,2,1,0:T(8,128)(2,1)S(1)} %get-tuple-element.33.inner_rim, ...), custom_call_target="tpu_custom_call" | custom-call | flops 1000000000 | bytes 3000000 | tf_op jit(solution)/shard_map/up_rim/pallas_call | solution.py:279
Async XLA Ops:
  1.0 9.2 %collective-permute-start.2 = (bf16[2,2,32,384]{3,2,1,0:T(8,128)(2,1)S(1)}, bf16[2,2,32,384]{3,2,1,0:T(8,128)(2,1)S(1)}, u32[]{:S(2)}, u32[]{:S(2)}) collective-permute-start(bf16[2,2,32,384]{3,2,1,0:T(8,128)(2,1)S(1)} %get-tuple-element.26), channel_id=1, source_target_pairs={{0,0},{1,2},{2,1},{3,4},{4,3},{5,6},{6,5},{7,8},{8,7},{9,10},{10,9... | collective-permute-start | bytes 294920 | tf_op jit(solution)/shard_map/ppermute | solution.py:22
  6.3 4.7 %collective-permute-start.3 = (bf16[2,2,32,384]{3,2,1,0:T(8,128)(2,1)S(1)}, bf16[2,2,32,384]{3,2,1,0:T(8,128)(2,1)S(1)}, u32[]{:S(2)}, u32[]{:S(2)}) collective-permute-start(bf16[2,2,32,384]{3,2,1,0:T(8,128)(2,1)S(1)} %get-tuple-element.27), channel_id=1, source_target_pairs={{0,1},{1,0},{2,3},{3,2},{4,5},{5,4},{6,7},{7,6},{8,9},{9,8},{10,11... | collective-permute-start | bytes 294920 | tf_op jit(solution)/shard_map/ppermute | solution.py:22
  6.4 8.1 %collective-permute-start = (bf16[2,6,32,384]{3,2,1,0:T(8,128)(2,1)}, bf16[2,6,32,384]{3,2,1,0:T(8,128)(2,1)S(1)}, u32[]{:S(2)}, u32[]{:S(2)}) collective-permute-start(bf16[2,6,32,384]{3,2,1,0:T(8,128)(2,1)} %features.1), channel_id=1, source_target_pairs={{0,32},{1,33},{2,34},{3,35},{4,36},{5,37},{6,38},{7,39},{8,40},{9,... | collective-permute-start | bytes 884744 | tf_op jit(solution)/shard_map/ppermute | solution.py:22
  11.8 6.3 %collective-permute-start.4 = (bf16[2,2,2,32,384]{4,3,2,1,0:T(8,128)(2,1)S(1)}, bf16[2,2,2,32,384]{4,3,2,1,0:T(8,128)(2,1)S(1)}, u32[]{:S(2)}, u32[]{:S(2)}) collective-permute-start(bf16[2,2,2,32,384]{4,3,2,1,0:T(8,128)(2,1)S(1)} %halo.1), channel_id=1, source_target_pairs={{0,32},{1,33},{2,34},{3,35},{4,36},{5,37},{6,38},{7,39},{8,40},{9,... | collective-permute-start | bytes 589832 | tf_op jit(solution)/shard_map/ppermute | solution.py:22
  16.7 6.3 %collective-permute-start.1 = (bf16[2,4,32,384]{3,2,1,0:T(8,128)(2,1)S(1)}, bf16[2,4,32,384]{3,2,1,0:T(8,128)(2,1)S(1)}, u32[]{:S(2)}, u32[]{:S(2)}) collective-permute-start(bf16[2,4,32,384]{3,2,1,0:T(8,128)(2,1)S(1)} %get-tuple-element.24.own), channel_id=1, source_target_pairs={{0,32},{1,33},{2,34},{3,35},{4,36},{5,37},{6,38},{7,39},{8,40},{9,... | collective-permute-start | bytes 589832 | tf_op jit(solution)/shard_map/ppermute | solution.py:22
  20.1 6.3 %collective-permute-start.5 = (bf16[2,2,2,32,384]{4,3,2,1,0:T(8,128)(2,1)S(1)}, bf16[2,2,2,32,384]{4,3,2,1,0:T(8,128)(2,1)S(1)}, u32[]{:S(2)}, u32[]{:S(2)}) collective-permute-start(bf16[2,2,2,32,384]{4,3,2,1,0:T(8,128)(2,1)S(1)} %rim.1.after.rim_own), channel_id=1, source_target_pairs={{0,32},{1,33},{2,34},{3,35},{4,36},{5,37},{6,38},{7,39},{8,40},{9,... | collective-permute-start | bytes 589832 | tf_op jit(solution)/shard_map/ppermute | solution.py:22

commit v4 on v3

--- a/solution.py
+++ b/solution.py
@@ -1,3 +1,5 @@
+import functools
+
 import jax
 import jax.numpy as jnp
 from jax import lax
@@ -36,15 +38,20 @@
     ]
 
 
+def parity_kernel(flags, out):
+    out[...] = jnp.zeros(out.shape, F32) + flags[3].astype(F32)
+
+
 def prepare_kernel(
-    features, gain, res_weight, own, act, gain_out, res_held, partial, gain_in, sems
+    features, gain, up_weight, time_weight, res_held,
+    own, act, gain_out, partial, up_out, time_out,
+    gain_in, sems,
 ):
     rows, cols, ch = own.shape[1:]
     copies = [
         pltpu.make_async_copy(source, target, sems.at[i])
         for i, (source, target) in enumerate(
-            ((gain, gain_in), (features, own))
-            + tuple((res_weight.at[kt], res_held.at[kt]) for kt in (2, 1, 0))
+            ((gain, gain_in), (features, own), (up_weight, up_out), (time_weight, time_out))
         )
     ]
     for copy in copies:
@@ -54,28 +61,19 @@
     g = gain_in[...].reshape(1, ch)
     gain_out[...] = g
     act[...] = activated(own[...].astype(F32), g.reshape(1, 1, 1, ch)).astype(BF16)
-    copies[2].wait()
     both = taps(inner_windows(act, 0, 2, cols, ch), res_held.at[2])
-    copies[3].wait()
     late = taps(inner_windows(act, 0, 1, cols, ch), res_held.at[1])
     half = late.shape[0]
     acc = jnp.concatenate([both[:half], both[half:] + late], axis=0)
     branch = columns_summed(acc, cols, ch).reshape(2, rows - 2, cols, ch)
     partial[...] = own[:, 1 : rows - 1].astype(F32) + branch
-    copies[4].wait()
-
-
-def combine_kernel(up_weight, time_weight, after, combined, time_out, up_in, sems):
-    del after
-    ch = time_out.shape[1]
-    copies = [
-        pltpu.make_async_copy(source, target, sems.at[i])
-        for i, (source, target) in enumerate(((up_weight, up_in), (time_weight, time_out)))
-    ]
-    for copy in copies:
-        copy.start()
-    copies[0].wait()
-    w = [[up_in[kh, kw].astype(F32) for kw in range(3)] for kh in range(3)]
+    copies[2].wait()
+    copies[3].wait()
+
+
+def combine(up_weight, combined):
+    ch = up_weight.shape[-1]
+    w = [[up_weight[kh, kw].astype(F32) for kw in range(3)] for kh in range(3)]
     for phase in range(2):
         for tap in range(2):
             if phase == 0:
@@ -84,7 +82,6 @@
                 r = [w[0][k] + w[1][k] for k in range(3)] if tap == 0 else w[2]
             block = jnp.concatenate([r[0], r[0] + r[1], r[1] + r[2], r[2]], axis=0)
             combined[phase, tap * ch : (tap + 1) * ch] = block.T.astype(BF16)
-    copies[1].wait()
 
 
 def columns_summed(acc, cols, ch):
@@ -149,7 +146,7 @@
     out[:, 1, 1] = below + branch[:, 1, 1]
 
 
-def rim_kernel(flags, act_prev, halo, partial, res_held, out, act):
+def rim_value(flags, act_prev, halo, partial, res_held, out, act):
     rows = act_prev.shape[1]
     cols, ch = partial.shape[3:]
     keep = flags[0].astype(BF16)
@@ -168,6 +165,28 @@
     out[:, 1, 1] = (blended[:, 1, 1] * flags[2].astype(F32)).astype(BF16)
 
 
+def rim_first_kernel(flags, act_prev, halo, partial, res_held, up_weight, out, combined, act):
+    @pl.when(flags[4] == 1)
+    def _():
+        rim_value(flags, act_prev, halo, partial, res_held, out, act)
+
+    @pl.when(flags[4] == 0)
+    def _():
+        out[...] = jnp.zeros(out.shape, BF16)
+        combine(up_weight, combined)
+
+
+def rim_second_kernel(flags, act_prev, halo, partial, res_held, up_weight, out, combined, act):
+    @pl.when(flags[4] == 0)
+    def _():
+        rim_value(flags, act_prev, halo, partial, res_held, out, act)
+
+    @pl.when(flags[4] == 1)
+    def _():
+        out[...] = jnp.zeros(out.shape, BF16)
+        combine(up_weight, combined)
+
+
 def time_products(windows, weight, first):
     ch = weight.shape[1]
     count = len(windows)
@@ -197,7 +216,21 @@
     return line
 
 
-def up_inner_kernel(flags, own, prev, rim_own, time_weight, weight, stage, inner_rim, rim_part, stack, up, woven):
+def by_core(kernel, flags, *refs):
+    second, first, *rest = refs
+
+    @pl.when(flags[4] == 0)
+    def _():
+        kernel(flags, first, *rest)
+
+    @pl.when(flags[4] == 1)
+    def _():
+        kernel(flags, second, *rest)
+
+
+def up_inner_kernel(
+    flags, weight, own, prev, rim_first, rim_second, time_weight, stage, inner_rim, rim_part, stack, up, woven
+):
     frames, lines, cols, ch = own.shape
     co = stage.shape[-1]
     stack[2:4] = own[...]
@@ -219,23 +252,25 @@
         for f in range(2 * frames):
             for j in range(pairs):
                 stage[f, 2 * j + 1 - phase] = line(f * pairs + j)
-    half = rim_own.shape[1] * rim_own.shape[2] * cols
+    half = rim_first.shape[1] * rim_first.shape[2] * cols
+    rim_own = jnp.where(flags[4] == 1, rim_first[...], rim_second[...])
     first = rim_own[0].reshape(half, ch)
     rim_part[0:half] = time_products([first], time_weight, 2)
     rim_part[half:] = time_products([first, rim_own[1].reshape(half, ch)], time_weight, 1)
 
 
 def up_rim_kernel(
-    flags, part, prev, inner_rim, inner_stage, time_weight, weight, out, up, woven, stage, sems
+    flags, weight, part, second, first, inner_rim, inner_stage, time_weight, out, up, woven, stage, sems
 ):
-    frames, sides, lines, cols, ch = prev.shape
+    frames, sides, lines, cols, ch = first.shape
     co = out.shape[-1]
     middle = pltpu.make_async_copy(inner_stage, out.at[:, 3 : 3 + inner_stage.shape[1]], sems.at[6])
     middle.start()
     keep = flags[0].astype(BF16)
     half = sides * lines * cols
-    before = prev[0].reshape(half, ch) * keep
-    last = prev[1].reshape(half, ch) * keep
+    prev = jnp.where(flags[4] == 1, second[...], first[...]) * keep
+    before = prev[0].reshape(half, ch)
+    last = prev[1].reshape(half, ch)
     products = (
         part[0:half] + time_products([before, last], time_weight, 0),
         part[half:] + time_products([last], time_weight, 0),
@@ -274,7 +309,7 @@
         copy.wait()
 
 
-def call(kernel, name, shapes, specs, scratch, mib, args, out_specs=None, us=1):
+def call(kernel, name, shapes, specs, scratch, mib, args, out_specs=None, in_out=None, us=1):
     several = isinstance(shapes, list)
     return pl.pallas_call(
         kernel,
@@ -284,6 +319,7 @@
         scratch_shapes=scratch,
         compiler_params=pltpu.CompilerParams(vmem_limit_bytes=mib * 2**20),
         cost_estimate=pl.CostEstimate(flops=us * 10**9, bytes_accessed=us * 3 * 10**9 // 1000, transcendentals=0),
+        input_output_aliases=in_out or {},
         name=name,
     )(*args)
 
@@ -305,7 +341,7 @@
     nt, nr = lax.axis_size("tm"), lax.axis_size("rows")
     co = up_weight.shape[-1]
     t, r = lax.axis_index("tm"), lax.axis_index("rows")
-    flags = jnp.stack([t > 0, r > 0, r < nr - 1, (r & 1) == 1]).astype(jnp.int32)
+    flags = jnp.stack([t > 0, r > 0, r < nr - 1, (r & 1) == 1, (t & 1) == 1]).astype(jnp.int32)
     sizes = (nt, nr)
     shape = jax.ShapeDtypeStruct
 
@@ -318,7 +354,8 @@
     def later(block):
         return moved(block, sizes, lambda t, r: ((t + 1) % nt, r))
 
-    odd = (r & 1) == 1
+    parity = call(parity_kernel, "parity", vmem_out((1, ch), F32), [SMEM], [], 1, (flags,), us=5)
+    odd = parity.reshape(1, 1, 1, ch) > 0.5
     top, bottom = features[:, :2], features[:, -2:]
     to_pair = jnp.where(odd, top, bottom)
     to_cross = jnp.where(odd, bottom, top)
@@ -326,20 +363,24 @@
     prev = later(sent)
     cross = moved(to_cross, sizes, lambda t, r: (t, crossed(r)))
     pair = moved(to_pair, sizes, lambda t, r: (t, paired(r)))
-    own, act_own, gain, res_held, inner_own = call(
+    res_held = in_vmem(res_weight)
+    up_turned = jnp.swapaxes(up_weight, 2, 3)
+    own, act_own, gain, inner_own, up_held, time_held = call(
         prepare_kernel,
         "prepare",
         [
             vmem_out(features.shape, BF16),
             vmem_out(features.shape, BF16),
             vmem_out((1, ch), F32),
-            vmem_out(res_weight.shape, BF16),
             vmem_out((2, rows - 2, cols, ch), F32),
+            vmem_out(up_turned.shape, BF16),
+            vmem_out(time_weight.shape, BF16),
         ],
-        [HBM] * 3,
-        [pltpu.VMEM((ch,), F32), pltpu.SemaphoreType.DMA((5,))],
+        [HBM] * 4 + [VMEM],
+        [pltpu.VMEM((ch,), F32), pltpu.SemaphoreType.DMA((4,))],
         16,
-        tuple(in_hbm(a) for a in (features, norm_gain, res_weight)),
+        (in_hbm(features), in_hbm(norm_gain), in_hbm(up_turned), in_hbm(time_weight), res_held),
+        us=3,
     )
     lines = rows - 2
     halo = call(
@@ -360,7 +401,7 @@
         [SMEM] + [VMEM] * 4,
         [],
         16,
-        (flags, prev, gain, in_vmem(res_held), inner_own),
+        (flags, prev, gain, res_held, inner_own),
     )
     inner_prev = later(inner)
     side_rows = [pltpu.VMEM((2, 2, 4, cols, ch), BF16)]
@@ -371,50 +412,52 @@
         [SMEM] + [VMEM] * 6,
         side_rows,
         16,
-        (flags, act_own, halo, own, cross, pair, in_vmem(res_held)),
-    )
-    rim = call(
-        rim_kernel,
-        "rim",
-        shape((2, 2, 2, cols, ch), BF16),
-        [SMEM] + [VMEM] * 4,
+        (flags, act_own, halo, own, cross, pair, res_held),
+    )
+    rim_shape = vmem_out((2, 2, 2, cols, ch), BF16)
+    sums_shape = vmem_out((2, 2 * ch, 4 * co), BF16)
+    first, first_sums = call(
+        rim_first_kernel,
+        "rim_first",
+        [rim_shape, sums_shape],
+        [SMEM] + [VMEM] * 5,
         side_rows,
-        16,
-        (flags, act_prev, prev_halo, rim_own, in_vmem(res_held)),
-    )
-    rim_prev = later(rim)
-    up_turned = jnp.swapaxes(up_weight, 2, 3)
-    combined, time_held = call(
-        combine_kernel,
-        "combine",
-        [vmem_out((2, 2 * ch, 4 * co), BF16), vmem_out(time_weight.shape, BF16)],
-        [HBM] * 2 + [VMEM],
-        [pltpu.VMEM(up_turned.shape, BF16), pltpu.SemaphoreType.DMA((2,))],
-        16,
-        (in_hbm(up_turned), in_hbm(time_weight), rim),
-    )
+        24,
+        (flags, act_prev, prev_halo, rim_own, res_held, in_vmem(up_held)),
+    )
+    first_prev = later(first)
+    rim, second_sums = call(
+        rim_second_kernel,
+        "rim_second",
+        [rim_shape, sums_shape],
+        [SMEM] + [VMEM] * 5,
+        side_rows,
+        24,
+        (flags, act_prev, prev_halo, rim_own, res_held, in_vmem(up_held)),
+    )
+    second_prev = moved(rim, sizes, lambda t, r: (t ^ 1, r))
     stage, inner_rim, rim_part = call(
-        up_inner_kernel,
+        functools.partial(by_core, up_inner_kernel),
         "up_inner",
         [
             vmem_out((2 * frames, 2 * (lines - 1), 2 * cols, co), BF16),
             vmem_out((2, 2, 2, cols, ch), BF16),
             vmem_out((frames * 4 * cols, 2 * ch), F32),
         ],
-        [SMEM] + [VMEM] * 5,
+        [SMEM] + [VMEM] * 7,
         [
             pltpu.VMEM((4, lines, cols, ch), BF16),
             pltpu.VMEM((2, 2, lines, cols, ch), BF16),
             pltpu.VMEM((2, 2 * frames * (lines - 1) * 2 * cols, 128), F32),
         ],
         24,
-        (flags, inner, inner_prev, rim, in_vmem(time_held), in_vmem(combined)),
+        (flags, second_sums, first_sums, inner, inner_prev, first, rim, in_vmem(time_held)),
     )
     return call(
-        up_rim_kernel,
+        functools.partial(by_core, up_rim_kernel),
         "up_rim",
         shape((2 * frames, 2 * rows, 2 * cols, co), BF16),
-        [SMEM] + [VMEM] * 6,
+        [SMEM] + [VMEM] * 8,
         [
             pltpu.VMEM((2, 2, 2, 3, cols, ch), BF16),
             pltpu.VMEM((2, 2 * frames * 3 * 2 * cols, 128), F32),
@@ -422,7 +465,7 @@
             pltpu.SemaphoreType.DMA((7,)),
         ],
         24,
-        (flags, rim_part, rim_prev, inner_rim, stage, in_vmem(time_held), in_vmem(combined)),
+        (flags, second_sums, first_sums, rim_part, second_prev, first_prev, inner_rim, stage, in_vmem(time_held)),
         out_specs=HBM,
     )
 

time: 29.5 us -> 29.6 us (level)
  Pallas kernels: 18.4 us -> 17.4 us
  other arithmetic: 1.04 us -> 0.05 us
  starting transfers between devices: 7.3 us -> 7.91 us
  waiting for transfers between devices: 2.54 us -> 3.13 us
  local copies, waits for them, and re-layouts: 0 us -> 0.49 us
    select_n x1, other arithmetic: 0.96 us -> 0.03 us  [shards(): to_pair = jnp.where(odd, top, bottom)]
    pallas_call x8 -> x9, Pallas kernels: 18.4 us -> 17.4 us  [call(): pl.pallas_call(kernel, out_shape=shapes, in_specs=specs, out_specs=out_sp...]
    ppermute x6 -> x7, starting transfers between devices: 7.3 us -> 7.91 us  [moved(): return lax.ppermute(block, ('tm', 'rows'), pairs)]
    ppermute x6 -> x7, waiting for transfers between devices: 2.54 us -> 3.13 us  [moved(): return lax.ppermute(block, ('tm', 'rows'), pairs)]
    unnamed x0 -> x4, local copies, waits for them, and re-layouts: none -> 0.38 us
  transfers between devices with their start and end apart: 6 -> 7, of which waited for: 4 -> 5; matrix products, arithmetic and copies ran while one was open for 0% -> 0% of each run, Pallas kernels for 53% -> 48%
where the time goes in v4:
time: 29.6 us; the launch traced here: 29.3 us
  Pallas kernels  17.4 us (59%)
  starting transfers between devices  7.91 us (27%)
  waiting for transfers between devices  3.13 us (11%)
  local copies, waits for them, and re-layouts  0.49 us (2%)
    pallas_call x9, Pallas kernels, call(): pl.pallas_call(kernel, out_shape=shapes, in_specs=specs, out_specs=out_sp...  17.4 us
    ppermute x7, starting transfers between devices, moved(): return lax.ppermute(block, ('tm', 'rows'), pairs)  7.91 us
    ppermute x7, waiting for transfers between devices, moved(): return lax.ppermute(block, ('tm', 'rows'), pairs)  3.13 us
  transfers between devices with their start and end apart: 7, of which 5 were waited for; matrix products, arithmetic and copies ran while one was open for 0% of the time, Pallas kernels for 48%

profile of v4, /device:TPU:192, one launch (start us, length us, event | category | flops | bytes accessed | tf_op | source)
XLA Modules:
  0.0 29.3 jit_solution(7606027942095623352)
XLA Ops:
  0.0 0.1 stack.23
  0.1 0.0 copy-start.1
  0.1 0.0 copy-start
  0.1 0.5 %parity.1 = f32[1,384]{1,0:T(1,128)S(1)} custom-call(s32[5]{0:T(128)S(1)} %convert_element_type.3.flags), custom_call_target="tpu_custom_call" | custom-call | flops 5000000000 | bytes 15000000 | tf_op jit(solution)/shard_map/parity/pallas_call | solution.py:314
  0.7 0.4 %copy-done.1 = bf16[2,6,32,384]{3,2,1,0:T(8,128)(2,1)S(1)} copy-done((bf16[2,6,32,384]{3,2,1,0:T(8,128)(2,1)S(1)}, bf16[2,6,32,384]{3,2,1,0:T(8,128)(2,1)}, u32[]{:S(2)}) %copy-start.1) | copy-done | bytes 294936
  1.1 5.6 %collective-permute-start.1 = (bf16[2,2,32,384]{3,2,1,0:T(8,128)(2,1)S(1)}, bf16[2,2,32,384]{3,2,1,0:T(8,128)(2,1)S(1)}, u32[]{:S(2)}, u32[]{:S(2)}) collective-permute-start(bf16[2,2,32,384]{3,2,1,0:T(8,128)(2,1)S(1)} %get-tuple-element.27), channel_id=1, source_target_pairs={{0,0},{1,2},{2,1},{3,4},{4,3},{5,6},{6,5},{7,8},{8,7},{9,10},{10,9... | collective-permute-start | bytes 294920 | tf_op jit(solution)/shard_map/ppermute | solution.py:24
  6.7 0.1 collective-permute-start.2
  6.8 0.0 collective-permute-start
  6.9 0.0 copy-done
  6.9 2.6 %prepare.1 = (bf16[2,6,32,384]{3,2,1,0:T(8,128)(2,1)S(1)}, bf16[2,6,32,384]{3,2,1,0:T(8,128)(2,1)S(1)}, f32[1,384]{1,0:T(1,128)S(1)}, f32[2,4,32,384]{3,2,1,0:T(...) custom-call(bf16[2,6,32,384]{3,2,1,0:T(8,128)(2,1)} %features.1, f32[384]{0:T(512)} %gain.1, ...), custom_call_target="tpu_custom_call" | custom-call | flops 3000000000 | bytes 9000000 | tf_op jit(solution)/shard_map/prepare/pallas_call | solution.py:314
  9.5 0.5 %collective-permute-done.1.cross = bf16[2,2,32,384]{3,2,1,0:T(8,128)(2,1)S(1)} collective-permute-done((bf16[2,2,32,384]{3,2,1,0:T(8,128)(2,1)S(1)}, bf16[2,2,32,384]{3,2,1,0:T(8,128)(2,1)S(1)}, u32[]{:S(2)}, u32[]{:S(2)}) %collective-permute-start.1) | collective-permute-done | bytes 98336 | tf_op jit(solution)/shard_map/ppermute | solution.py:24
  10.0 1.5 %collective-permute-done.2.pair = bf16[2,2,32,384]{3,2,1,0:T(8,128)(2,1)S(1)} collective-permute-done((bf16[2,2,32,384]{3,2,1,0:T(8,128)(2,1)S(1)}, bf16[2,2,32,384]{3,2,1,0:T(8,128)(2,1)S(1)}, u32[]{:S(2)}, u32[]{:S(2)}) %collective-permute-start.2) | collective-permute-done | bytes 98336 | tf_op jit(solution)/shard_map/ppermute | solution.py:24
  11.4 0.8 %halo.1 = bf16[2,2,2,32,384]{4,3,2,1,0:T(8,128)(2,1)S(1)} custom-call(s32[5]{0:T(128)S(1)} %convert_element_type.3.flags, bf16[2,2,32,384]{3,2,1,0:T(8,128)(2,1)S(1)} %collective-permute-done.1.cross, bf16[2,2,32,384]{3,2,1,0:T(8,128)(2,1)S(1)} %collective-permute-done.2.pair, f32[1,384]{1,0:T(1,128)S(1)} %get-tuple-element.24.gain), custom_call_target="tpu_custom_call" | custom-call | flops 1000000000 | bytes 3000000 | tf_op jit(solution)/shard_map/halo/pallas_call | solution.py:314
  12.2 0.0 collective-permute-start.3
  12.2 2.0 %rim_own.1.partial = f32[2,2,2,32,384]{4,3,2,1,0:T(8,128)S(1)} custom-call(s32[5]{0:T(128)S(1)} %convert_element_type.3.flags, bf16[2,6,32,384]{3,2,1,0:T(8,128)(2,1)S(1)} %get-tuple-element.29.act_own, bf16[2,2,2,32,384]{4,3,2,1,0:T(8,128)(2,1)S(1)} %halo.1, bf16[2,6,32,384]{3,2,1,0:T(8,128)(2,1)S(1)} %get-tuple-element.30.own, ...), custom_call_target="tpu_custom_call" | custom-call | flops 1000000000 | bytes 3000000 | tf_op jit(solution)/shard_map/rim_own/pallas_call | solution.py:314
  14.2 0.0 collective-permute-done.prev
  14.3 2.2 %inner.1 = (bf16[2,4,32,384]{3,2,1,0:T(8,128)(2,1)S(1)}, bf16[2,6,32,384]{3,2,1,0:T(8,128)(2,1)S(1)}) custom-call(s32[5]{0:T(128)S(1)} %convert_element_type.3.flags, bf16[2,6,32,384]{3,2,1,0:T(8,128)(2,1)S(1)} %collective-permute-done.prev, f32[1,384]{1,0:T(1,128)S(1)} %get-tuple-element.24.gain, bf16[3,3,3,384,384]{4,3,2,1,0:T(8,128)(2,1)S(1)} %copy-done, ...), custom_call_target="tpu_custom_call" | custom-call | flops 1000000000 | bytes 3000000 | tf_op jit(solution)/shard_map/inner/pallas_call | solution.py:314
  16.4 1.6 %collective-permute-start.4 = (bf16[2,4,32,384]{3,2,1,0:T(8,128)(2,1)S(1)}, bf16[2,4,32,384]{3,2,1,0:T(8,128)(2,1)S(1)}, u32[]{:S(2)}, u32[]{:S(2)}) collective-permute-start(bf16[2,4,32,384]{3,2,1,0:T(8,128)(2,1)S(1)} %get-tuple-element.34.refs_2_), channel_id=1, source_target_pairs={{0,32},{1,33},{2,34},{3,35},{4,36},{5,37},{6,38},{7,39},{8,40},{9,... | collective-permute-start | bytes 589832 | tf_op jit(solution)/shard_map/ppermute | solution.py:24
  18.0 0.5 %collective-permute-done.3.halo = bf16[2,2,2,32,384]{4,3,2,1,0:T(8,128)(2,1)S(1)} collective-permute-done((bf16[2,2,2,32,384]{4,3,2,1,0:T(8,128)(2,1)S(1)}, bf16[2,2,2,32,384]{4,3,2,1,0:T(8,128)(2,1)S(1)}, u32[]{:S(2)}, u32[]{:S(2)}) %collective-permute-start.3) | collective-permute-done | bytes 196640 | tf_op jit(solution)/shard_map/ppermute | solution.py:24
  18.5 1.4 %rim_first.1 = (bf16[2,2,2,32,384]{4,3,2,1,0:T(8,128)(2,1)S(1)}, bf16[2,768,768]{2,1,0:T(8,128)(2,1)S(1)}) custom-call(s32[5]{0:T(128)S(1)} %convert_element_type.3.flags, bf16[2,6,32,384]{3,2,1,0:T(8,128)(2,1)S(1)} %get-tuple-element.26.act_prev, bf16[2,2,2,32,384]{4,3,2,1,0:T(8,128)(2,1)S(1)} %collective-permute-done.3.halo, ...), custom_call_target="tpu_custom_call" | custom-call | flops 1000000000 | bytes 3000000 | tf_op jit(solution)/shard_map/rim_first/pallas_call | solution.py:314
  19.9 0.2 collective-permute-start.6
  20.1 2.0 %rim_second.1 = (bf16[2,2,2,32,384]{4,3,2,1,0:T(8,128)(2,1)S(1)}, bf16[2,768,768]{2,1,0:T(8,128)(2,1)S(1)}) custom-call(s32[5]{0:T(128)S(1)} %convert_element_type.3.flags, bf16[2,6,32,384]{3,2,1,0:T(8,128)(2,1)S(1)} %get-tuple-element.26.act_prev, bf16[2,2,2,32,384]{4,3,2,1,0:T(8,128)(2,1)S(1)} %collective-permute-done.3.halo, ...), custom_call_target="tpu_custom_call" | custom-call | flops 1000000000 | bytes 3000000 | tf_op jit(solution)/shard_map/rim_second/pallas_call | solution.py:314
  22.1 0.4 %collective-permute-start.5 = (bf16[2,2,2,32,384]{4,3,2,1,0:T(8,128)(2,1)S(1)}, bf16[2,2,2,32,384]{4,3,2,1,0:T(8,128)(2,1)S(1)}, u32[]{:S(2)}, u32[]{:S(2)}) collective-permute-start(bf16[2,2,2,32,384]{4,3,2,1,0:T(8,128)(2,1)S(1)} %get-tuple-element.36.refs_5_), channel_id=1, source_target_pairs={{0,32},{1,33},{2,34},{3,35},{4,36},{5,37},{6,38},{7,39},{8,40},{9,... | collective-permute-start | bytes 589832 | tf_op jit(solution)/shard_map/ppermute | solution.py:24
  22.4 0.3 collective-permute-done.4.refs_3_
  22.7 3.1 %up_inner.1 = (bf16[4,6,64,192]{3,2,1,0:T(8,128)(2,1)S(1)}, bf16[2,2,2,32,384]{4,3,2,1,0:T(8,128)(2,1)S(1)}, f32[256,768]{1,0:T(8,128)S(1)}) custom-call(s32[5]{0:T(128)S(1)} %convert_element_type.3.flags, bf16[2,768,768]{2,1,0:T(8,128)(2,1)S(1)} %get-tuple-element.32.refs_0_, bf16[2,768,768]{2,1,0:T(8,128)(2,1)S(1)} %get-tuple-element.33.refs_1_, ...), custom_call_target="tpu_custom_call" | custom-call | flops 1000000000 | bytes 3000000 | tf_op jit(solution)/shard_map/up_inner/pallas_call | solution.py:314
  25.8 0.4 %collective-permute-done.6.refs_4_ = bf16[2,2,2,32,384]{4,3,2,1,0:T(8,128)(2,1)S(1)} collective-permute-done((bf16[2,2,2,32,384]{4,3,2,1,0:T(8,128)(2,1)S(1)}, bf16[2,2,2,32,384]{4,3,2,1,0:T(8,128)(2,1)S(1)}, u32[]{:S(2)}, u32[]{:S(2)}) %collective-permute-start.6) | collective-permute-done | bytes 196640 | tf_op jit(solution)/shard_map/ppermute | solution.py:24
  26.2 0.0 collective-permute-done.5.refs_3_
  26.2 2.9 %up_rim.1 = bf16[4,12,64,192]{3,2,1,0:T(8,128)(2,1)} custom-call(s32[5]{0:T(128)S(1)} %convert_element_type.3.flags, bf16[2,768,768]{2,1,0:T(8,128)(2,1)S(1)} %get-tuple-element.32.refs_0_, bf16[2,768,768]{2,1,0:T(8,128)(2,1)S(1)} %get-tuple-element.33.refs_1_, f32[256,768]{1,0:T(8,128)S(1)} %get-tuple-element.38.refs_2_, ...), custom_call_target="tpu_custom_call" | custom-call | flops 1000000000 | bytes 3000000 | tf_op jit(solution)/shard_map/up_rim/pallas_call | solution.py:314
  (3 shorter events, 0.1 us)
Async XLA Ops:
  0.1 1.0 %copy-start.1 = (bf16[2,6,32,384]{3,2,1,0:T(8,128)(2,1)S(1)}, bf16[2,6,32,384]{3,2,1,0:T(8,128)(2,1)}, u32[]{:S(2)}) copy-start(bf16[2,6,32,384]{3,2,1,0:T(8,128)(2,1)} %features.1) | copy-start | bytes 884740
  0.1 6.8 %copy-start = (bf16[3,3,3,384,384]{4,3,2,1,0:T(8,128)(2,1)S(1)}, bf16[3,3,3,384,384]{4,3,2,1,0:T(8,128)(2,1)}, u32[]{:S(2)}) copy-start(bf16[3,3,3,384,384]{4,3,2,1,0:T(8,128)(2,1)} %res_held.9) | copy-start | bytes 23887876
  1.1 8.9 %collective-permute-start.1 = (bf16[2,2,32,384]{3,2,1,0:T(8,128)(2,1)S(1)}, bf16[2,2,32,384]{3,2,1,0:T(8,128)(2,1)S(1)}, u32[]{:S(2)}, u32[]{:S(2)}) collective-permute-start(bf16[2,2,32,384]{3,2,1,0:T(8,128)(2,1)S(1)} %get-tuple-element.27), channel_id=1, source_target_pairs={{0,0},{1,2},{2,1},{3,4},{4,3},{5,6},{6,5},{7,8},{8,7},{9,10},{10,9... | collective-permute-start | bytes 294920 | tf_op jit(solution)/shard_map/ppermute | solution.py:24
  6.7 4.7 %collective-permute-start.2 = (bf16[2,2,32,384]{3,2,1,0:T(8,128)(2,1)S(1)}, bf16[2,2,32,384]{3,2,1,0:T(8,128)(2,1)S(1)}, u32[]{:S(2)}, u32[]{:S(2)}) collective-permute-start(bf16[2,2,32,384]{3,2,1,0:T(8,128)(2,1)S(1)} %get-tuple-element.28), channel_id=1, source_target_pairs={{0,1},{1,0},{2,3},{3,2},{4,5},{5,4},{6,7},{7,6},{8,9},{9,8},{10,11... | collective-permute-start | bytes 294920 | tf_op jit(solution)/shard_map/ppermute | solution.py:24
  6.8 7.4 %collective-permute-start = (bf16[2,6,32,384]{3,2,1,0:T(8,128)(2,1)S(1)}, bf16[2,6,32,384]{3,2,1,0:T(8,128)(2,1)S(1)}, u32[]{:S(2)}, u32[]{:S(2)}) collective-permute-start(bf16[2,6,32,384]{3,2,1,0:T(8,128)(2,1)S(1)} %copy-done.1), channel_id=1, source_target_pairs={{0,32},{1,33},{2,34},{3,35},{4,36},{5,37},{6,38},{7,39},{8,40},{9,... | collective-permute-start | bytes 884744 | tf_op jit(solution)/shard_map/ppermute | solution.py:24
  12.2 6.3 %collective-permute-start.3 = (bf16[2,2,2,32,384]{4,3,2,1,0:T(8,128)(2,1)S(1)}, bf16[2,2,2,32,384]{4,3,2,1,0:T(8,128)(2,1)S(1)}, u32[]{:S(2)}, u32[]{:S(2)}) collective-permute-start(bf16[2,2,2,32,384]{4,3,2,1,0:T(8,128)(2,1)S(1)} %halo.1), channel_id=1, source_target_pairs={{0,32},{1,33},{2,34},{3,35},{4,36},{5,37},{6,38},{7,39},{8,40},{9,... | collective-permute-start | bytes 589832 | tf_op jit(solution)/shard_map/ppermute | solution.py:24
  16.4 6.3 %collective-permute-start.4 = (bf16[2,4,32,384]{3,2,1,0:T(8,128)(2,1)S(1)}, bf16[2,4,32,384]{3,2,1,0:T(8,128)(2,1)S(1)}, u32[]{:S(2)}, u32[]{:S(2)}) collective-permute-start(bf16[2,4,32,384]{3,2,1,0:T(8,128)(2,1)S(1)} %get-tuple-element.34.refs_2_), channel_id=1, source_target_pairs={{0,32},{1,33},{2,34},{3,35},{4,36},{5,37},{6,38},{7,39},{8,40},{9,... | collective-permute-start | bytes 589832 | tf_op jit(solution)/shard_map/ppermute | solution.py:24
  19.9 6.3 %collective-permute-start.6 = (bf16[2,2,2,32,384]{4,3,2,1,0:T(8,128)(2,1)S(1)}, bf16[2,2,2,32,384]{4,3,2,1,0:T(8,128)(2,1)S(1)}, u32[]{:S(2)}, u32[]{:S(2)}) collective-permute-start(bf16[2,2,2,32,384]{4,3,2,1,0:T(8,128)(2,1)S(1)} %get-tuple-element.35.refs_4_), channel_id=1, source_target_pairs={{0,32},{1,33},{2,34},{3,35},{4,36},{5,37},{6,38},{7,39},{8,40},{9,... | collective-permute-start | bytes 589832 | tf_op jit(solution)/shard_map/ppermute | solution.py:24
  22.1 4.1 %collective-permute-start.5 = (bf16[2,2,2,32,384]{4,3,2,1,0:T(8,128)(2,1)S(1)}, bf16[2,2,2,32,384]{4,3,2,1,0:T(8,128)(2,1)S(1)}, u32[]{:S(2)}, u32[]{:S(2)}) collective-permute-start(bf16[2,2,2,32,384]{4,3,2,1,0:T(8,128)(2,1)S(1)} %get-tuple-element.36.refs_5_), channel_id=1, source_target_pairs={{0,32},{1,33},{2,34},{3,35},{4,36},{5,37},{6,38},{7,39},{8,40},{9,... | collective-permute-start | bytes 589832 | tf_op jit(solution)/shard_map/ppermute | solution.py:24

commit v5 on v3

--- a/solution.py
+++ b/solution.py
@@ -8,7 +8,6 @@
 F32 = jnp.float32
 BF16 = jnp.bfloat16
 VMEM = pl.BlockSpec(memory_space=pltpu.VMEM)
-SMEM = pl.BlockSpec(memory_space=pltpu.SMEM)
 HBM = pl.BlockSpec(memory_space=pltpu.HBM)
 
 
@@ -20,6 +19,12 @@
             to_t, to_r = target(t, r)
             pairs.append((t * nr + r, to_t * nr + to_r))
     return lax.ppermute(block, ("tm", "rows"), pairs)
+
+
+def place():
+    t, r = lax.axis_index("tm"), lax.axis_index("rows")
+    conditions = (t > 0, r > 0, r < lax.axis_size("rows") - 1, (r & 1) == 1)
+    return [condition.astype(jnp.int32) for condition in conditions]
 
 
 def activated(values, gain):
@@ -102,7 +107,8 @@
     return jnp.dot(lhs, rhs, preferred_element_type=F32)
 
 
-def inner_kernel(flags, prev, gain, res_held, partial, out, act):
+def inner_kernel(prev, gain, res_held, partial, out, act):
+    flags = place()
     rows, cols, ch = act.shape[1:]
     keep = flags[0].astype(F32)
     act[...] = (activated(prev[...].astype(F32), gain[...].reshape(1, 1, 1, ch)) * keep).astype(BF16)
@@ -114,7 +120,8 @@
     out[...] = (partial[...] + branch).astype(BF16)
 
 
-def halo_kernel(flags, cross, pair, gain, out):
+def halo_kernel(cross, pair, gain, out):
+    flags = place()
     ch = pair.shape[-1]
     odd = flags[3]
     inside = jnp.where(odd == 1, flags[2], flags[1]).astype(F32)
@@ -129,7 +136,8 @@
     ]
 
 
-def rim_own_kernel(flags, act_own, halo, own, cross, pair, res_held, out, act):
+def rim_own_kernel(act_own, halo, own, cross, pair, res_held, out, act):
+    flags = place()
     rows, cols, ch = own.shape[1:]
     odd = flags[3]
     act[:, 0, 0:2] = halo[:, 0]
@@ -149,7 +157,8 @@
     out[:, 1, 1] = below + branch[:, 1, 1]
 
 
-def rim_kernel(flags, act_prev, halo, partial, res_held, out, act):
+def rim_kernel(act_prev, halo, partial, res_held, out, act):
+    flags = place()
     rows = act_prev.shape[1]
     cols, ch = partial.shape[3:]
     keep = flags[0].astype(BF16)
@@ -197,7 +206,8 @@
     return line
 
 
-def up_inner_kernel(flags, own, prev, rim_own, time_weight, weight, stage, inner_rim, rim_part, stack, up, woven):
+def up_inner_kernel(own, prev, rim_own, time_weight, weight, stage, inner_rim, rim_part, stack, up, woven):
+    flags = place()
     frames, lines, cols, ch = own.shape
     co = stage.shape[-1]
     stack[2:4] = own[...]
@@ -226,8 +236,9 @@
 
 
 def up_rim_kernel(
-    flags, part, prev, inner_rim, inner_stage, time_weight, weight, out, up, woven, stage, sems
+    part, prev, inner_rim, inner_stage, time_weight, weight, out, up, woven, stage, sems
 ):
+    flags = place()
     frames, sides, lines, cols, ch = prev.shape
     co = out.shape[-1]
     middle = pltpu.make_async_copy(inner_stage, out.at[:, 3 : 3 + inner_stage.shape[1]], sems.at[6])
@@ -305,7 +316,6 @@
     nt, nr = lax.axis_size("tm"), lax.axis_size("rows")
     co = up_weight.shape[-1]
     t, r = lax.axis_index("tm"), lax.axis_index("rows")
-    flags = jnp.stack([t > 0, r > 0, r < nr - 1, (r & 1) == 1]).astype(jnp.int32)
     sizes = (nt, nr)
     shape = jax.ShapeDtypeStruct
 
@@ -346,10 +356,10 @@
         halo_kernel,
         "halo",
         vmem_out((2, 2, 2, cols, ch), BF16),
-        [SMEM] + [VMEM] * 3,
+        [VMEM] * 3,
         [],
         8,
-        (flags, cross, pair, gain),
+        (cross, pair, gain),
     )
     prev_halo = later(halo)
     act_prev_shape = vmem_out((2, rows, cols, ch), BF16)
@@ -357,10 +367,10 @@
         inner_kernel,
         "inner",
         [shape((2, lines, cols, ch), BF16), act_prev_shape],
-        [SMEM] + [VMEM] * 4,
+        [VMEM] * 4,
         [],
         16,
-        (flags, prev, gain, in_vmem(res_held), inner_own),
+        (prev, gain, in_vmem(res_held), inner_own),
     )
     inner_prev = later(inner)
     side_rows = [pltpu.VMEM((2, 2, 4, cols, ch), BF16)]
@@ -368,19 +378,19 @@
         rim_own_kernel,
         "rim_own",
         vmem_out((2, 2, 2, cols, ch), F32),
-        [SMEM] + [VMEM] * 6,
+        [VMEM] * 6,
         side_rows,
         16,
-        (flags, act_own, halo, own, cross, pair, in_vmem(res_held)),
+        (act_own, halo, own, cross, pair, in_vmem(res_held)),
     )
     rim = call(
         rim_kernel,
         "rim",
         shape((2, 2, 2, cols, ch), BF16),
-        [SMEM] + [VMEM] * 4,
+        [VMEM] * 4,
         side_rows,
         16,
-        (flags, act_prev, prev_halo, rim_own, in_vmem(res_held)),
+        (act_prev, prev_halo, rim_own, in_vmem(res_held)),
     )
     rim_prev = later(rim)
     up_turned = jnp.swapaxes(up_weight, 2, 3)
@@ -401,20 +411,20 @@
             vmem_out((2, 2, 2, cols, ch), BF16),
             vmem_out((frames * 4 * cols, 2 * ch), F32),
         ],
-        [SMEM] + [VMEM] * 5,
+        [VMEM] * 5,
         [
             pltpu.VMEM((4, lines, cols, ch), BF16),
             pltpu.VMEM((2, 2, lines, cols, ch), BF16),
             pltpu.VMEM((2, 2 * frames * (lines - 1) * 2 * cols, 128), F32),
         ],
         24,
-        (flags, inner, inner_prev, rim, in_vmem(time_held), in_vmem(combined)),
+        (inner, inner_prev, rim, in_vmem(time_held), in_vmem(combined)),
     )
     return call(
         up_rim_kernel,
         "up_rim",
         shape((2 * frames, 2 * rows, 2 * cols, co), BF16),
-        [SMEM] + [VMEM] * 6,
+        [VMEM] * 6,
         [
             pltpu.VMEM((2, 2, 2, 3, cols, ch), BF16),
             pltpu.VMEM((2, 2 * frames * 3 * 2 * cols, 128), F32),
@@ -422,7 +432,7 @@
             pltpu.SemaphoreType.DMA((7,)),
         ],
         24,
-        (flags, rim_part, rim_prev, inner_rim, stage, in_vmem(time_held), in_vmem(combined)),
+        (rim_part, rim_prev, inner_rim, stage, in_vmem(time_held), in_vmem(combined)),
         out_specs=HBM,
     )
 

time: 29.5 us -> 28.4 us (0.963)
  Pallas kernels: 18.4 us -> 14.9 us
  waiting for transfers between devices: 2.54 us -> 5.2 us
    pallas_call x8, Pallas kernels: 18.4 us -> 14.9 us  [call(): pl.pallas_call(kernel, out_shape=shapes, in_specs=specs, out_specs=out_sp...]
    ppermute x6, waiting for transfers between devices: 2.54 us -> 5.2 us  [moved(): return lax.ppermute(block, ('tm', 'rows'), pairs)]
  transfers between devices with their start and end apart: 6 -> 6, of which waited for: 4 -> 4; matrix products, arithmetic and copies ran while one was open for 0% -> 0% of each run, Pallas kernels for 53% -> 44%
where the time goes in v5:
time: 28.4 us; the launch traced here: 28.3 us
  Pallas kernels  14.9 us (52%)
  starting transfers between devices  7.09 us (25%)
  waiting for transfers between devices  5.2 us (18%)
  other arithmetic  0.96 us (3%)
    pallas_call x8, Pallas kernels, call(): pl.pallas_call(kernel, out_shape=shapes, in_specs=specs, out_specs=out_sp...  14.9 us
    ppermute x6, starting transfers between devices, moved(): return lax.ppermute(block, ('tm', 'rows'), pairs)  7.09 us
    ppermute x6, waiting for transfers between devices, moved(): return lax.ppermute(block, ('tm', 'rows'), pairs)  5.2 us
    select_n x1, other arithmetic, shards(): to_pair = jnp.where(odd, top, bottom)  0.96 us
  transfers between devices with their start and end apart: 6, of which 4 were waited for; matrix products, arithmetic and copies ran while one was open for 0% of the time, Pallas kernels for 44%

profile of v5, /device:TPU:192, one launch (start us, length us, event | category | flops | bytes accessed | tf_op | source)
XLA Modules:
  0.0 28.3 jit_solution(2593746587887485623)
XLA Ops:
  0.0 1.0 %broadcast_select_fusion = (bf16[2,2,32,384]{3,2,1,0:T(8,128)(2,1)S(1)}, bf16[2,2,32,384]{3,2,1,0:T(8,128)(2,1)S(1)}) fusion(pred[]{:T(512)S(6)} %eq.3, bf16[2,6,32,384]{3,2,1,0:T(8,128)(2,1)} %features.1), kind=kLoop, calls=%fused_computation | loop fusion | flops 98304 | bytes 393217 | tf_op jit(solution)/shard_map/jit(_where)/select_n | solution.py:333
  1.0 5.4 %collective-permute-start.2 = (bf16[2,2,32,384]{3,2,1,0:T(8,128)(2,1)S(1)}, bf16[2,2,32,384]{3,2,1,0:T(8,128)(2,1)S(1)}, u32[]{:S(2)}, u32[]{:S(2)}) collective-permute-start(bf16[2,2,32,384]{3,2,1,0:T(8,128)(2,1)S(1)} %get-tuple-element.26), channel_id=1, source_target_pairs={{0,0},{1,2},{2,1},{3,4},{4,3},{5,6},{6,5},{7,8},{8,7},{9,10},{10,9... | collective-permute-start | bytes 294920 | tf_op jit(solution)/shard_map/ppermute | solution.py:21
  6.3 0.0 collective-permute-start
  6.4 0.1 collective-permute-start.3
  6.5 3.5 %prepare.1 = (bf16[2,6,32,384]{3,2,1,0:T(8,128)(2,1)S(1)}, bf16[2,6,32,384]{3,2,1,0:T(8,128)(2,1)S(1)}, f32[1,384]{1,0:T(1,128)S(1)}, bf16[3,3,3,384,384]{4,3,2,1,0:T(8,128)(2,1)S(1)}, f32[2,4,32,384]{3,2,1,0:T(8,128)S(1)}) custom-call(bf16[2,6,32,384]{3,2,1,0:T(8,128)(2,1)} %features.1, f32[384]{0:T(512)} %gain.1, bf16[3,3,3,384,384]{4,3,2,1,0:T(8,128)(2,1)} %res_weight.1), custom_call_target="tpu_custom_call" | custom-call | flops 1000000000 | bytes 3000000 | tf_op jit(solution)/shard_map/prepare/pallas_call | solution.py:290
  10.0 0.0 collective-permute-done.2.cross
  10.0 1.6 %collective-permute-done.3.pair = bf16[2,2,32,384]{3,2,1,0:T(8,128)(2,1)S(1)} collective-permute-done((bf16[2,2,32,384]{3,2,1,0:T(8,128)(2,1)S(1)}, bf16[2,2,32,384]{3,2,1,0:T(8,128)(2,1)S(1)}, u32[]{:S(2)}, u32[]{:S(2)}) %collective-permute-start.3) | collective-permute-done | bytes 98336 | tf_op jit(solution)/shard_map/ppermute | solution.py:21
  11.7 0.2 halo.1
  11.9 0.6 %collective-permute-start.4 = (bf16[2,2,2,32,384]{4,3,2,1,0:T(8,128)(2,1)S(1)}, bf16[2,2,2,32,384]{4,3,2,1,0:T(8,128)(2,1)S(1)}, u32[]{:S(2)}, u32[]{:S(2)}) collective-permute-start(bf16[2,2,2,32,384]{4,3,2,1,0:T(8,128)(2,1)S(1)} %halo.1), channel_id=1, source_target_pairs={{0,32},{1,33},{2,34},{3,35},{4,36},{5,37},{6,38},{7,39},{8,40},{9,... | collective-permute-start | bytes 589832 | tf_op jit(solution)/shard_map/ppermute | solution.py:21
  12.5 1.4 %rim_own.1.partial = f32[2,2,2,32,384]{4,3,2,1,0:T(8,128)S(1)} custom-call(bf16[2,6,32,384]{3,2,1,0:T(8,128)(2,1)S(1)} %get-tuple-element.28.act_own, bf16[2,2,2,32,384]{4,3,2,1,0:T(8,128)(2,1)S(1)} %halo.1, bf16[2,6,32,384]{3,2,1,0:T(8,128)(2,1)S(1)} %get-tuple-element.29.own, bf16[2,2,32,384]{3,2,1,0:T(8,128)(2,1)S(1)} %collective-permute-done.2.cross, ...), custom_call_target="tpu_custom_call" | custom-call | flops 1000000000 | bytes 3000000 | tf_op jit(solution)/shard_map/rim_own/pallas_call | solution.py:290
  13.9 0.0 collective-permute-done.prev
  13.9 1.6 %inner.1 = (bf16[2,4,32,384]{3,2,1,0:T(8,128)(2,1)S(1)}, bf16[2,6,32,384]{3,2,1,0:T(8,128)(2,1)S(1)}) custom-call(bf16[2,6,32,384]{3,2,1,0:T(8,128)(2,1)S(1)} %collective-permute-done.prev, f32[1,384]{1,0:T(1,128)S(1)} %get-tuple-element.21.gain, bf16[3,3,3,384,384]{4,3,2,1,0:T(8,128)(2,1)S(1)} %get-tuple-element.22.res_held, ...), custom_call_target="tpu_custom_call" | custom-call | flops 1000000000 | bytes 3000000 | tf_op jit(solution)/shard_map/inner/pallas_call | solution.py:290
  15.6 1.0 %collective-permute-start.1 = (bf16[2,4,32,384]{3,2,1,0:T(8,128)(2,1)S(1)}, bf16[2,4,32,384]{3,2,1,0:T(8,128)(2,1)S(1)}, u32[]{:S(2)}, u32[]{:S(2)}) collective-permute-start(bf16[2,4,32,384]{3,2,1,0:T(8,128)(2,1)S(1)} %get-tuple-element.24.own), channel_id=1, source_target_pairs={{0,32},{1,33},{2,34},{3,35},{4,36},{5,37},{6,38},{7,39},{8,40},{9,... | collective-permute-start | bytes 589832 | tf_op jit(solution)/shard_map/ppermute | solution.py:21
  16.6 1.6 %collective-permute-done.4.halo = bf16[2,2,2,32,384]{4,3,2,1,0:T(8,128)(2,1)S(1)} collective-permute-done((bf16[2,2,2,32,384]{4,3,2,1,0:T(8,128)(2,1)S(1)}, bf16[2,2,2,32,384]{4,3,2,1,0:T(8,128)(2,1)S(1)}, u32[]{:S(2)}, u32[]{:S(2)}) %collective-permute-start.4) | collective-permute-done | bytes 196640 | tf_op jit(solution)/shard_map/ppermute | solution.py:21
  18.2 1.4 %rim.1.after.rim_own = bf16[2,2,2,32,384]{4,3,2,1,0:T(8,128)(2,1)S(1)} custom-call(bf16[2,6,32,384]{3,2,1,0:T(8,128)(2,1)S(1)} %get-tuple-element.25.act_prev, bf16[2,2,2,32,384]{4,3,2,1,0:T(8,128)(2,1)S(1)} %collective-permute-done.4.halo, f32[2,2,2,32,384]{4,3,2,1,0:T(8,128)S(1)} %rim_own.1.partial, bf16[3,3,3,384,384]{4,3,2,1,0:T(8,128)(2,1)S(1)} %get-tuple-element.22.res_held), custom_call_target="tpu_custom_call" | custom-call | flops 1000000000 | bytes 3000000 | tf_op jit(solution)/shard_map/rim/pallas_call | solution.py:290
  19.6 0.0 collective-permute-start.5
  19.6 2.1 %combine.1 = (bf16[2,768,768]{2,1,0:T(8,128)(2,1)S(1)}, bf16[3,384,768]{2,1,0:T(8,128)(2,1)S(1)}) custom-call(bf16[3,3,192,384]{3,2,1,0:T(8,128)(2,1)} %bitcast.1, bf16[3,384,768]{2,1,0:T(8,128)(2,1)} %time_weight.1, bf16[2,2,2,32,384]{4,3,2,1,0:T(8,128)(2,1)S(1)} %rim.1.after.rim_own), custom_call_target="tpu_custom_call" | custom-call | flops 1000000000 | bytes 3000000 | tf_op jit(solution)/shard_map/combine/pallas_call | solution.py:290
  21.7 0.1 collective-permute-done.1.prev
  21.9 2.3 %up_inner.1 = (bf16[4,6,64,192]{3,2,1,0:T(8,128)(2,1)S(1)}, bf16[2,2,2,32,384]{4,3,2,1,0:T(8,128)(2,1)S(1)}, f32[256,768]{1,0:T(8,128)S(1)}) custom-call(bf16[2,4,32,384]{3,2,1,0:T(8,128)(2,1)S(1)} %get-tuple-element.24.own, bf16[2,4,32,384]{3,2,1,0:T(8,128)(2,1)S(1)} %collective-permute-done.1.prev, bf16[2,2,2,32,384]{4,3,2,1,0:T(8,128)(2,1)S(1)} %rim.1.after.rim_own, ...), custom_call_target="tpu_custom_call" | custom-call | flops 1000000000 | bytes 3000000 | tf_op jit(solution)/shard_map/up_inner/pallas_call | solution.py:290
  24.2 1.8 %collective-permute-done.5.prev = bf16[2,2,2,32,384]{4,3,2,1,0:T(8,128)(2,1)S(1)} collective-permute-done((bf16[2,2,2,32,384]{4,3,2,1,0:T(8,128)(2,1)S(1)}, bf16[2,2,2,32,384]{4,3,2,1,0:T(8,128)(2,1)S(1)}, u32[]{:S(2)}, u32[]{:S(2)}) %collective-permute-start.5) | collective-permute-done | bytes 196640 | tf_op jit(solution)/shard_map/ppermute | solution.py:21
  25.9 2.4 %up_rim.1 = bf16[4,12,64,192]{3,2,1,0:T(8,128)(2,1)} custom-call(f32[256,768]{1,0:T(8,128)S(1)} %get-tuple-element.32.part, bf16[2,2,2,32,384]{4,3,2,1,0:T(8,128)(2,1)S(1)} %collective-permute-done.5.prev, bf16[2,2,2,32,384]{4,3,2,1,0:T(8,128)(2,1)S(1)} %get-tuple-element.33.inner_rim, bf16[4,6,64,192]{3,2,1,0:T(8,128)(2,1)S(1)} %get-tuple-element.34.inner_stage, ...), custom_call_target="tpu_custom_call" | custom-call | flops 1000000000 | bytes 3000000 | tf_op jit(solution)/shard_map/up_rim/pallas_call | solution.py:290
Async XLA Ops:
  1.0 9.0 %collective-permute-start.2 = (bf16[2,2,32,384]{3,2,1,0:T(8,128)(2,1)S(1)}, bf16[2,2,32,384]{3,2,1,0:T(8,128)(2,1)S(1)}, u32[]{:S(2)}, u32[]{:S(2)}) collective-permute-start(bf16[2,2,32,384]{3,2,1,0:T(8,128)(2,1)S(1)} %get-tuple-element.26), channel_id=1, source_target_pairs={{0,0},{1,2},{2,1},{3,4},{4,3},{5,6},{6,5},{7,8},{8,7},{9,10},{10,9... | collective-permute-start | bytes 294920 | tf_op jit(solution)/shard_map/ppermute | solution.py:21
  6.3 7.6 %collective-permute-start = (bf16[2,6,32,384]{3,2,1,0:T(8,128)(2,1)}, bf16[2,6,32,384]{3,2,1,0:T(8,128)(2,1)S(1)}, u32[]{:S(2)}, u32[]{:S(2)}) collective-permute-start(bf16[2,6,32,384]{3,2,1,0:T(8,128)(2,1)} %features.1), channel_id=1, source_target_pairs={{0,32},{1,33},{2,34},{3,35},{4,36},{5,37},{6,38},{7,39},{8,40},{9,... | collective-permute-start | bytes 884744 | tf_op jit(solution)/shard_map/ppermute | solution.py:21
  6.4 5.3 %collective-permute-start.3 = (bf16[2,2,32,384]{3,2,1,0:T(8,128)(2,1)S(1)}, bf16[2,2,32,384]{3,2,1,0:T(8,128)(2,1)S(1)}, u32[]{:S(2)}, u32[]{:S(2)}) collective-permute-start(bf16[2,2,32,384]{3,2,1,0:T(8,128)(2,1)S(1)} %get-tuple-element.27), channel_id=1, source_target_pairs={{0,1},{1,0},{2,3},{3,2},{4,5},{5,4},{6,7},{7,6},{8,9},{9,8},{10,11... | collective-permute-start | bytes 294920 | tf_op jit(solution)/shard_map/ppermute | solution.py:21
  11.9 6.3 %collective-permute-start.4 = (bf16[2,2,2,32,384]{4,3,2,1,0:T(8,128)(2,1)S(1)}, bf16[2,2,2,32,384]{4,3,2,1,0:T(8,128)(2,1)S(1)}, u32[]{:S(2)}, u32[]{:S(2)}) collective-permute-start(bf16[2,2,2,32,384]{4,3,2,1,0:T(8,128)(2,1)S(1)} %halo.1), channel_id=1, source_target_pairs={{0,32},{1,33},{2,34},{3,35},{4,36},{5,37},{6,38},{7,39},{8,40},{9,... | collective-permute-start | bytes 589832 | tf_op jit(solution)/shard_map/ppermute | solution.py:21
  15.6 6.3 %collective-permute-start.1 = (bf16[2,4,32,384]{3,2,1,0:T(8,128)(2,1)S(1)}, bf16[2,4,32,384]{3,2,1,0:T(8,128)(2,1)S(1)}, u32[]{:S(2)}, u32[]{:S(2)}) collective-permute-start(bf16[2,4,32,384]{3,2,1,0:T(8,128)(2,1)S(1)} %get-tuple-element.24.own), channel_id=1, source_target_pairs={{0,32},{1,33},{2,34},{3,35},{4,36},{5,37},{6,38},{7,39},{8,40},{9,... | collective-permute-start | bytes 589832 | tf_op jit(solution)/shard_map/ppermute | solution.py:21
  19.6 6.3 %collective-permute-start.5 = (bf16[2,2,2,32,384]{4,3,2,1,0:T(8,128)(2,1)S(1)}, bf16[2,2,2,32,384]{4,3,2,1,0:T(8,128)(2,1)S(1)}, u32[]{:S(2)}, u32[]{:S(2)}) collective-permute-start(bf16[2,2,2,32,384]{4,3,2,1,0:T(8,128)(2,1)S(1)} %rim.1.after.rim_own), channel_id=1, source_target_pairs={{0,32},{1,33},{2,34},{3,35},{4,36},{5,37},{6,38},{7,39},{8,40},{9,... | collective-permute-start | bytes 589832 | tf_op jit(solution)/shard_map/ppermute | solution.py:21

commit v6 on v4

--- a/solution.py
+++ b/solution.py
@@ -10,7 +10,6 @@
 F32 = jnp.float32
 BF16 = jnp.bfloat16
 VMEM = pl.BlockSpec(memory_space=pltpu.VMEM)
-SMEM = pl.BlockSpec(memory_space=pltpu.SMEM)
 HBM = pl.BlockSpec(memory_space=pltpu.HBM)
 
 
@@ -24,6 +23,12 @@
     return lax.ppermute(block, ("tm", "rows"), pairs)
 
 
+def place():
+    t, r = lax.axis_index("tm"), lax.axis_index("rows")
+    conditions = (t > 0, r > 0, r < lax.axis_size("rows") - 1, (r & 1) == 1, (t & 1) == 1)
+    return [condition.astype(jnp.int32) for condition in conditions]
+
+
 def activated(values, gain):
     inv = lax.rsqrt(jnp.mean(values * values, axis=-1, keepdims=True) + 1e-06)
     half = values * inv * gain * 0.5
@@ -38,7 +43,8 @@
     ]
 
 
-def parity_kernel(flags, out):
+def parity_kernel(out):
+    flags = place()
     out[...] = jnp.zeros(out.shape, F32) + flags[3].astype(F32)
 
 
@@ -99,7 +105,8 @@
     return jnp.dot(lhs, rhs, preferred_element_type=F32)
 
 
-def inner_kernel(flags, prev, gain, res_held, partial, out, act):
+def inner_kernel(prev, gain, res_held, partial, out, act):
+    flags = place()
     rows, cols, ch = act.shape[1:]
     keep = flags[0].astype(F32)
     act[...] = (activated(prev[...].astype(F32), gain[...].reshape(1, 1, 1, ch)) * keep).astype(BF16)
@@ -111,7 +118,8 @@
     out[...] = (partial[...] + branch).astype(BF16)
 
 
-def halo_kernel(flags, cross, pair, gain, out):
+def halo_kernel(cross, pair, gain, out):
+    flags = place()
     ch = pair.shape[-1]
     odd = flags[3]
     inside = jnp.where(odd == 1, flags[2], flags[1]).astype(F32)
@@ -126,7 +134,8 @@
     ]
 
 
-def rim_own_kernel(flags, act_own, halo, own, cross, pair, res_held, out, act):
+def rim_own_kernel(act_own, halo, own, cross, pair, res_held, out, act):
+    flags = place()
     rows, cols, ch = own.shape[1:]
     odd = flags[3]
     act[:, 0, 0:2] = halo[:, 0]
@@ -165,7 +174,8 @@
     out[:, 1, 1] = (blended[:, 1, 1] * flags[2].astype(F32)).astype(BF16)
 
 
-def rim_first_kernel(flags, act_prev, halo, partial, res_held, up_weight, out, combined, act):
+def rim_first_kernel(act_prev, halo, partial, res_held, up_weight, out, combined, act):
+    flags = place()
     @pl.when(flags[4] == 1)
     def _():
         rim_value(flags, act_prev, halo, partial, res_held, out, act)
@@ -176,7 +186,8 @@
         combine(up_weight, combined)
 
 
-def rim_second_kernel(flags, act_prev, halo, partial, res_held, up_weight, out, combined, act):
+def rim_second_kernel(act_prev, halo, partial, res_held, up_weight, out, combined, act):
+    flags = place()
     @pl.when(flags[4] == 0)
     def _():
         rim_value(flags, act_prev, halo, partial, res_held, out, act)
@@ -216,7 +227,8 @@
     return line
 
 
-def by_core(kernel, flags, *refs):
+def by_core(kernel, *refs):
+    flags = place()
     second, first, *rest = refs
 
     @pl.when(flags[4] == 0)
@@ -341,7 +353,6 @@
     nt, nr = lax.axis_size("tm"), lax.axis_size("rows")
     co = up_weight.shape[-1]
     t, r = lax.axis_index("tm"), lax.axis_index("rows")
-    flags = jnp.stack([t > 0, r > 0, r < nr - 1, (r & 1) == 1, (t & 1) == 1]).astype(jnp.int32)
     sizes = (nt, nr)
     shape = jax.ShapeDtypeStruct
 
@@ -354,7 +365,7 @@
     def later(block):
         return moved(block, sizes, lambda t, r: ((t + 1) % nt, r))
 
-    parity = call(parity_kernel, "parity", vmem_out((1, ch), F32), [SMEM], [], 1, (flags,), us=5)
+    parity = call(parity_kernel, "parity", vmem_out((1, ch), F32), [], [], 1, (), us=5)
     odd = parity.reshape(1, 1, 1, ch) > 0.5
     top, bottom = features[:, :2], features[:, -2:]
     to_pair = jnp.where(odd, top, bottom)
@@ -387,10 +398,10 @@
         halo_kernel,
         "halo",
         vmem_out((2, 2, 2, cols, ch), BF16),
-        [SMEM] + [VMEM] * 3,
+        [VMEM] * 3,
         [],
         8,
-        (flags, cross, pair, gain),
+        (cross, pair, gain),
     )
     prev_halo = later(halo)
     act_prev_shape = vmem_out((2, rows, cols, ch), BF16)
@@ -398,10 +409,10 @@
         inner_kernel,
         "inner",
         [shape((2, lines, cols, ch), BF16), act_prev_shape],
-        [SMEM] + [VMEM] * 4,
+        [VMEM] * 4,
         [],
         16,
-        (flags, prev, gain, res_held, inner_own),
+        (prev, gain, res_held, inner_own),
     )
     inner_prev = later(inner)
     side_rows = [pltpu.VMEM((2, 2, 4, cols, ch), BF16)]
@@ -409,10 +420,10 @@
         rim_own_kernel,
         "rim_own",
         vmem_out((2, 2, 2, cols, ch), F32),
-        [SMEM] + [VMEM] * 6,
+        [VMEM] * 6,
         side_rows,
         16,
-        (flags, act_own, halo, own, cross, pair, res_held),
+        (act_own, halo, own, cross, pair, res_held),
     )
     rim_shape = vmem_out((2, 2, 2, cols, ch), BF16)
     sums_shape = vmem_out((2, 2 * ch, 4 * co), BF16)
@@ -420,20 +431,20 @@
         rim_first_kernel,
         "rim_first",
         [rim_shape, sums_shape],
-        [SMEM] + [VMEM] * 5,
+        [VMEM] * 5,
         side_rows,
         24,
-        (flags, act_prev, prev_halo, rim_own, res_held, in_vmem(up_held)),
+        (act_prev, prev_halo, rim_own, res_held, in_vmem(up_held)),
     )
     first_prev = later(first)
     rim, second_sums = call(
         rim_second_kernel,
         "rim_second",
         [rim_shape, sums_shape],
-        [SMEM] + [VMEM] * 5,
+        [VMEM] * 5,
         side_rows,
         24,
-        (flags, act_prev, prev_halo, rim_own, res_held, in_vmem(up_held)),
+        (act_prev, prev_halo, rim_own, res_held, in_vmem(up_held)),
     )
     second_prev = moved(rim, sizes, lambda t, r: (t ^ 1, r))
     stage, inner_rim, rim_part = call(
@@ -444,20 +455,20 @@
             vmem_out((2, 2, 2, cols, ch), BF16),
             vmem_out((frames * 4 * cols, 2 * ch), F32),
         ],
-        [SMEM] + [VMEM] * 7,
+        [VMEM] * 7,
         [
             pltpu.VMEM((4, lines, cols, ch), BF16),
             pltpu.VMEM((2, 2, lines, cols, ch), BF16),
             pltpu.VMEM((2, 2 * frames * (lines - 1) * 2 * cols, 128), F32),
         ],
         24,
-        (flags, second_sums, first_sums, inner, inner_prev, first, rim, in_vmem(time_held)),
+        (second_sums, first_sums, inner, inner_prev, first, rim, in_vmem(time_held)),
     )
     return call(
         functools.partial(by_core, up_rim_kernel),
         "up_rim",
         shape((2 * frames, 2 * rows, 2 * cols, co), BF16),
-        [SMEM] + [VMEM] * 8,
+        [VMEM] * 8,
         [
             pltpu.VMEM((2, 2, 2, 3, cols, ch), BF16),
             pltpu.VMEM((2, 2 * frames * 3 * 2 * cols, 128), F32),
@@ -465,7 +476,7 @@
             pltpu.SemaphoreType.DMA((7,)),
         ],
         24,
-        (flags, second_sums, first_sums, rim_part, second_prev, first_prev, inner_rim, stage, in_vmem(time_held)),
+        (second_sums, first_sums, rim_part, second_prev, first_prev, inner_rim, stage, in_vmem(time_held)),
         out_specs=HBM,
     )
 

time: 29.6 us -> 27.8 us (0.939)
  Pallas kernels: 17.4 us -> 12.9 us
  waiting for transfers between devices: 3.13 us -> 6.95 us
  starting transfers between devices: 7.91 us -> 6.37 us
  local copies, waits for them, and re-layouts: 0.49 us -> 0.93 us
    pallas_call x9, Pallas kernels: 17.4 us -> 12.9 us  [call(): pl.pallas_call(kernel, out_shape=shapes, in_specs=specs, out_specs=out_sp...]
    ppermute x7, waiting for transfers between devices: 3.13 us -> 6.95 us  [moved(): return lax.ppermute(block, ('tm', 'rows'), pairs)]
    ppermute x7, starting transfers between devices: 7.91 us -> 6.37 us  [moved(): return lax.ppermute(block, ('tm', 'rows'), pairs)]
    unnamed x4, local copies, waits for them, and re-layouts: 0.38 us -> 0.93 us
  transfers between devices with their start and end apart: 7 -> 7, of which waited for: 5 -> 6; matrix products, arithmetic and copies ran while one was open for 0% -> 0% of each run, Pallas kernels for 48% -> 38%
where the time goes in v6:
time: 27.8 us; the launch traced here: 27.5 us
  Pallas kernels  12.9 us (46%)
  waiting for transfers between devices  6.95 us (25%)
  starting transfers between devices  6.37 us (23%)
  local copies, waits for them, and re-layouts  0.93 us (3%)
  between operations  0.28 us (1%)
    pallas_call x9, Pallas kernels, call(): pl.pallas_call(kernel, out_shape=shapes, in_specs=specs, out_specs=out_sp...  12.9 us
    ppermute x7, waiting for transfers between devices, moved(): return lax.ppermute(block, ('tm', 'rows'), pairs)  6.95 us
    ppermute x7, starting transfers between devices, moved(): return lax.ppermute(block, ('tm', 'rows'), pairs)  6.37 us
    unnamed x4, local copies, waits for them, and re-layouts  0.93 us
  transfers between devices with their start and end apart: 7, of which 6 were waited for; matrix products, arithmetic and copies ran while one was open for 0% of the time, Pallas kernels for 38%

profile of v6, /device:TPU:192, one launch (start us, length us, event | category | flops | bytes accessed | tf_op | source)
XLA Modules:
  0.0 27.5 jit_solution(8004972780982817527)
XLA Ops:
  0.0 0.0 copy-start.1
  0.0 0.0 copy-start
  0.0 0.9 %copy-done.1 = bf16[2,6,32,384]{3,2,1,0:T(8,128)(2,1)S(1)} copy-done((bf16[2,6,32,384]{3,2,1,0:T(8,128)(2,1)S(1)}, bf16[2,6,32,384]{3,2,1,0:T(8,128)(2,1)}, u32[]{:S(2)}) %copy-start.1) | copy-done | bytes 294936
  1.0 5.6 %collective-permute-start.1 = (bf16[2,2,32,384]{3,2,1,0:T(8,128)(2,1)S(1)}, bf16[2,2,32,384]{3,2,1,0:T(8,128)(2,1)S(1)}, u32[]{:S(2)}, u32[]{:S(2)}) collective-permute-start(bf16[2,2,32,384]{3,2,1,0:T(8,128)(2,1)S(1)} %get-tuple-element.27), channel_id=1, source_target_pairs={{0,0},{1,2},{2,1},{3,4},{4,3},{5,6},{6,5},{7,8},{8,7},{9,10},{10,9... | collective-permute-start | bytes 294920 | tf_op jit(solution)/shard_map/ppermute | solution.py:23
  6.6 0.1 collective-permute-start.2
  6.7 0.0 collective-permute-start
  6.8 0.0 copy-done
  6.8 2.6 %prepare.1 = (bf16[2,6,32,384]{3,2,1,0:T(8,128)(2,1)S(1)}, bf16[2,6,32,384]{3,2,1,0:T(8,128)(2,1)S(1)}, f32[1,384]{1,0:T(1,128)S(1)}, f32[2,4,32,384]{3,2,1,0:T(...) custom-call(bf16[2,6,32,384]{3,2,1,0:T(8,128)(2,1)} %features.1, f32[384]{0:T(512)} %gain.1, ...), custom_call_target="tpu_custom_call" | custom-call | flops 3000000000 | bytes 9000000 | tf_op jit(solution)/shard_map/prepare/pallas_call | solution.py:326
  9.4 0.5 %collective-permute-done.1.cross = bf16[2,2,32,384]{3,2,1,0:T(8,128)(2,1)S(1)} collective-permute-done((bf16[2,2,32,384]{3,2,1,0:T(8,128)(2,1)S(1)}, bf16[2,2,32,384]{3,2,1,0:T(8,128)(2,1)S(1)}, u32[]{:S(2)}, u32[]{:S(2)}) %collective-permute-start.1) | collective-permute-done | bytes 98336 | tf_op jit(solution)/shard_map/ppermute | solution.py:23
  9.9 1.5 %collective-permute-done.2.pair = bf16[2,2,32,384]{3,2,1,0:T(8,128)(2,1)S(1)} collective-permute-done((bf16[2,2,32,384]{3,2,1,0:T(8,128)(2,1)S(1)}, bf16[2,2,32,384]{3,2,1,0:T(8,128)(2,1)S(1)}, u32[]{:S(2)}, u32[]{:S(2)}) %collective-permute-start.2) | collective-permute-done | bytes 98336 | tf_op jit(solution)/shard_map/ppermute | solution.py:23
  11.3 0.2 halo.1
  11.5 0.0 collective-permute-start.3
  11.6 1.4 %rim_own.1.partial = f32[2,2,2,32,384]{4,3,2,1,0:T(8,128)S(1)} custom-call(bf16[2,6,32,384]{3,2,1,0:T(8,128)(2,1)S(1)} %get-tuple-element.29.act_own, bf16[2,2,2,32,384]{4,3,2,1,0:T(8,128)(2,1)S(1)} %halo.1, bf16[2,6,32,384]{3,2,1,0:T(8,128)(2,1)S(1)} %get-tuple-element.30.own, bf16[2,2,32,384]{3,2,1,0:T(8,128)(2,1)S(1)} %collective-permute-done.1.cross, ...), custom_call_target="tpu_custom_call" | custom-call | flops 1000000000 | bytes 3000000 | tf_op jit(solution)/shard_map/rim_own/pallas_call | solution.py:326
  13.0 1.1 %collective-permute-done.prev = bf16[2,6,32,384]{3,2,1,0:T(8,128)(2,1)S(1)} collective-permute-done((bf16[2,6,32,384]{3,2,1,0:T(8,128)(2,1)S(1)}, bf16[2,6,32,384]{3,2,1,0:T(8,128)(2,1)S(1)}, u32[]{:S(2)}, u32[]{:S(2)}) %collective-permute-start) | collective-permute-done | bytes 294944 | tf_op jit(solution)/shard_map/ppermute | solution.py:23
  14.1 1.6 %inner.1 = (bf16[2,4,32,384]{3,2,1,0:T(8,128)(2,1)S(1)}, bf16[2,6,32,384]{3,2,1,0:T(8,128)(2,1)S(1)}) custom-call(bf16[2,6,32,384]{3,2,1,0:T(8,128)(2,1)S(1)} %collective-permute-done.prev, f32[1,384]{1,0:T(1,128)S(1)} %get-tuple-element.24.gain, bf16[3,3,3,384,384]{4,3,2,1,0:T(8,128)(2,1)S(1)} %copy-done, f32[2,4,32,384]{3,2,1,0:T(8,128)S(1)} %get-tuple-element.25.partial), custom_call_target="tpu_custom_call" | custom-call | flops 1000000000 | bytes 3000000 | tf_op jit(solution)/shard_map/inner/pallas_call | solution.py:326
  15.7 0.5 %collective-permute-start.4 = (bf16[2,4,32,384]{3,2,1,0:T(8,128)(2,1)S(1)}, bf16[2,4,32,384]{3,2,1,0:T(8,128)(2,1)S(1)}, u32[]{:S(2)}, u32[]{:S(2)}) collective-permute-start(bf16[2,4,32,384]{3,2,1,0:T(8,128)(2,1)S(1)} %get-tuple-element.34.refs_2_), channel_id=1, source_target_pairs={{0,32},{1,33},{2,34},{3,35},{4,36},{5,37},{6,38},{7,39},{8,40},{9,... | collective-permute-start | bytes 589832 | tf_op jit(solution)/shard_map/ppermute | solution.py:23
  16.2 1.6 %collective-permute-done.3.halo = bf16[2,2,2,32,384]{4,3,2,1,0:T(8,128)(2,1)S(1)} collective-permute-done((bf16[2,2,2,32,384]{4,3,2,1,0:T(8,128)(2,1)S(1)}, bf16[2,2,2,32,384]{4,3,2,1,0:T(8,128)(2,1)S(1)}, u32[]{:S(2)}, u32[]{:S(2)}) %collective-permute-start.3) | collective-permute-done | bytes 196640 | tf_op jit(solution)/shard_map/ppermute | solution.py:23
  17.9 0.8 %rim_first.1 = (bf16[2,2,2,32,384]{4,3,2,1,0:T(8,128)(2,1)S(1)}, bf16[2,768,768]{2,1,0:T(8,128)(2,1)S(1)}) custom-call(bf16[2,6,32,384]{3,2,1,0:T(8,128)(2,1)S(1)} %get-tuple-element.26.act_prev, bf16[2,2,2,32,384]{4,3,2,1,0:T(8,128)(2,1)S(1)} %collective-permute-done.3.halo, f32[2,2,2,32,384]{4,3,2,1,0:T(8,128)S(1)} %rim_own.1.partial, ...), custom_call_target="tpu_custom_call" | custom-call | flops 1000000000 | bytes 3000000 | tf_op jit(solution)/shard_map/rim_first/pallas_call | solution.py:326
  18.6 0.0 collective-permute-start.6
  18.7 1.4 %rim_second.1 = (bf16[2,2,2,32,384]{4,3,2,1,0:T(8,128)(2,1)S(1)}, bf16[2,768,768]{2,1,0:T(8,128)(2,1)S(1)}) custom-call(bf16[2,6,32,384]{3,2,1,0:T(8,128)(2,1)S(1)} %get-tuple-element.26.act_prev, bf16[2,2,2,32,384]{4,3,2,1,0:T(8,128)(2,1)S(1)} %collective-permute-done.3.halo, f32[2,2,2,32,384]{4,3,2,1,0:T(8,128)S(1)} %rim_own.1.partial, ...), custom_call_target="tpu_custom_call" | custom-call | flops 1000000000 | bytes 3000000 | tf_op jit(solution)/shard_map/rim_second/pallas_call | solution.py:326
  20.1 0.1 collective-permute-start.5
  20.2 1.8 %collective-permute-done.4.refs_3_ = bf16[2,4,32,384]{3,2,1,0:T(8,128)(2,1)S(1)} collective-permute-done((bf16[2,4,32,384]{3,2,1,0:T(8,128)(2,1)S(1)}, bf16[2,4,32,384]{3,2,1,0:T(8,128)(2,1)S(1)}, u32[]{:S(2)}, u32[]{:S(2)}) %collective-permute-start.4) | collective-permute-done | bytes 196640 | tf_op jit(solution)/shard_map/ppermute | solution.py:23
  22.0 2.5 %up_inner.1 = (bf16[4,6,64,192]{3,2,1,0:T(8,128)(2,1)S(1)}, bf16[2,2,2,32,384]{4,3,2,1,0:T(8,128)(2,1)S(1)}, f32[256,768]{1,0:T(8,128)S(1)}) custom-call(bf16[2,768,768]{2,1,0:T(8,128)(2,1)S(1)} %get-tuple-element.32.refs_0_, bf16[2,768,768]{2,1,0:T(8,128)(2,1)S(1)} %get-tuple-element.33.refs_1_, bf16[2,4,32,384]{3,2,1,0:T(8,128)(2,1)S(1)} %get-tuple-element.34.refs_2_, ...), custom_call_target="tpu_custom_call" | custom-call | flops 1000000000 | bytes 3000000 | tf_op jit(solution)/shard_map/up_inner/pallas_call | solution.py:326
  24.5 0.4 %collective-permute-done.6.refs_4_ = bf16[2,2,2,32,384]{4,3,2,1,0:T(8,128)(2,1)S(1)} collective-permute-done((bf16[2,2,2,32,384]{4,3,2,1,0:T(8,128)(2,1)S(1)}, bf16[2,2,2,32,384]{4,3,2,1,0:T(8,128)(2,1)S(1)}, u32[]{:S(2)}, u32[]{:S(2)}) %collective-permute-start.6) | collective-permute-done | bytes 196640 | tf_op jit(solution)/shard_map/ppermute | solution.py:23
  25.0 0.0 collective-permute-done.5.refs_3_
  25.0 2.4 %up_rim.1 = bf16[4,12,64,192]{3,2,1,0:T(8,128)(2,1)} custom-call(bf16[2,768,768]{2,1,0:T(8,128)(2,1)S(1)} %get-tuple-element.32.refs_0_, bf16[2,768,768]{2,1,0:T(8,128)(2,1)S(1)} %get-tuple-element.33.refs_1_, f32[256,768]{1,0:T(8,128)S(1)} %get-tuple-element.38.refs_2_, bf16[2,2,2,32,384]{4,3,2,1,0:T(8,128)(2,1)S(1)} %collective-permute-done.5.refs_3_, ...), custom_call_target="tpu_custom_call" | custom-call | flops 1000000000 | bytes 3000000 | tf_op jit(solution)/shard_map/up_rim/pallas_call | solution.py:326
  (3 shorter events, 0.1 us)
Async XLA Ops:
  0.0 1.0 %copy-start.1 = (bf16[2,6,32,384]{3,2,1,0:T(8,128)(2,1)S(1)}, bf16[2,6,32,384]{3,2,1,0:T(8,128)(2,1)}, u32[]{:S(2)}) copy-start(bf16[2,6,32,384]{3,2,1,0:T(8,128)(2,1)} %features.1) | copy-start | bytes 884740
  0.0 6.8 %copy-start = (bf16[3,3,3,384,384]{4,3,2,1,0:T(8,128)(2,1)S(1)}, bf16[3,3,3,384,384]{4,3,2,1,0:T(8,128)(2,1)}, u32[]{:S(2)}) copy-start(bf16[3,3,3,384,384]{4,3,2,1,0:T(8,128)(2,1)} %res_held.9) | copy-start | bytes 23887876
  1.0 8.9 %collective-permute-start.1 = (bf16[2,2,32,384]{3,2,1,0:T(8,128)(2,1)S(1)}, bf16[2,2,32,384]{3,2,1,0:T(8,128)(2,1)S(1)}, u32[]{:S(2)}, u32[]{:S(2)}) collective-permute-start(bf16[2,2,32,384]{3,2,1,0:T(8,128)(2,1)S(1)} %get-tuple-element.27), channel_id=1, source_target_pairs={{0,0},{1,2},{2,1},{3,4},{4,3},{5,6},{6,5},{7,8},{8,7},{9,10},{10,9... | collective-permute-start | bytes 294920 | tf_op jit(solution)/shard_map/ppermute | solution.py:23
  6.6 4.7 %collective-permute-start.2 = (bf16[2,2,32,384]{3,2,1,0:T(8,128)(2,1)S(1)}, bf16[2,2,32,384]{3,2,1,0:T(8,128)(2,1)S(1)}, u32[]{:S(2)}, u32[]{:S(2)}) collective-permute-start(bf16[2,2,32,384]{3,2,1,0:T(8,128)(2,1)S(1)} %get-tuple-element.28), channel_id=1, source_target_pairs={{0,1},{1,0},{2,3},{3,2},{4,5},{5,4},{6,7},{7,6},{8,9},{9,8},{10,11... | collective-permute-start | bytes 294920 | tf_op jit(solution)/shard_map/ppermute | solution.py:23
  6.7 7.4 %collective-permute-start = (bf16[2,6,32,384]{3,2,1,0:T(8,128)(2,1)S(1)}, bf16[2,6,32,384]{3,2,1,0:T(8,128)(2,1)S(1)}, u32[]{:S(2)}, u32[]{:S(2)}) collective-permute-start(bf16[2,6,32,384]{3,2,1,0:T(8,128)(2,1)S(1)} %copy-done.1), channel_id=1, source_target_pairs={{0,32},{1,33},{2,34},{3,35},{4,36},{5,37},{6,38},{7,39},{8,40},{9,... | collective-permute-start | bytes 884744 | tf_op jit(solution)/shard_map/ppermute | solution.py:23
  11.5 6.3 %collective-permute-start.3 = (bf16[2,2,2,32,384]{4,3,2,1,0:T(8,128)(2,1)S(1)}, bf16[2,2,2,32,384]{4,3,2,1,0:T(8,128)(2,1)S(1)}, u32[]{:S(2)}, u32[]{:S(2)}) collective-permute-start(bf16[2,2,2,32,384]{4,3,2,1,0:T(8,128)(2,1)S(1)} %halo.1), channel_id=1, source_target_pairs={{0,32},{1,33},{2,34},{3,35},{4,36},{5,37},{6,38},{7,39},{8,40},{9,... | collective-permute-start | bytes 589832 | tf_op jit(solution)/shard_map/ppermute | solution.py:23
  15.7 6.3 %collective-permute-start.4 = (bf16[2,4,32,384]{3,2,1,0:T(8,128)(2,1)S(1)}, bf16[2,4,32,384]{3,2,1,0:T(8,128)(2,1)S(1)}, u32[]{:S(2)}, u32[]{:S(2)}) collective-permute-start(bf16[2,4,32,384]{3,2,1,0:T(8,128)(2,1)S(1)} %get-tuple-element.34.refs_2_), channel_id=1, source_target_pairs={{0,32},{1,33},{2,34},{3,35},{4,36},{5,37},{6,38},{7,39},{8,40},{9,... | collective-permute-start | bytes 589832 | tf_op jit(solution)/shard_map/ppermute | solution.py:23
  18.6 6.3 %collective-permute-start.6 = (bf16[2,2,2,32,384]{4,3,2,1,0:T(8,128)(2,1)S(1)}, bf16[2,2,2,32,384]{4,3,2,1,0:T(8,128)(2,1)S(1)}, u32[]{:S(2)}, u32[]{:S(2)}) collective-permute-start(bf16[2,2,2,32,384]{4,3,2,1,0:T(8,128)(2,1)S(1)} %get-tuple-element.35.refs_4_), channel_id=1, source_target_pairs={{0,32},{1,33},{2,34},{3,35},{4,36},{5,37},{6,38},{7,39},{8,40},{9,... | collective-permute-start | bytes 589832 | tf_op jit(solution)/shard_map/ppermute | solution.py:23
  20.1 4.9 %collective-permute-start.5 = (bf16[2,2,2,32,384]{4,3,2,1,0:T(8,128)(2,1)S(1)}, bf16[2,2,2,32,384]{4,3,2,1,0:T(8,128)(2,1)S(1)}, u32[]{:S(2)}, u32[]{:S(2)}) collective-permute-start(bf16[2,2,2,32,384]{4,3,2,1,0:T(8,128)(2,1)S(1)} %get-tuple-element.36.refs_5_), channel_id=1, source_target_pairs={{0,32},{1,33},{2,34},{3,35},{4,36},{5,37},{6,38},{7,39},{8,40},{9,... | collective-permute-start | bytes 589832 | tf_op jit(solution)/shard_map/ppermute | solution.py:23

commit v7 on v6

--- a/solution.py
+++ b/solution.py
@@ -87,7 +87,7 @@
             else:
                 r = [w[0][k] + w[1][k] for k in range(3)] if tap == 0 else w[2]
             block = jnp.concatenate([r[0], r[0] + r[1], r[1] + r[2], r[2]], axis=0)
-            combined[phase, tap * ch : (tap + 1) * ch] = block.T.astype(BF16)
+            combined[phase, tap * ch : (tap + 1) * ch] = block.astype(BF16).T
 
 
 def columns_summed(acc, cols, ch):
@@ -206,8 +206,11 @@
     return jnp.dot(lhs, rhs, preferred_element_type=F32)
 
 
-def woven_columns(upper, lower, weight, woven, cols, co):
-    y = jnp.dot(jnp.concatenate([upper, lower], axis=1), weight, preferred_element_type=F32)
+def both_lines(upper, lower, weight):
+    return jnp.dot(jnp.concatenate([upper, lower], axis=1), weight, preferred_element_type=F32)
+
+
+def woven_columns(y, woven, cols, co):
     size = y.shape[0]
     a, b = y[:, : 2 * co], y[:, 2 * co :]
     col = lax.broadcasted_iota(jnp.int32, (size, 2 * co), 0) % cols
@@ -259,8 +262,9 @@
     size = 2 * frames * pairs * cols
     upper = up[:, :, 0:pairs].reshape(size, ch)
     lower = up[:, :, 1 : pairs + 1].reshape(size, ch)
+    wide = both_lines(upper, lower, jnp.concatenate([weight[0], weight[1]], axis=1))
     for phase in range(2):
-        line = woven_columns(upper, lower, weight[phase], woven, cols, co)
+        line = woven_columns(wide[:, phase * 4 * co : (phase + 1) * 4 * co], woven, cols, co)
         for f in range(2 * frames):
             for j in range(pairs):
                 stage[f, 2 * j + 1 - phase] = line(f * pairs + j)
@@ -308,7 +312,7 @@
             lines_taken = [up[:, :, s, i + step : i + step + 1] for s, i, _ in picks]
             return jnp.concatenate(lines_taken, axis=2).reshape(size, ch)
 
-        line = woven_columns(taken(0), taken(1), weight[phase], woven, cols, co)
+        line = woven_columns(both_lines(taken(0), taken(1), weight[phase]), woven, cols, co)
         for j, (_, _, row) in enumerate(picks):
             for f in range(2 * frames):
                 stage[phase, j, f, 0] = line(f * 3 + j)

time: 27.8 us -> 27.8 us (level)
  no operation moved by 1% of the time
where the time goes in v7:
time: 27.8 us; the launch traced here: 27.4 us
  Pallas kernels  12.9 us (46%)
  waiting for transfers between devices  6.96 us (25%)
  starting transfers between devices  6.37 us (23%)
  local copies, waits for them, and re-layouts  0.93 us (3%)
  between operations  0.28 us (1%)
    pallas_call x9, Pallas kernels, call(): pl.pallas_call(kernel, out_shape=shapes, in_specs=specs, out_specs=out_sp...  12.9 us
    ppermute x7, waiting for transfers between devices, moved(): return lax.ppermute(block, ('tm', 'rows'), pairs)  6.96 us
    ppermute x7, starting transfers between devices, moved(): return lax.ppermute(block, ('tm', 'rows'), pairs)  6.37 us
    unnamed x4, local copies, waits for them, and re-layouts  0.93 us
  transfers between devices with their start and end apart: 7, of which 6 were waited for; matrix products, arithmetic and copies ran while one was open for 0% of the time, Pallas kernels for 38%

profile of v7, /device:TPU:192, one launch (start us, length us, event | category | flops | bytes accessed | tf_op | source)
XLA Modules:
  0.0 27.4 jit_solution(2257735817619014937)
XLA Ops:
  0.0 0.0 copy-start.1
  0.0 0.0 copy-start
  0.0 0.9 %copy-done.1 = bf16[2,6,32,384]{3,2,1,0:T(8,128)(2,1)S(1)} copy-done((bf16[2,6,32,384]{3,2,1,0:T(8,128)(2,1)S(1)}, bf16[2,6,32,384]{3,2,1,0:T(8,128)(2,1)}, u32[]{:S(2)}) %copy-start.1) | copy-done | bytes 294936
  1.0 5.6 %collective-permute-start.1 = (bf16[2,2,32,384]{3,2,1,0:T(8,128)(2,1)S(1)}, bf16[2,2,32,384]{3,2,1,0:T(8,128)(2,1)S(1)}, u32[]{:S(2)}, u32[]{:S(2)}) collective-permute-start(bf16[2,2,32,384]{3,2,1,0:T(8,128)(2,1)S(1)} %get-tuple-element.27), channel_id=1, source_target_pairs={{0,0},{1,2},{2,1},{3,4},{4,3},{5,6},{6,5},{7,8},{8,7},{9,10},{10,9... | collective-permute-start | bytes 294920 | tf_op jit(solution)/shard_map/ppermute | solution.py:23
  6.6 0.1 collective-permute-start.2
  6.7 0.0 collective-permute-start
  6.8 0.0 copy-done
  6.8 2.6 %prepare.1 = (bf16[2,6,32,384]{3,2,1,0:T(8,128)(2,1)S(1)}, bf16[2,6,32,384]{3,2,1,0:T(8,128)(2,1)S(1)}, f32[1,384]{1,0:T(1,128)S(1)}, f32[2,4,32,384]{3,2,1,0:T(...) custom-call(bf16[2,6,32,384]{3,2,1,0:T(8,128)(2,1)} %features.1, f32[384]{0:T(512)} %gain.1, ...), custom_call_target="tpu_custom_call" | custom-call | flops 3000000000 | bytes 9000000 | tf_op jit(solution)/shard_map/prepare/pallas_call | solution.py:330
  9.4 0.5 %collective-permute-done.1.cross = bf16[2,2,32,384]{3,2,1,0:T(8,128)(2,1)S(1)} collective-permute-done((bf16[2,2,32,384]{3,2,1,0:T(8,128)(2,1)S(1)}, bf16[2,2,32,384]{3,2,1,0:T(8,128)(2,1)S(1)}, u32[]{:S(2)}, u32[]{:S(2)}) %collective-permute-start.1) | collective-permute-done | bytes 98336 | tf_op jit(solution)/shard_map/ppermute | solution.py:23
  9.9 1.5 %collective-permute-done.2.pair = bf16[2,2,32,384]{3,2,1,0:T(8,128)(2,1)S(1)} collective-permute-done((bf16[2,2,32,384]{3,2,1,0:T(8,128)(2,1)S(1)}, bf16[2,2,32,384]{3,2,1,0:T(8,128)(2,1)S(1)}, u32[]{:S(2)}, u32[]{:S(2)}) %collective-permute-start.2) | collective-permute-done | bytes 98336 | tf_op jit(solution)/shard_map/ppermute | solution.py:23
  11.3 0.2 halo.1
  11.5 0.0 collective-permute-start.3
  11.6 1.4 %rim_own.1.partial = f32[2,2,2,32,384]{4,3,2,1,0:T(8,128)S(1)} custom-call(bf16[2,6,32,384]{3,2,1,0:T(8,128)(2,1)S(1)} %get-tuple-element.29.act_own, bf16[2,2,2,32,384]{4,3,2,1,0:T(8,128)(2,1)S(1)} %halo.1, bf16[2,6,32,384]{3,2,1,0:T(8,128)(2,1)S(1)} %get-tuple-element.30.own, bf16[2,2,32,384]{3,2,1,0:T(8,128)(2,1)S(1)} %collective-permute-done.1.cross, ...), custom_call_target="tpu_custom_call" | custom-call | flops 1000000000 | bytes 3000000 | tf_op jit(solution)/shard_map/rim_own/pallas_call | solution.py:330
  13.0 1.1 %collective-permute-done.prev = bf16[2,6,32,384]{3,2,1,0:T(8,128)(2,1)S(1)} collective-permute-done((bf16[2,6,32,384]{3,2,1,0:T(8,128)(2,1)S(1)}, bf16[2,6,32,384]{3,2,1,0:T(8,128)(2,1)S(1)}, u32[]{:S(2)}, u32[]{:S(2)}) %collective-permute-start) | collective-permute-done | bytes 294944 | tf_op jit(solution)/shard_map/ppermute | solution.py:23
  14.1 1.6 %inner.1 = (bf16[2,4,32,384]{3,2,1,0:T(8,128)(2,1)S(1)}, bf16[2,6,32,384]{3,2,1,0:T(8,128)(2,1)S(1)}) custom-call(bf16[2,6,32,384]{3,2,1,0:T(8,128)(2,1)S(1)} %collective-permute-done.prev, f32[1,384]{1,0:T(1,128)S(1)} %get-tuple-element.24.gain, bf16[3,3,3,384,384]{4,3,2,1,0:T(8,128)(2,1)S(1)} %copy-done, f32[2,4,32,384]{3,2,1,0:T(8,128)S(1)} %get-tuple-element.25.partial), custom_call_target="tpu_custom_call" | custom-call | flops 1000000000 | bytes 3000000 | tf_op jit(solution)/shard_map/inner/pallas_call | solution.py:330
  15.7 0.5 %collective-permute-start.4 = (bf16[2,4,32,384]{3,2,1,0:T(8,128)(2,1)S(1)}, bf16[2,4,32,384]{3,2,1,0:T(8,128)(2,1)S(1)}, u32[]{:S(2)}, u32[]{:S(2)}) collective-permute-start(bf16[2,4,32,384]{3,2,1,0:T(8,128)(2,1)S(1)} %get-tuple-element.34.refs_2_), channel_id=1, source_target_pairs={{0,32},{1,33},{2,34},{3,35},{4,36},{5,37},{6,38},{7,39},{8,40},{9,... | collective-permute-start | bytes 589832 | tf_op jit(solution)/shard_map/ppermute | solution.py:23
  16.2 1.6 %collective-permute-done.3.halo = bf16[2,2,2,32,384]{4,3,2,1,0:T(8,128)(2,1)S(1)} collective-permute-done((bf16[2,2,2,32,384]{4,3,2,1,0:T(8,128)(2,1)S(1)}, bf16[2,2,2,32,384]{4,3,2,1,0:T(8,128)(2,1)S(1)}, u32[]{:S(2)}, u32[]{:S(2)}) %collective-permute-start.3) | collective-permute-done | bytes 196640 | tf_op jit(solution)/shard_map/ppermute | solution.py:23
  17.9 0.7 %rim_first.1 = (bf16[2,2,2,32,384]{4,3,2,1,0:T(8,128)(2,1)S(1)}, bf16[2,768,768]{2,1,0:T(8,128)(2,1)S(1)}) custom-call(bf16[2,6,32,384]{3,2,1,0:T(8,128)(2,1)S(1)} %get-tuple-element.26.act_prev, bf16[2,2,2,32,384]{4,3,2,1,0:T(8,128)(2,1)S(1)} %collective-permute-done.3.halo, f32[2,2,2,32,384]{4,3,2,1,0:T(8,128)S(1)} %rim_own.1.partial, ...), custom_call_target="tpu_custom_call" | custom-call | flops 1000000000 | bytes 3000000 | tf_op jit(solution)/shard_map/rim_first/pallas_call | solution.py:330
  18.6 0.0 collective-permute-start.6
  18.6 1.4 %rim_second.1 = (bf16[2,2,2,32,384]{4,3,2,1,0:T(8,128)(2,1)S(1)}, bf16[2,768,768]{2,1,0:T(8,128)(2,1)S(1)}) custom-call(bf16[2,6,32,384]{3,2,1,0:T(8,128)(2,1)S(1)} %get-tuple-element.26.act_prev, bf16[2,2,2,32,384]{4,3,2,1,0:T(8,128)(2,1)S(1)} %collective-permute-done.3.halo, f32[2,2,2,32,384]{4,3,2,1,0:T(8,128)S(1)} %rim_own.1.partial, ...), custom_call_target="tpu_custom_call" | custom-call | flops 1000000000 | bytes 3000000 | tf_op jit(solution)/shard_map/rim_second/pallas_call | solution.py:330
  20.1 0.1 collective-permute-start.5
  20.2 1.9 %collective-permute-done.4.refs_3_ = bf16[2,4,32,384]{3,2,1,0:T(8,128)(2,1)S(1)} collective-permute-done((bf16[2,4,32,384]{3,2,1,0:T(8,128)(2,1)S(1)}, bf16[2,4,32,384]{3,2,1,0:T(8,128)(2,1)S(1)}, u32[]{:S(2)}, u32[]{:S(2)}) %collective-permute-start.4) | collective-permute-done | bytes 196640 | tf_op jit(solution)/shard_map/ppermute | solution.py:23
  22.0 2.5 %up_inner.1 = (bf16[4,6,64,192]{3,2,1,0:T(8,128)(2,1)S(1)}, bf16[2,2,2,32,384]{4,3,2,1,0:T(8,128)(2,1)S(1)}, f32[256,768]{1,0:T(8,128)S(1)}) custom-call(bf16[2,768,768]{2,1,0:T(8,128)(2,1)S(1)} %get-tuple-element.32.refs_0_, bf16[2,768,768]{2,1,0:T(8,128)(2,1)S(1)} %get-tuple-element.33.refs_1_, bf16[2,4,32,384]{3,2,1,0:T(8,128)(2,1)S(1)} %get-tuple-element.34.refs_2_, ...), custom_call_target="tpu_custom_call" | custom-call | flops 1000000000 | bytes 3000000 | tf_op jit(solution)/shard_map/up_inner/pallas_call | solution.py:330
  24.5 0.4 %collective-permute-done.6.refs_4_ = bf16[2,2,2,32,384]{4,3,2,1,0:T(8,128)(2,1)S(1)} collective-permute-done((bf16[2,2,2,32,384]{4,3,2,1,0:T(8,128)(2,1)S(1)}, bf16[2,2,2,32,384]{4,3,2,1,0:T(8,128)(2,1)S(1)}, u32[]{:S(2)}, u32[]{:S(2)}) %collective-permute-start.6) | collective-permute-done | bytes 196640 | tf_op jit(solution)/shard_map/ppermute | solution.py:23
  24.9 0.0 collective-permute-done.5.refs_3_
  24.9 2.4 %up_rim.1 = bf16[4,12,64,192]{3,2,1,0:T(8,128)(2,1)} custom-call(bf16[2,768,768]{2,1,0:T(8,128)(2,1)S(1)} %get-tuple-element.32.refs_0_, bf16[2,768,768]{2,1,0:T(8,128)(2,1)S(1)} %get-tuple-element.33.refs_1_, f32[256,768]{1,0:T(8,128)S(1)} %get-tuple-element.38.refs_2_, bf16[2,2,2,32,384]{4,3,2,1,0:T(8,128)(2,1)S(1)} %collective-permute-done.5.refs_3_, ...), custom_call_target="tpu_custom_call" | custom-call | flops 1000000000 | bytes 3000000 | tf_op jit(solution)/shard_map/up_rim/pallas_call | solution.py:330
  (3 shorter events, 0.1 us)
Async XLA Ops:
  0.0 1.0 %copy-start.1 = (bf16[2,6,32,384]{3,2,1,0:T(8,128)(2,1)S(1)}, bf16[2,6,32,384]{3,2,1,0:T(8,128)(2,1)}, u32[]{:S(2)}) copy-start(bf16[2,6,32,384]{3,2,1,0:T(8,128)(2,1)} %features.1) | copy-start | bytes 884740
  0.0 6.8 %copy-start = (bf16[3,3,3,384,384]{4,3,2,1,0:T(8,128)(2,1)S(1)}, bf16[3,3,3,384,384]{4,3,2,1,0:T(8,128)(2,1)}, u32[]{:S(2)}) copy-start(bf16[3,3,3,384,384]{4,3,2,1,0:T(8,128)(2,1)} %res_held.9) | copy-start | bytes 23887876
  1.0 8.9 %collective-permute-start.1 = (bf16[2,2,32,384]{3,2,1,0:T(8,128)(2,1)S(1)}, bf16[2,2,32,384]{3,2,1,0:T(8,128)(2,1)S(1)}, u32[]{:S(2)}, u32[]{:S(2)}) collective-permute-start(bf16[2,2,32,384]{3,2,1,0:T(8,128)(2,1)S(1)} %get-tuple-element.27), channel_id=1, source_target_pairs={{0,0},{1,2},{2,1},{3,4},{4,3},{5,6},{6,5},{7,8},{8,7},{9,10},{10,9... | collective-permute-start | bytes 294920 | tf_op jit(solution)/shard_map/ppermute | solution.py:23
  6.6 4.7 %collective-permute-start.2 = (bf16[2,2,32,384]{3,2,1,0:T(8,128)(2,1)S(1)}, bf16[2,2,32,384]{3,2,1,0:T(8,128)(2,1)S(1)}, u32[]{:S(2)}, u32[]{:S(2)}) collective-permute-start(bf16[2,2,32,384]{3,2,1,0:T(8,128)(2,1)S(1)} %get-tuple-element.28), channel_id=1, source_target_pairs={{0,1},{1,0},{2,3},{3,2},{4,5},{5,4},{6,7},{7,6},{8,9},{9,8},{10,11... | collective-permute-start | bytes 294920 | tf_op jit(solution)/shard_map/ppermute | solution.py:23
  6.7 7.4 %collective-permute-start = (bf16[2,6,32,384]{3,2,1,0:T(8,128)(2,1)S(1)}, bf16[2,6,32,384]{3,2,1,0:T(8,128)(2,1)S(1)}, u32[]{:S(2)}, u32[]{:S(2)}) collective-permute-start(bf16[2,6,32,384]{3,2,1,0:T(8,128)(2,1)S(1)} %copy-done.1), channel_id=1, source_target_pairs={{0,32},{1,33},{2,34},{3,35},{4,36},{5,37},{6,38},{7,39},{8,40},{9,... | collective-permute-start | bytes 884744 | tf_op jit(solution)/shard_map/ppermute | solution.py:23
  11.5 6.3 %collective-permute-start.3 = (bf16[2,2,2,32,384]{4,3,2,1,0:T(8,128)(2,1)S(1)}, bf16[2,2,2,32,384]{4,3,2,1,0:T(8,128)(2,1)S(1)}, u32[]{:S(2)}, u32[]{:S(2)}) collective-permute-start(bf16[2,2,2,32,384]{4,3,2,1,0:T(8,128)(2,1)S(1)} %halo.1), channel_id=1, source_target_pairs={{0,32},{1,33},{2,34},{3,35},{4,36},{5,37},{6,38},{7,39},{8,40},{9,... | collective-permute-start | bytes 589832 | tf_op jit(solution)/shard_map/ppermute | solution.py:23
  15.7 6.3 %collective-permute-start.4 = (bf16[2,4,32,384]{3,2,1,0:T(8,128)(2,1)S(1)}, bf16[2,4,32,384]{3,2,1,0:T(8,128)(2,1)S(1)}, u32[]{:S(2)}, u32[]{:S(2)}) collective-permute-start(bf16[2,4,32,384]{3,2,1,0:T(8,128)(2,1)S(1)} %get-tuple-element.34.refs_2_), channel_id=1, source_target_pairs={{0,32},{1,33},{2,34},{3,35},{4,36},{5,37},{6,38},{7,39},{8,40},{9,... | collective-permute-start | bytes 589832 | tf_op jit(solution)/shard_map/ppermute | solution.py:23
  18.6 6.3 %collective-permute-start.6 = (bf16[2,2,2,32,384]{4,3,2,1,0:T(8,128)(2,1)S(1)}, bf16[2,2,2,32,384]{4,3,2,1,0:T(8,128)(2,1)S(1)}, u32[]{:S(2)}, u32[]{:S(2)}) collective-permute-start(bf16[2,2,2,32,384]{4,3,2,1,0:T(8,128)(2,1)S(1)} %get-tuple-element.35.refs_4_), channel_id=1, source_target_pairs={{0,32},{1,33},{2,34},{3,35},{4,36},{5,37},{6,38},{7,39},{8,40},{9,... | collective-permute-start | bytes 589832 | tf_op jit(solution)/shard_map/ppermute | solution.py:23
  20.1 4.9 %collective-permute-start.5 = (bf16[2,2,2,32,384]{4,3,2,1,0:T(8,128)(2,1)S(1)}, bf16[2,2,2,32,384]{4,3,2,1,0:T(8,128)(2,1)S(1)}, u32[]{:S(2)}, u32[]{:S(2)}) collective-permute-start(bf16[2,2,2,32,384]{4,3,2,1,0:T(8,128)(2,1)S(1)} %get-tuple-element.36.refs_5_), channel_id=1, source_target_pairs={{0,32},{1,33},{2,34},{3,35},{4,36},{5,37},{6,38},{7,39},{8,40},{9,... | collective-permute-start | bytes 589832 | tf_op jit(solution)/shard_map/ppermute | solution.py:23
